TPU v7x, 32 devices: a whole 2x2x4 slice. The times are simulated.
32 devices in a mesh: seq: 8 (over y, x, core), head: 4 (over z).
Axes of the slice: x: 2, y: 2, z: 4, core: 2. Of those that a mesh axis runs over, the one named last changes fastest.
Arguments:
- queries: bfloat16 [1024, 2048], P('seq', 'head'), may hold values from -150 to 150
- keys: bfloat16 [1024, 1024], P('seq', 'head'), may hold values from -5 to 5
- values: bfloat16 [1024, 1024], P('seq', 'head'), may hold values from -5 to 5
- prefix_resid: bfloat16 [1024, 5376], P('seq', 'head'), may hold values from -6 to 6
- opt_queries: bfloat16 [8, 64, 2048], P('seq', None, 'head'), may hold values from -150 to 150
- opt_keys: bfloat16 [8, 64, 1024], P('seq', None, 'head'), may hold values from -5 to 5
- opt_values: bfloat16 [8, 64, 1024], P('seq', None, 'head'), may hold values from -5 to 5
- opt_resid: bfloat16 [8, 64, 5376], P('seq', None, 'head'), may hold values from -6 to 6
- out_weight: bfloat16 [2048, 5376], P('seq', 'head'), may hold values from -0.5347495 to 0.5347495
- norm_gain: float32 [5376], P('head'), may hold values from 0.1 to 1.9
- option_bounds: int32 [8, 2], P('seq'), may hold values from 0 to 64, as said below
Outputs:
- prefix_out: bfloat16 [1024, 5376], P('seq', 'head')
- option_out: bfloat16 [8, 64, 5376], P('seq', None, 'head')
- option_summary: float32 [8, 5376], P('seq', 'head')
Inputs may be any that keep to these rules, and one draw needn't show every extreme that they name: `option_bounds`: column 0 is an option's first answer position and column 1 its length, with 0 <= start < length; some option has length 64.
All inputs are finite; a program needn't handle non-finite values.
Results may differ from a plain program's by a relative error of at most 0.009.
Values may be sent and summed in bfloat16 or wider, within the bound.
No kernel may reach another device: no remote copies, remote signals or barrier semaphores. Data moves between devices by JAX's collectives and lax.ppermute only.
A program may use at most 64 MiB of HBM per device.

v0:
```python
import jax
import jax.numpy as jnp
from jax import lax
from jax.sharding import PartitionSpec as P

D = 5376
HD = 128
WINDOW = 1024
OPT_LEN = 64


score_scale = 168.0 ** (-0.5)
epsilon = 1e-06


def passed_along(value, axis, steps):
    count = lax.axis_size(axis)
    initial, last = (max(0, -steps), min(count, count - steps))
    return lax.ppermute(value, axis, [(source, source + steps) for source in range(initial, last)])


def from_root(block, axis, owner):
    block = jnp.where(lax.axis_index(axis) == owner, block, jnp.zeros_like(block))
    return lax.psum(block, axis)


def attend(query_rows, key_rows, value_rows, allowed):
    row_count = query_rows.shape[0]
    kv_heads = key_rows.shape[1] // HD
    groups = query_rows.shape[1] // key_rows.shape[1]
    query_view = query_rows.reshape(row_count, kv_heads, groups, HD)
    key_view = key_rows.reshape(-1, kv_heads, HD)
    scores = (
        jnp.einsum("rkgd,lkd->kgrl", query_view, key_view, preferred_element_type=jnp.float32)
        * score_scale
    )
    scores = jnp.where(allowed[None, None], scores, -jnp.inf)
    row_max = jnp.max(scores, axis=-1, keepdims=True)
    weights = jnp.exp(scores - row_max)
    weights = (weights / jnp.sum(weights, axis=-1, keepdims=True)).astype(jnp.bfloat16)
    value_view = value_rows.reshape(-1, kv_heads, HD)
    attended = jnp.einsum("kgrl,lkd->rkgd", weights, value_view, preferred_element_type=jnp.float32)
    return attended.reshape(row_count, -1).astype(jnp.bfloat16)


def body(
    queries,
    keys,
    values,
    prefix_resid,
    opt_queries,
    opt_keys,
    opt_values,
    opt_resid,
    out_weight,
    norm_gain,
    option_bounds,
):
    local_rows = queries.shape[0]
    seq_count = lax.axis_size("seq")
    seq_index = lax.axis_index("seq")
    halo_count = WINDOW // local_rows
    earlier_keys = []
    earlier_values = []
    carried = (keys, values)
    for hop_index in range(halo_count):
        carried = passed_along((carried[0], carried[1]), "seq", 1)
        earlier_keys.insert(0, carried[0])
        earlier_values.insert(0, carried[1])
    window_keys = jnp.concatenate(earlier_keys + [keys], axis=0)
    window_values = jnp.concatenate(earlier_values + [values], axis=0)
    query_pos = seq_index * local_rows + jnp.arange(local_rows, dtype=jnp.int32)
    key_pos = (seq_index - halo_count) * local_rows + jnp.arange(
        window_keys.shape[0], dtype=jnp.int32
    )
    allowed = (
        (key_pos[None] <= query_pos[:, None])
        & (key_pos[None] > query_pos[:, None] - WINDOW)
        & (key_pos[None] >= 0)
    )
    prefix_attn = attend(queries, window_keys, window_values, allowed)
    final_keys, final_values = (
        from_root(window_keys[local_rows:], "seq", seq_count - 1),
        from_root(window_values[local_rows:], "seq", seq_count - 1),
    )
    joined_keys = jnp.concatenate([final_keys, opt_keys[0]], axis=0)
    joined_values = jnp.concatenate([final_values, opt_values[0]], axis=0)
    positions = jnp.arange(WINDOW + OPT_LEN, dtype=jnp.int32)
    option_pos = jnp.arange(OPT_LEN, dtype=jnp.int32)
    option_allowed = jnp.where(
        positions[None] < WINDOW,
        positions[None] > option_pos[:, None],
        positions[None] - WINDOW <= option_pos[:, None],
    )
    option_attn = attend(opt_queries[0], joined_keys, joined_values, option_allowed)
    stacked = jnp.concatenate([prefix_attn, option_attn], axis=0)
    weight_share = lax.all_gather(out_weight, "seq", axis=0, tiled=True)
    head_cols = stacked.shape[1]
    attn_whole = lax.all_gather(stacked, "head", axis=1, tiled=True)
    projected = jnp.zeros((stacked.shape[0], weight_share.shape[1]), jnp.float32)
    for group in range(lax.axis_size("head")):
        partial_value = jnp.dot(
            attn_whole[:, group * head_cols : (group + 1) * head_cols],
            weight_share[group * head_cols : (group + 1) * head_cols],
            preferred_element_type=jnp.float32,
        )
        projected = projected + lax.optimization_barrier(partial_value.astype(jnp.bfloat16)).astype(
            jnp.float32
        )
    squares = lax.psum(jnp.sum(projected * projected, axis=1), "head")
    normed = projected * lax.rsqrt(squares / D + epsilon)[:, None] * norm_gain[None, :]
    prefix_out = (prefix_resid.astype(jnp.float32) + normed[:local_rows]).astype(jnp.bfloat16)
    option_full = opt_resid[0].astype(jnp.float32) + normed[local_rows:]
    start_pos = option_bounds[0, 0]
    length = option_bounds[0, 1]
    inside = option_pos < length
    option_out = jnp.where(inside[:, None], option_full, 0.0).astype(jnp.bfloat16)
    chosen = inside & (option_pos >= start_pos)
    option_summary = jnp.sum(
        jnp.where(chosen[:, None], option_out.astype(jnp.float32), 0.0), axis=0
    ) / (length - start_pos).astype(jnp.float32)
    return (prefix_out, option_out[None], option_summary[None])


def solution(mesh):
    return jax.shard_map(
        body,
        mesh=mesh,
        in_specs=(
            P("seq", "head"),
            P("seq", "head"),
            P("seq", "head"),
            P("seq", "head"),
            P("seq", None, "head"),
            P("seq", None, "head"),
            P("seq", None, "head"),
            P("seq", None, "head"),
            P("seq", "head"),
            P("head"),
            P("seq", None),
        ),
        out_specs=(P("seq", "head"), P("seq", None, "head"), P("seq", "head")),
        check_vma=False,
    )
```

profile of v0, /device:TPU:0, one launch (start us, length us, event | category | flops | bytes accessed | tf_op | source)
XLA Modules:
  0.0 198.4 jit_solution(1420929579561163917)
XLA Ops:
  7.2 0.0 all-reduce.3.cloned.1.call-start
  7.2 0.9 copy.21
  8.2 2.4 %collective-permute-start = (bf16[128,256]{0,1:T(8,128)(2,1)S(1)}, bf16[128,256]{0,1:T(8,128)(2,1)S(1)}, u32[]{:S(2)}, u32[]{:S(2)}) collective-permute-start(bf16[128,256]{0,1:T(8,128)(2,1)S(1)} %copy.21), channel_id=1, source_target_pairs={{0,4},{4,8},{8,12},{12,16},{16,20},{20,24},{24,28},{1,5},{5,9},{9,... | collective-permute-start | bytes 196616 | tf_op jit(solution)/shard_map/ppermute | solution.py:19
  10.5 1.0 copy.23
  11.5 4.5 %collective-permute-start.8 = (bf16[128,256]{0,1:T(8,128)(2,1)S(1)}, bf16[128,256]{0,1:T(8,128)(2,1)S(1)}, u32[]{:S(2)}, u32[]{:S(2)}) collective-permute-start(bf16[128,256]{0,1:T(8,128)(2,1)S(1)} %copy.23), channel_id=1, source_target_pairs={{0,4},{4,8},{8,12},{12,16},{16,20},{20,24},{24,28},{1,5},{5,9},{9,... | collective-permute-start | bytes 196616 | tf_op jit(solution)/shard_map/ppermute | solution.py:19
  16.0 0.0 collective-permute-done
  16.0 1.9 collective-permute-start.1
  17.9 0.0 collective-permute-done.8
  18.0 3.5 %collective-permute-start.9 = (bf16[128,256]{0,1:T(8,128)(2,1)S(1)}, bf16[128,256]{0,1:T(8,128)(2,1)S(1)}, u32[]{:S(2)}, u32[]{:S(2)}) collective-permute-start(bf16[128,256]{0,1:T(8,128)(2,1)S(1)} %collective-permute-done.8), channel_id=1, source_target_pairs={{0,4},{4,8},{8,12},{12,16},{16,20},{20,24},{24,28},{1,5},{5,9},{9,... | collective-permute-start | bytes 196616 | tf_op jit(solution)/shard_map/ppermute | solution.py:19
  21.5 0.0 collective-permute-done.1
  21.5 2.0 %collective-permute-start.2 = (bf16[128,256]{0,1:T(8,128)(2,1)S(1)}, bf16[128,256]{0,1:T(8,128)(2,1)S(1)}, u32[]{:S(2)}, u32[]{:S(2)}) collective-permute-start(bf16[128,256]{0,1:T(8,128)(2,1)S(1)} %collective-permute-done.1), channel_id=1, source_target_pairs={{0,4},{4,8},{8,12},{12,16},{16,20},{20,24},{24,28},{1,5},{5,9},{9,... | collective-permute-start | bytes 196616 | tf_op jit(solution)/shard_map/ppermute | solution.py:19
  23.5 0.0 collective-permute-done.9
  23.5 3.5 %collective-permute-start.10 = (bf16[128,256]{0,1:T(8,128)(2,1)S(1)}, bf16[128,256]{0,1:T(8,128)(2,1)S(1)}, u32[]{:S(2)}, u32[]{:S(2)}) collective-permute-start(bf16[128,256]{0,1:T(8,128)(2,1)S(1)} %collective-permute-done.9), channel_id=1, source_target_pairs={{0,4},{4,8},{8,12},{12,16},{16,20},{20,24},{24,28},{1,5},{5,9},{9,... | collective-permute-start | bytes 196616 | tf_op jit(solution)/shard_map/ppermute | solution.py:19
  27.0 0.0 collective-permute-done.2
  27.1 2.8 %collective-permute-start.3 = (bf16[128,256]{0,1:T(8,128)(2,1)S(1)}, bf16[128,256]{0,1:T(8,128)(2,1)S(1)}, u32[]{:S(2)}, u32[]{:S(2)}) collective-permute-start(bf16[128,256]{0,1:T(8,128)(2,1)S(1)} %collective-permute-done.2), channel_id=1, source_target_pairs={{0,4},{4,8},{8,12},{12,16},{16,20},{20,24},{24,28},{1,5},{5,9},{9,... | collective-permute-start | bytes 196616 | tf_op jit(solution)/shard_map/ppermute | solution.py:19
  29.9 0.0 collective-permute-done.10
  29.9 3.6 %collective-permute-start.11 = (bf16[128,256]{0,1:T(8,128)(2,1)S(1)}, bf16[128,256]{0,1:T(8,128)(2,1)S(1)}, u32[]{:S(2)}, u32[]{:S(2)}) collective-permute-start(bf16[128,256]{0,1:T(8,128)(2,1)S(1)} %collective-permute-done.10), channel_id=1, source_target_pairs={{0,4},{4,8},{8,12},{12,16},{16,20},{20,24},{24,28},{1,5},{5,9},{9,... | collective-permute-start | bytes 196616 | tf_op jit(solution)/shard_map/ppermute | solution.py:19
  33.5 0.0 collective-permute-done.3
  33.5 2.9 %collective-permute-start.4 = (bf16[128,256]{0,1:T(8,128)(2,1)S(1)}, bf16[128,256]{0,1:T(8,128)(2,1)S(1)}, u32[]{:S(2)}, u32[]{:S(2)}) collective-permute-start(bf16[128,256]{0,1:T(8,128)(2,1)S(1)} %collective-permute-done.3), channel_id=1, source_target_pairs={{0,4},{4,8},{8,12},{12,16},{16,20},{20,24},{24,28},{1,5},{5,9},{9,... | collective-permute-start | bytes 196616 | tf_op jit(solution)/shard_map/ppermute | solution.py:19
  36.4 0.0 collective-permute-done.11
  36.4 3.6 %collective-permute-start.12 = (bf16[128,256]{0,1:T(8,128)(2,1)S(1)}, bf16[128,256]{0,1:T(8,128)(2,1)S(1)}, u32[]{:S(2)}, u32[]{:S(2)}) collective-permute-start(bf16[128,256]{0,1:T(8,128)(2,1)S(1)} %collective-permute-done.11), channel_id=1, source_target_pairs={{0,4},{4,8},{8,12},{12,16},{16,20},{20,24},{24,28},{1,5},{5,9},{9,... | collective-permute-start | bytes 196616 | tf_op jit(solution)/shard_map/ppermute | solution.py:19
  39.9 2.9 %collective-permute-start.5 = (bf16[128,256]{0,1:T(8,128)(2,1)S(1)}, bf16[128,256]{0,1:T(8,128)(2,1)S(1)}, u32[]{:S(2)}, u32[]{:S(2)}) collective-permute-start(bf16[128,256]{0,1:T(8,128)(2,1)S(1)} %collective-permute-done.4), channel_id=1, source_target_pairs={{0,4},{4,8},{8,12},{12,16},{16,20},{20,24},{24,28},{1,5},{5,9},{9,... | collective-permute-start | bytes 196616 | tf_op jit(solution)/shard_map/ppermute | solution.py:19
  42.8 0.0 collective-permute-done.12
  42.8 3.6 %collective-permute-start.13 = (bf16[128,256]{0,1:T(8,128)(2,1)S(1)}, bf16[128,256]{0,1:T(8,128)(2,1)S(1)}, u32[]{:S(2)}, u32[]{:S(2)}) collective-permute-start(bf16[128,256]{0,1:T(8,128)(2,1)S(1)} %collective-permute-done.12), channel_id=1, source_target_pairs={{0,4},{4,8},{8,12},{12,16},{16,20},{20,24},{24,28},{1,5},{5,9},{9,... | collective-permute-start | bytes 196616 | tf_op jit(solution)/shard_map/ppermute | solution.py:19
  46.4 0.0 collective-permute-done.5
  46.4 2.9 %collective-permute-start.6 = (bf16[128,256]{0,1:T(8,128)(2,1)S(1)}, bf16[128,256]{0,1:T(8,128)(2,1)S(1)}, u32[]{:S(2)}, u32[]{:S(2)}) collective-permute-start(bf16[128,256]{0,1:T(8,128)(2,1)S(1)} %collective-permute-done.5), channel_id=1, source_target_pairs={{0,4},{4,8},{8,12},{12,16},{16,20},{20,24},{24,28},{1,5},{5,9},{9,... | collective-permute-start | bytes 196616 | tf_op jit(solution)/shard_map/ppermute | solution.py:19
  49.3 3.6 %collective-permute-start.14 = (bf16[128,256]{0,1:T(8,128)(2,1)S(1)}, bf16[128,256]{0,1:T(8,128)(2,1)S(1)}, u32[]{:S(2)}, u32[]{:S(2)}) collective-permute-start(bf16[128,256]{0,1:T(8,128)(2,1)S(1)} %collective-permute-done.13), channel_id=1, source_target_pairs={{0,4},{4,8},{8,12},{12,16},{16,20},{20,24},{24,28},{1,5},{5,9},{9,... | collective-permute-start | bytes 196616 | tf_op jit(solution)/shard_map/ppermute | solution.py:19
  52.9 2.9 %collective-permute-start.7 = (bf16[128,256]{0,1:T(8,128)(2,1)S(1)}, bf16[128,256]{0,1:T(8,128)(2,1)S(1)}, u32[]{:S(2)}, u32[]{:S(2)}) collective-permute-start(bf16[128,256]{0,1:T(8,128)(2,1)S(1)} %collective-permute-done.6), channel_id=1, source_target_pairs={{0,4},{4,8},{8,12},{12,16},{16,20},{20,24},{24,28},{1,5},{5,9},{9,... | collective-permute-start | bytes 196616 | tf_op jit(solution)/shard_map/ppermute | solution.py:19
  55.8 3.6 %collective-permute-start.15 = (bf16[128,256]{0,1:T(8,128)(2,1)S(1)}, bf16[128,256]{0,1:T(8,128)(2,1)S(1)}, u32[]{:S(2)}, u32[]{:S(2)}) collective-permute-start(bf16[128,256]{0,1:T(8,128)(2,1)S(1)} %collective-permute-done.14), channel_id=1, source_target_pairs={{0,4},{4,8},{8,12},{12,16},{16,20},{20,24},{24,28},{1,5},{5,9},{9,... | collective-permute-start | bytes 196616 | tf_op jit(solution)/shard_map/ppermute | solution.py:19
  59.7 0.5 collective-permute-done.15
  60.6 0.1 broadcast_select_fusion
  60.7 1.0 copy.29
  61.7 1.0 copy.32
  62.7 0.0 all-reduce.3.cloned.1.call-update
  62.7 0.0 copy-start.8
  62.7 0.0 all-gather.2.cloned.1.call-start
  62.8 0.7 all-gather.2.cloned.1.call-update
  63.6 0.1 copy-done.1
  63.7 1.0 copy.20
  64.7 0.6 fusion.58
  66.6 1.3 compare_and_fusion
  67.9 0.1 fusion.24
  68.0 0.9 and_and_fusion
  68.9 1.0 fusion.62
  69.8 1.3 fusion.15
  71.1 52.8 %all-reduce.3.cloned.1.call-done = (bf16[1024,2,128]{2,0,1:T(8,128)(2,1)}, bf16[1024,2,128]{2,0,1:T(8,128)(2,1)}) async-done(((bf16[1024,2,128]{2,0,1:T(8,128)(2,1)}, bf16[1024,2,128]{2,0,1:T(8,128)(2,1)}), (bf16[1024,2,128]{2,0,1:T(8,128)(2,1)}, bf16[1024,2,128]{2,0,1:T(8,128)(2,1)})) %all-reduce.3.cloned.1.call-update) | async-done | bytes 1048592 | tf_op jit(solution)/shard_map/psum | solution.py:24
  123.9 1.7 fusion.59
  125.6 0.4 fusion.16
  126.0 0.1 copy.45
  126.2 22.5 %all_gather.6 = bf16[192,2048]{0,1:T(8,128)(2,1)S(1)} all-gather(bf16[192,512]{0,1:T(8,128)(2,1)S(1)} %pad_maximum_fusion), channel_id=1, replica_groups=mesh['seq'=8,'head'=4] {'head'}, dimensions={1}, use_global_device_ids=true | all-gather | bytes 983040 | tf_op jit(solution)/shard_map/all_gather | solution.py:99
  148.7 19.4 %all-gather.2.cloned.1.call-done = bf16[2048,1344]{0,1:T(8,128)(2,1)} async-done(((bf16[256,1344]{0,1:T(8,128)(2,1)}), bf16[2048,1344]{0,1:T(8,128)(2,1)}) %all-gather.2.cloned.1.call-update) | async-done | bytes 5505040 | tf_op jit(solution)/shard_map/all_gather | solution.py:97
  168.1 2.0 convolution_convert_fusion.3
  170.1 2.0 convolution_convert_fusion.2
  172.1 2.0 convolution_convert_fusion.1
  174.0 2.0 convolution_convert_fusion
  176.0 0.0 copy-start.7
  176.0 0.4 multiply_reduce_fusion
  176.4 11.7 %psum.23 = f32[192]{0:T(256)S(1)} all-reduce(f32[192]{0:T(256)S(1)} %multiply_reduce_fusion), channel_id=1, replica_groups=mesh['seq'=8,'head'=4] {'head'}, use_global_device_ids=true, to_apply=%region_7.8 | all-reduce | flops 192 | bytes 1536 | tf_op jit(solution)/shard_map/psum | solution.py:110
  188.1 0.3 multiply_multiply_fusion
  188.5 0.7 copy-done
  189.1 0.1 fusion.17
  189.2 0.9 copy.37
  190.1 0.8 select_reduce_fusion
  190.9 0.6 div.46
  (53 shorter events, 0.8 us)
Async XLA Ops:
  7.2 116.8 %all-reduce.3.cloned.1.call-start = ((), (), s32[]{:S(2)}) async-start(), calls=%async_computation.1 | async-start | bytes 2097152 | tf_op jit(solution)/shard_map/psum | solution.py:24
  8.2 7.8 %collective-permute-start = (bf16[128,256]{0,1:T(8,128)(2,1)S(1)}, bf16[128,256]{0,1:T(8,128)(2,1)S(1)}, u32[]{:S(2)}, u32[]{:S(2)}) collective-permute-start(bf16[128,256]{0,1:T(8,128)(2,1)S(1)} %copy.21), channel_id=1, source_target_pairs={{0,4},{4,8},{8,12},{12,16},{16,20},{20,24},{24,28},{1,5},{5,9},{9,... | collective-permute-start | bytes 196616 | tf_op jit(solution)/shard_map/ppermute | solution.py:19
  11.5 6.5 %collective-permute-start.8 = (bf16[128,256]{0,1:T(8,128)(2,1)S(1)}, bf16[128,256]{0,1:T(8,128)(2,1)S(1)}, u32[]{:S(2)}, u32[]{:S(2)}) collective-permute-start(bf16[128,256]{0,1:T(8,128)(2,1)S(1)} %copy.23), channel_id=1, source_target_pairs={{0,4},{4,8},{8,12},{12,16},{16,20},{20,24},{24,28},{1,5},{5,9},{9,... | collective-permute-start | bytes 196616 | tf_op jit(solution)/shard_map/ppermute | solution.py:19
  16.0 5.5 %collective-permute-start.1 = (bf16[128,256]{0,1:T(8,128)(2,1)S(1)}, bf16[128,256]{0,1:T(8,128)(2,1)S(1)}, u32[]{:S(2)}, u32[]{:S(2)}) collective-permute-start(bf16[128,256]{0,1:T(8,128)(2,1)S(1)} %collective-permute-done), channel_id=1, source_target_pairs={{0,4},{4,8},{8,12},{12,16},{16,20},{20,24},{24,28},{1,5},{5,9},{9,... | collective-permute-start | bytes 196616 | tf_op jit(solution)/shard_map/ppermute | solution.py:19
  18.0 5.6 %collective-permute-start.9 = (bf16[128,256]{0,1:T(8,128)(2,1)S(1)}, bf16[128,256]{0,1:T(8,128)(2,1)S(1)}, u32[]{:S(2)}, u32[]{:S(2)}) collective-permute-start(bf16[128,256]{0,1:T(8,128)(2,1)S(1)} %collective-permute-done.8), channel_id=1, source_target_pairs={{0,4},{4,8},{8,12},{12,16},{16,20},{20,24},{24,28},{1,5},{5,9},{9,... | collective-permute-start | bytes 196616 | tf_op jit(solution)/shard_map/ppermute | solution.py:19
  21.5 5.6 %collective-permute-start.2 = (bf16[128,256]{0,1:T(8,128)(2,1)S(1)}, bf16[128,256]{0,1:T(8,128)(2,1)S(1)}, u32[]{:S(2)}, u32[]{:S(2)}) collective-permute-start(bf16[128,256]{0,1:T(8,128)(2,1)S(1)} %collective-permute-done.1), channel_id=1, source_target_pairs={{0,4},{4,8},{8,12},{12,16},{16,20},{20,24},{24,28},{1,5},{5,9},{9,... | collective-permute-start | bytes 196616 | tf_op jit(solution)/shard_map/ppermute | solution.py:19
  23.5 6.4 %collective-permute-start.10 = (bf16[128,256]{0,1:T(8,128)(2,1)S(1)}, bf16[128,256]{0,1:T(8,128)(2,1)S(1)}, u32[]{:S(2)}, u32[]{:S(2)}) collective-permute-start(bf16[128,256]{0,1:T(8,128)(2,1)S(1)} %collective-permute-done.9), channel_id=1, source_target_pairs={{0,4},{4,8},{8,12},{12,16},{16,20},{20,24},{24,28},{1,5},{5,9},{9,... | collective-permute-start | bytes 196616 | tf_op jit(solution)/shard_map/ppermute | solution.py:19
  27.1 6.4 %collective-permute-start.3 = (bf16[128,256]{0,1:T(8,128)(2,1)S(1)}, bf16[128,256]{0,1:T(8,128)(2,1)S(1)}, u32[]{:S(2)}, u32[]{:S(2)}) collective-permute-start(bf16[128,256]{0,1:T(8,128)(2,1)S(1)} %collective-permute-done.2), channel_id=1, source_target_pairs={{0,4},{4,8},{8,12},{12,16},{16,20},{20,24},{24,28},{1,5},{5,9},{9,... | collective-permute-start | bytes 196616 | tf_op jit(solution)/shard_map/ppermute | solution.py:19
  29.9 6.5 %collective-permute-start.11 = (bf16[128,256]{0,1:T(8,128)(2,1)S(1)}, bf16[128,256]{0,1:T(8,128)(2,1)S(1)}, u32[]{:S(2)}, u32[]{:S(2)}) collective-permute-start(bf16[128,256]{0,1:T(8,128)(2,1)S(1)} %collective-permute-done.10), channel_id=1, source_target_pairs={{0,4},{4,8},{8,12},{12,16},{16,20},{20,24},{24,28},{1,5},{5,9},{9,... | collective-permute-start | bytes 196616 | tf_op jit(solution)/shard_map/ppermute | solution.py:19
  33.5 6.5 %collective-permute-start.4 = (bf16[128,256]{0,1:T(8,128)(2,1)S(1)}, bf16[128,256]{0,1:T(8,128)(2,1)S(1)}, u32[]{:S(2)}, u32[]{:S(2)}) collective-permute-start(bf16[128,256]{0,1:T(8,128)(2,1)S(1)} %collective-permute-done.3), channel_id=1, source_target_pairs={{0,4},{4,8},{8,12},{12,16},{16,20},{20,24},{24,28},{1,5},{5,9},{9,... | collective-permute-start | bytes 196616 | tf_op jit(solution)/shard_map/ppermute | solution.py:19
  36.4 6.5 %collective-permute-start.12 = (bf16[128,256]{0,1:T(8,128)(2,1)S(1)}, bf16[128,256]{0,1:T(8,128)(2,1)S(1)}, u32[]{:S(2)}, u32[]{:S(2)}) collective-permute-start(bf16[128,256]{0,1:T(8,128)(2,1)S(1)} %collective-permute-done.11), channel_id=1, source_target_pairs={{0,4},{4,8},{8,12},{12,16},{16,20},{20,24},{24,28},{1,5},{5,9},{9,... | collective-permute-start | bytes 196616 | tf_op jit(solution)/shard_map/ppermute | solution.py:19
  39.9 6.5 %collective-permute-start.5 = (bf16[128,256]{0,1:T(8,128)(2,1)S(1)}, bf16[128,256]{0,1:T(8,128)(2,1)S(1)}, u32[]{:S(2)}, u32[]{:S(2)}) collective-permute-start(bf16[128,256]{0,1:T(8,128)(2,1)S(1)} %collective-permute-done.4), channel_id=1, source_target_pairs={{0,4},{4,8},{8,12},{12,16},{16,20},{20,24},{24,28},{1,5},{5,9},{9,... | collective-permute-start | bytes 196616 | tf_op jit(solution)/shard_map/ppermute | solution.py:19
  42.8 6.5 %collective-permute-start.13 = (bf16[128,256]{0,1:T(8,128)(2,1)S(1)}, bf16[128,256]{0,1:T(8,128)(2,1)S(1)}, u32[]{:S(2)}, u32[]{:S(2)}) collective-permute-start(bf16[128,256]{0,1:T(8,128)(2,1)S(1)} %collective-permute-done.12), channel_id=1, source_target_pairs={{0,4},{4,8},{8,12},{12,16},{16,20},{20,24},{24,28},{1,5},{5,9},{9,... | collective-permute-start | bytes 196616 | tf_op jit(solution)/shard_map/ppermute | solution.py:19
  46.4 6.5 %collective-permute-start.6 = (bf16[128,256]{0,1:T(8,128)(2,1)S(1)}, bf16[128,256]{0,1:T(8,128)(2,1)S(1)}, u32[]{:S(2)}, u32[]{:S(2)}) collective-permute-start(bf16[128,256]{0,1:T(8,128)(2,1)S(1)} %collective-permute-done.5), channel_id=1, source_target_pairs={{0,4},{4,8},{8,12},{12,16},{16,20},{20,24},{24,28},{1,5},{5,9},{9,... | collective-permute-start | bytes 196616 | tf_op jit(solution)/shard_map/ppermute | solution.py:19
  49.3 6.5 %collective-permute-start.14 = (bf16[128,256]{0,1:T(8,128)(2,1)S(1)}, bf16[128,256]{0,1:T(8,128)(2,1)S(1)}, u32[]{:S(2)}, u32[]{:S(2)}) collective-permute-start(bf16[128,256]{0,1:T(8,128)(2,1)S(1)} %collective-permute-done.13), channel_id=1, source_target_pairs={{0,4},{4,8},{8,12},{12,16},{16,20},{20,24},{24,28},{1,5},{5,9},{9,... | collective-permute-start | bytes 196616 | tf_op jit(solution)/shard_map/ppermute | solution.py:19
  52.9 6.5 %collective-permute-start.7 = (bf16[128,256]{0,1:T(8,128)(2,1)S(1)}, bf16[128,256]{0,1:T(8,128)(2,1)S(1)}, u32[]{:S(2)}, u32[]{:S(2)}) collective-permute-start(bf16[128,256]{0,1:T(8,128)(2,1)S(1)} %collective-permute-done.6), channel_id=1, source_target_pairs={{0,4},{4,8},{8,12},{12,16},{16,20},{20,24},{24,28},{1,5},{5,9},{9,... | collective-permute-start | bytes 196616 | tf_op jit(solution)/shard_map/ppermute | solution.py:19
  55.8 4.5 %collective-permute-start.15 = (bf16[128,256]{0,1:T(8,128)(2,1)S(1)}, bf16[128,256]{0,1:T(8,128)(2,1)S(1)}, u32[]{:S(2)}, u32[]{:S(2)}) collective-permute-start(bf16[128,256]{0,1:T(8,128)(2,1)S(1)} %collective-permute-done.14), channel_id=1, source_target_pairs={{0,4},{4,8},{8,12},{12,16},{16,20},{20,24},{24,28},{1,5},{5,9},{9,... | collective-permute-start | bytes 196616 | tf_op jit(solution)/shard_map/ppermute | solution.py:19
  61.7 1.8 copy-start.3
  62.7 0.9 copy-start.5
  62.7 0.9 copy-start.4
  62.7 0.9 copy-start.6
  62.7 1.1 copy-start.1
  62.7 2.0 copy-start.8
  62.7 105.4 %all-gather.2.cloned.1.call-start = ((), (), s32[]{:S(2)}) async-start(), calls=%async_computation | async-start | bytes 6193152 | tf_op jit(solution)/shard_map/all_gather | solution.py:97
  123.9 1.7 copy-start.9
  176.0 12.1 %copy-start.7 = (f32[1344]{0:T(1024)S(1)}, f32[1344]{0:T(1024)}, u32[]{:S(2)}) copy-start(f32[1344]{0:T(1024)} %param.20) | copy-start | bytes 16132
  188.1 1.0 copy-start
  189.1 1.0 copy-start.2
Sparse Core Ops, SparseCore 0:
  62.8 61.0 all-reduce.2
  125.8 42.2 all-gather.1
where the time goes:
time: 199 us; the launch traced here: 198 us
  waiting for transfers between devices  73.5 us (37%)
  starting transfers between devices  50 us (25%)
  blocking collectives  34.1 us (17%)
  between operations  15.9 us (8%)
  matrix products  12.3 us (6%)
  local copies, waits for them, and re-layouts  8.52 us (4%)
  other arithmetic  3.97 us (2%)
    psum x1, waiting for transfers between devices, from_root(): return lax.psum(block, axis)  52.8 us
    ppermute x16, starting transfers between devices, passed_along(): lax.ppermute(value, axis, [(source, source + steps) for source in range(i...  50 us
    all_gather x1, blocking collectives, body(): attn_whole = lax.all_gather(stacked, 'head', axis=1, tiled=True)  22.5 us
    all_gather x1, waiting for transfers between devices, body(): weight_share = lax.all_gather(out_weight, 'seq', axis=0, tiled=True)  19.4 us
    psum x1, blocking collectives, body(): squares = lax.psum(jnp.sum(projected * projected, axis=1), 'head')  11.7 us
    dot_general x4, matrix products, body(): jnp.dot(attn_whole[:, group * head_cols:(group + 1) * head_cols], weight_...  7.92 us
    unnamed x40, local copies, waits for them, and re-layouts  5.04 us
  transfers between devices with their start and end apart: 18, of which 3 were waited for; matrix products, arithmetic and copies ran while one was open for 5% of the time, Pallas kernels for 0%

commit v1 on v0

--- a/solution.py
+++ b/solution.py
@@ -1,16 +1,18 @@
+import functools
+
 import jax
 import jax.numpy as jnp
 from jax import lax
+from jax.experimental import pallas as pl
+from jax.experimental.pallas import tpu as pltpu
 from jax.sharding import PartitionSpec as P
 
-D = 5376
 HD = 128
 WINDOW = 1024
-OPT_LEN = 64
-
-
 score_scale = 168.0 ** (-0.5)
+exp2_scale = score_scale * 1.4426950408889634
 epsilon = 1e-06
+VMEM_BYTES = 40 * 1024 * 1024
 
 
 def passed_along(value, axis, steps):
@@ -43,7 +45,7 @@
     return attended.reshape(row_count, -1).astype(jnp.bfloat16)
 
 
-def body(
+def general_body(
     queries,
     keys,
     values,
@@ -57,6 +59,7 @@
     option_bounds,
 ):
     local_rows = queries.shape[0]
+    opt_len = opt_queries.shape[1]
     seq_count = lax.axis_size("seq")
     seq_index = lax.axis_index("seq")
     halo_count = WINDOW // local_rows
@@ -85,8 +88,8 @@
     )
     joined_keys = jnp.concatenate([final_keys, opt_keys[0]], axis=0)
     joined_values = jnp.concatenate([final_values, opt_values[0]], axis=0)
-    positions = jnp.arange(WINDOW + OPT_LEN, dtype=jnp.int32)
-    option_pos = jnp.arange(OPT_LEN, dtype=jnp.int32)
+    positions = jnp.arange(WINDOW + opt_len, dtype=jnp.int32)
+    option_pos = jnp.arange(opt_len, dtype=jnp.int32)
     option_allowed = jnp.where(
         positions[None] < WINDOW,
         positions[None] > option_pos[:, None],
@@ -108,7 +111,8 @@
             jnp.float32
         )
     squares = lax.psum(jnp.sum(projected * projected, axis=1), "head")
-    normed = projected * lax.rsqrt(squares / D + epsilon)[:, None] * norm_gain[None, :]
+    width = norm_gain.shape[0] * lax.axis_size("head")
+    normed = projected * lax.rsqrt(squares / width + epsilon)[:, None] * norm_gain[None, :]
     prefix_out = (prefix_resid.astype(jnp.float32) + normed[:local_rows]).astype(jnp.bfloat16)
     option_full = opt_resid[0].astype(jnp.float32) + normed[local_rows:]
     start_pos = option_bounds[0, 0]
@@ -120,6 +124,276 @@
         jnp.where(chosen[:, None], option_out.astype(jnp.float32), 0.0), axis=0
     ) / (length - start_pos).astype(jnp.float32)
     return (prefix_out, option_out[None], option_summary[None])
+
+
+SMEM = pltpu.MemorySpace.SMEM
+VMEM = pltpu.MemorySpace.VMEM
+
+
+def dot_nt(a, b):
+    return lax.dot_general(a, b, (((1,), (1,)), ((), ())), preferred_element_type=jnp.float32)
+
+
+def dot_nn(a, b):
+    return lax.dot_general(a, b, (((1,), (0,)), ((), ())), preferred_element_type=jnp.float32)
+
+
+def call(kernel, out_shape, count, flops=0, moved=0, in_specs=None, scratch=()):
+    many = isinstance(out_shape, (list, tuple))
+    return pl.pallas_call(
+        kernel,
+        out_shape=out_shape,
+        in_specs=in_specs or [pl.BlockSpec(memory_space=VMEM)] * count,
+        out_specs=[pl.BlockSpec(memory_space=VMEM)] * len(out_shape)
+        if many
+        else pl.BlockSpec(memory_space=VMEM),
+        scratch_shapes=list(scratch),
+        cost_estimate=pl.CostEstimate(flops=flops, bytes_accessed=moved, transcendentals=0),
+        compiler_params=pltpu.CompilerParams(vmem_limit_bytes=VMEM_BYTES),
+    )
+
+
+def masks(s):
+    parity = lax.rem(s, 2)
+    return (0 * parity, 4 - 2 * parity, 2 + 2 * parity, 0 * parity + 6)
+
+
+def pack_kernel(q, kt, vt, oq, ok, ov, keep_kv, send_kv, keep_q, send_q):
+    parity = lax.rem(lax.axis_index("seq"), 2)
+    rows, opt = q.shape[0], oq.shape[1]
+    wide = q.shape[1] // 2
+    for kv, qs, head in ((keep_kv, keep_q, parity), (send_kv, send_q, 1 - parity)):
+        at = pl.multiple_of(head * HD, HD)
+        at_q = pl.multiple_of(head * wide, wide)
+        kv[0:HD, :] = kt[pl.ds(at, HD), :]
+        kv[HD : 2 * HD, :] = vt[pl.ds(at, HD), :]
+        qs[0:rows, :] = q[:, pl.ds(at_q, wide)]
+        qs[rows : rows + opt, :] = oq[0, :, pl.ds(at_q, wide)]
+        qs[rows + opt : rows + 2 * opt, 0:HD] = ok[0, :, pl.ds(at, HD)]
+        qs[rows + opt : rows + 2 * opt, HD : 2 * HD] = ov[0, :, pl.ds(at, HD)]
+
+
+def attn_kernel(flip, rows, opt, kv0, kv1, kv2, kv3, qs, out):
+    s = lax.axis_index("seq")
+    slots = (kv0, kv1, kv2, kv3)
+    keys = jnp.concatenate(
+        [kv[b * 2 * HD : b * 2 * HD + HD, :] for kv in slots for b in (0, 1)], axis=1
+    )
+    values = jnp.concatenate(
+        [kv[b * 2 * HD + HD : (b + 1) * 2 * HD, :] for kv in slots for b in (0, 1)], axis=1
+    )
+    lane = lax.broadcasted_iota(jnp.int32, (1, rows), 1)
+    key_pos = jnp.concatenate(
+        [((s ^ m) ^ b) * rows + lane for m in masks(s) for b in (0, 1)], axis=1
+    )
+    query_pos = (s ^ flip) * rows + lax.broadcasted_iota(jnp.int32, (rows, 1), 0)
+    heads = qs.shape[1] // HD
+    for h in range(heads):
+        scores = dot_nn(qs[0:rows, h * HD : (h + 1) * HD], keys)
+        scores = jnp.where(key_pos <= query_pos, scores, -jnp.inf)
+        top = jnp.max(scores, axis=1, keepdims=True)
+        weights = jnp.exp2((scores - top) * exp2_scale)
+        total = jnp.sum(weights, axis=1, keepdims=True)
+        mixed = dot_nt(weights.astype(jnp.bfloat16), values)
+        out[0:rows, h * HD : (h + 1) * HD] = (mixed / total).astype(jnp.bfloat16)
+    oq = jnp.concatenate([qs[rows : rows + opt, h * HD : (h + 1) * HD] for h in range(heads)], axis=0)
+    own_keys = qs[rows + opt : rows + 2 * opt, 0:HD]
+    own_values = qs[rows + opt : rows + 2 * opt, HD : 2 * HD]
+    step = lax.rem(lax.broadcasted_iota(jnp.int32, (heads * opt, 1), 0), opt)
+    scores = jnp.where(key_pos > step, dot_nn(oq, keys), -jnp.inf)
+    own = dot_nt(oq, own_keys)
+    own = jnp.where(lax.broadcasted_iota(jnp.int32, (1, opt), 1) <= step, own, -jnp.inf)
+    top = jnp.maximum(
+        jnp.max(scores, axis=1, keepdims=True), jnp.max(own, axis=1, keepdims=True)
+    )
+    weights = jnp.exp2((scores - top) * exp2_scale)
+    own = jnp.exp2((own - top) * exp2_scale)
+    total = jnp.sum(weights, axis=1, keepdims=True) + jnp.sum(own, axis=1, keepdims=True)
+    mixed = dot_nt(weights.astype(jnp.bfloat16), values) + dot_nn(
+        own.astype(jnp.bfloat16), own_values
+    )
+    mixed = (mixed / total).astype(jnp.bfloat16)
+    for h in range(heads):
+        out[rows : rows + opt, h * HD : (h + 1) * HD] = mixed[h * opt : (h + 1) * opt]
+
+
+def project_kernel(w0, w1, w2, w3, a0, a1, a2, a3, out, held, placed, sems):
+    copies = [
+        pltpu.make_async_copy(w, held.at[j], sems.at[j]) for j, w in enumerate((w0, w1, w2, w3))
+    ]
+    for copy in copies:
+        copy.start()
+    s = lax.axis_index("seq")
+    z = lax.axis_index("head")
+    place = z ^ (z >> 1)
+    for t, a in enumerate((a0, a1, a2, a3)):
+        source = lax.rem(place + (4 - t), 4)
+        placed[source ^ (source >> 1)] = a[...]
+    for copy in copies:
+        copy.wait()
+    blocks = [placed[(s ^ m) >> 1] for m in masks(s)]
+    features = out.shape[0]
+    part = features // 3
+    for n in range(3):
+        total = dot_nt(held[0, n * part : (n + 1) * part, :], blocks[0])
+        for j in range(1, 4):
+            total += dot_nt(held[j, n * part : (n + 1) * part, :], blocks[j])
+        out[n * part : (n + 1) * part, :] = total.astype(out.dtype)
+
+
+def square_kernel(own, received, projected, squares):
+    total = own[...] + received[...].astype(jnp.float32)
+    projected[...] = total
+    squares[...] = jnp.sum(total * total, axis=0, keepdims=True)
+
+
+def spread_kernel(gain, out):
+    out[...] = jnp.broadcast_to(gain[...], (out.shape[1], out.shape[0])).T
+
+
+def finish_kernel(
+    rows, width, bounds, projected, s0, s1, s2, s3, resid_t, opt_resid, gain, out_t, opt_out, summary
+):
+    squares = s0[...] + s1[...] + s2[...] + s3[...]
+    scale = lax.rsqrt(squares / width + epsilon)
+    spread = gain[...]
+    normed = projected[:, 0:rows] * scale[:, 0:rows] * spread
+    out_t[...] = (resid_t[...].astype(jnp.float32) + normed).astype(jnp.bfloat16)
+    opt = opt_resid.shape[1]
+    normed = projected[:, rows : rows + opt] * scale[:, rows : rows + opt] * spread[:, 0:opt]
+    full = opt_resid[0].astype(jnp.float32) + normed.T
+    start, length = bounds[0, 0], bounds[0, 1]
+    position = lax.broadcasted_iota(jnp.int32, (opt, 1), 0)
+    kept = jnp.where(position < length, full, 0.0).astype(jnp.bfloat16)
+    opt_out[0] = kept
+    chosen = (position < length) & (position >= start)
+    count = (length - start).astype(jnp.float32)
+    summary[...] = (
+        jnp.sum(jnp.where(chosen, kept.astype(jnp.float32), 0.0), axis=0, keepdims=True) / count
+    )
+
+
+def paired_body(
+    queries,
+    keys,
+    values,
+    prefix_resid,
+    opt_queries,
+    opt_keys,
+    opt_values,
+    opt_resid,
+    out_weight,
+    norm_gain,
+    option_bounds,
+):
+    rows, opt = queries.shape[0], opt_queries.shape[1]
+    features = out_weight.shape[1]
+    wide = queries.shape[1] // 2
+    seq = range(lax.axis_size("seq"))
+    bf16, f32 = jnp.bfloat16, jnp.float32
+    shape = jax.ShapeDtypeStruct
+    pair = [(s, s ^ 1) for s in seq]
+    first = [(s, s ^ (2 if s % 2 else 4)) for s in seq]
+    second = [(s, s ^ (4 if s % 2 else 2)) for s in seq]
+    ring = [(0, 1), (1, 3), (3, 2), (2, 0)]
+
+    def turned(value, steps):
+        count = lax.axis_size("head")
+        return lax.ppermute(value, "head", [(i, (i + steps) % count) for i in range(count)])
+
+    weight = out_weight.T
+    weight_1 = lax.ppermute(weight, "seq", first)
+
+    keep_kv, send_kv, keep_q, send_q = call(
+        pack_kernel,
+        [shape((2 * HD, rows), bf16)] * 2 + [shape((rows + 2 * opt, wide), bf16)] * 2,
+        6,
+    )(queries, keys.T, values.T, opt_queries, opt_keys, opt_values)
+    pair_kv = lax.ppermute(send_kv, "seq", pair)
+    kv_0 = jnp.concatenate([keep_kv, pair_kv], axis=0)
+    kv_1 = lax.ppermute(kv_0, "seq", first)
+    kv_2 = lax.ppermute(kv_0, "seq", second)
+    pair_q = lax.ppermute(send_q, "seq", pair)
+    kv_3 = lax.ppermute(kv_1, "seq", second)
+
+    weight_2 = lax.ppermute(weight, "seq", second)
+    weight_3 = lax.ppermute(weight_1, "seq", second)
+    weights = (weight, weight_1, weight_2, weight_3)
+
+    def attention(flip, q):
+        return call(
+            functools.partial(attn_kernel, flip, rows, opt),
+            shape((rows + opt, wide), bf16),
+            5,
+            flops=4 * (rows + opt) * wide * WINDOW,
+        )(kv_0, kv_1, kv_2, kv_3, q)
+
+    def gathered(block):
+        blocks = [block]
+        for _ in range(3):
+            blocks.append(lax.ppermute(blocks[-1], "head", ring))
+        return blocks
+
+    def project(blocks, dtype):
+        return call(
+            project_kernel,
+            shape((features, rows + opt), dtype),
+            8,
+            flops=8 * features * wide * (rows + opt),
+            moved=8 * features * wide,
+            in_specs=[pl.BlockSpec(memory_space=pl.ANY)] * 4
+            + [pl.BlockSpec(memory_space=VMEM)] * 4,
+            scratch=[
+                pltpu.VMEM((4, features, wide), bf16),
+                pltpu.VMEM((4, rows + opt, wide), bf16),
+                pltpu.SemaphoreType.DMA((4,)),
+            ],
+        )(*weights, *blocks)
+
+    pair_blocks = gathered(attention(1, pair_q))
+    own_blocks = gathered(attention(0, keep_q))
+    received = lax.ppermute(project(pair_blocks, bf16), "seq", pair)
+    own = project(own_blocks, f32)
+    projected, squares = call(
+        square_kernel, [shape((features, rows + opt), f32), shape((1, rows + opt), f32)], 2
+    )(own, received)
+    spread = call(spread_kernel, shape((features, rows), f32), 1)(norm_gain[None])
+    out_t, opt_out, summary = call(
+        functools.partial(finish_kernel, rows, float(features * lax.axis_size("head"))),
+        [
+            shape((features, rows), bf16),
+            shape((1, opt, features), bf16),
+            shape((1, features), f32),
+        ],
+        9,
+        in_specs=[pl.BlockSpec(memory_space=SMEM)] + [pl.BlockSpec(memory_space=VMEM)] * 8,
+    )(
+        option_bounds,
+        projected,
+        squares,
+        turned(squares, 1),
+        turned(squares, 2),
+        turned(squares, 3),
+        prefix_resid.T,
+        opt_resid,
+        spread,
+    )
+    return out_t.T, opt_out, summary
+
+
+def body(*args):
+    queries, keys, out_weight = args[0], args[1], args[8]
+    seq, head = lax.axis_size("seq"), lax.axis_size("head")
+    paired = (
+        seq == 8
+        and head == 4
+        and seq * queries.shape[0] == WINDOW
+        and queries.shape[0] == HD
+        and keys.shape[1] == 2 * HD
+        and out_weight.shape[0] * 2 == queries.shape[1]
+        and out_weight.shape[0] * seq == queries.shape[1] * head
+    )
+    return paired_body(*args) if paired else general_body(*args)
 
 
 def solution(mesh):

time: 199 us -> 89.5 us (0.45)
  blocking collectives: 34.1 us -> 0 us
  waiting for transfers between devices: 73.5 us -> 46.1 us
  starting transfers between devices: 50 us -> 24.5 us
  between operations: 15.9 us -> 0.8 us
  matrix products: 12.3 us -> 0 us
  Pallas kernels: 0 us -> 8.14 us
  other arithmetic: 3.97 us -> 0 us
    psum x1 -> x0, waiting for transfers between devices: 52.8 us -> none  [from_root(): return lax.psum(block, axis)]
    ppermute x16 -> x18, waiting for transfers between devices: 0.57 us -> 46.1 us  [the longest x6 24.8 us: gathered(): blocks.append(lax.ppermute(blocks[-1], 'head', ring))]
    ppermute x16 -> x18, starting transfers between devices: 50 us -> 24.5 us  [the longest x6 9.48 us: gathered(): blocks.append(lax.ppermute(blocks[-1], 'head', ring))]
    all_gather x1 -> x0, blocking collectives: 22.5 us -> none  [body(): attn_whole = lax.all_gather(stacked, 'head', axis=1, tiled=True)]
    all_gather x1 -> x0, waiting for transfers between devices: 19.4 us -> none  [body(): weight_share = lax.all_gather(out_weight, 'seq', axis=0, tiled=True)]
    psum x1 -> x0, blocking collectives: 11.7 us -> none  [body(): squares = lax.psum(jnp.sum(projected * projected, axis=1), 'head')]
    dot_general x6 -> x0, matrix products: 9.6 us -> none  [the longest x4 7.92 us: body(): jnp.dot(attn_whole[:, group * head_cols:(group + 1) * head_cols], weight_...]
    pallas_call x0 -> x8, Pallas kernels: none -> 8.14 us  [the longest x2 3.93 us: project(): call(project_kernel, shape((features, rows + opt), dtype), 8, flops=8 * f...]
  transfers between devices with their start and end apart: 18 -> 18, of which waited for: 3 -> 13; matrix products, arithmetic and copies ran while one was open for 5% -> 2% of each run, Pallas kernels for 0% -> 5%
where the time goes in v1:
time: 89.5 us; the launch traced here: 89 us
  waiting for transfers between devices  46.1 us (52%)
  starting transfers between devices  24.5 us (27%)
  local copies, waits for them, and re-layouts  9.55 us (11%)
  Pallas kernels  8.14 us (9%)
    ppermute x6, waiting for transfers between devices, gathered(): blocks.append(lax.ppermute(blocks[-1], 'head', ring))  24.8 us
    ppermute x6, starting transfers between devices, gathered(): blocks.append(lax.ppermute(blocks[-1], 'head', ring))  9.48 us
    ppermute x1, waiting for transfers between devices, paired_body(): weight_1 = lax.ppermute(weight, 'seq', first)  9.26 us
    unnamed x25, local copies, waits for them, and re-layouts  7.13 us
    ppermute x3, starting transfers between devices, turned(): lax.ppermute(value, 'head', [(i, (i + steps) % count) for i in range(coun...  4.94 us
    pallas_call x2, Pallas kernels, project(): call(project_kernel, shape((features, rows + opt), dtype), 8, flops=8 * f...  3.93 us
    ppermute x1, waiting for transfers between devices, paired_body(): kv_2 = lax.ppermute(kv_0, 'seq', second)  3.86 us
    ppermute x1, waiting for transfers between devices, paired_body(): kv_1 = lax.ppermute(kv_0, 'seq', first)  3.42 us
  transfers between devices with their start and end apart: 18, of which 13 were waited for; matrix products, arithmetic and copies ran while one was open for 2% of the time, Pallas kernels for 5%

profile of v1, /device:TPU:0, one launch (start us, length us, event | category | flops | bytes accessed | tf_op | source)
XLA Modules:
  0.0 89.0 jit_solution(7714688832602661546)
XLA Ops:
  0.6 0.0 copy-start
  0.6 3.0 %collective-permute-start = (bf16[1344,256]{1,0:T(8,128)(2,1)}, bf16[1344,256]{1,0:T(8,128)(2,1)S(1)}, u32[]{:S(2)}, u32[]{:S(2)}) collective-permute-start(bf16[1344,256]{1,0:T(8,128)(2,1)} %bitcast.5), channel_id=1, source_target_pairs={{0,16},{4,12},{8,24},{12,4},{16,0},{20,28},{24,8},{28,20},{1,17},{... | collective-permute-start | bytes 2064392 | tf_op jit(solution)/shard_map/ppermute | solution.py:305
  3.7 1.5 %collective-permute-start.1 = (bf16[1344,256]{1,0:T(8,128)(2,1)}, bf16[1344,256]{1,0:T(8,128)(2,1)S(1)}, u32[]{:S(2)}, u32[]{:S(2)}) collective-permute-start(bf16[1344,256]{1,0:T(8,128)(2,1)} %bitcast.6), channel_id=1, source_target_pairs={{0,8},{4,20},{8,0},{12,28},{16,24},{20,4},{24,16},{28,12},{1,9},{5... | collective-permute-start | bytes 2064392 | tf_op jit(solution)/shard_map/ppermute | solution.py:319
  5.2 0.9 %copy.16 = bf16[128,256]{0,1:T(8,128)(2,1)S(1)} copy(bf16[128,256]{1,0:T(8,128)(2,1)} %param.12) | data formatting | bytes 131072 | tf_op args[1]
  6.1 1.0 %copy.17 = bf16[128,256]{0,1:T(8,128)(2,1)S(1)} copy(bf16[128,256]{1,0:T(8,128)(2,1)} %param.13) | data formatting | bytes 131072 | tf_op args[2]
  7.1 0.0 copy-start.5
  7.1 0.9 %copy-done.5 = bf16[128,512]{1,0:T(8,128)(2,1)S(1)} copy-done((bf16[128,512]{1,0:T(8,128)(2,1)S(1)}, bf16[128,512]{1,0:T(8,128)(2,1)}, u32[]{:S(2)}) %copy-start.5) | copy-done | bytes 131096
  8.0 0.8 copy-done.6
  8.8 0.8 copy-done.7
  9.6 0.8 copy-done.8
  10.4 0.1 collective-permute-start.3
  10.5 9.3 %collective-permute-done.w1 = bf16[1344,256]{1,0:T(8,128)(2,1)S(1)} collective-permute-done((bf16[1344,256]{1,0:T(8,128)(2,1)}, bf16[1344,256]{1,0:T(8,128)(2,1)S(1)}, u32[]{:S(2)}, u32[]{:S(2)}) %collective-permute-start) | collective-permute-done | bytes 688160 | tf_op jit(solution)/shard_map/ppermute | solution.py:305
  19.7 1.4 %collective-permute-start.2 = (bf16[1344,256]{1,0:T(8,128)(2,1)S(1)}, bf16[1344,256]{1,0:T(8,128)(2,1)S(1)}, u32[]{:S(2)}, u32[]{:S(2)}) collective-permute-start(bf16[1344,256]{1,0:T(8,128)(2,1)S(1)} %collective-permute-done.w1), channel_id=1, source_target_pairs={{0,8},{4,20},{8,0},{12,28},{16,24},{20,4},{24,16},{28,12},{1,9},{5... | collective-permute-start | bytes 2064392 | tf_op jit(solution)/shard_map/ppermute | solution.py:320
  21.1 0.0 collective-permute-done.3
  21.1 1.7 %collective-permute-start.4 = (bf16[512,128]{1,0:T(8,128)(2,1)S(1)}, bf16[512,128]{1,0:T(8,128)(2,1)S(1)}, u32[]{:S(2)}, u32[]{:S(2)}) collective-permute-start(bf16[512,128]{1,0:T(8,128)(2,1)S(1)} %constant_dynamic-update-slice_fusion.kv0), channel_id=1, source_target_pairs={{0,16},{4,12},{8,24},{12,4},{16,0},{20,28},{24,8},{28,20},{1,17},{... | collective-permute-start | bytes 393224 | tf_op jit(solution)/shard_map/ppermute | solution.py:314
  22.9 0.0 collective-permute-start.10
  22.9 1.3 %collective-permute-start.5 = (bf16[512,128]{1,0:T(8,128)(2,1)S(1)}, bf16[512,128]{1,0:T(8,128)(2,1)S(1)}, u32[]{:S(2)}, u32[]{:S(2)}) collective-permute-start(bf16[512,128]{1,0:T(8,128)(2,1)S(1)} %constant_dynamic-update-slice_fusion.kv0), channel_id=1, source_target_pairs={{0,8},{4,20},{8,0},{12,28},{16,24},{20,4},{24,16},{28,12},{1,9},{5... | collective-permute-start | bytes 393224 | tf_op jit(solution)/shard_map/ppermute | solution.py:315
  24.2 3.4 %collective-permute-done.4.kv1 = bf16[512,128]{1,0:T(8,128)(2,1)S(1)} collective-permute-done((bf16[512,128]{1,0:T(8,128)(2,1)S(1)}, bf16[512,128]{1,0:T(8,128)(2,1)S(1)}, u32[]{:S(2)}, u32[]{:S(2)}) %collective-permute-start.4) | collective-permute-done | bytes 131104 | tf_op jit(solution)/shard_map/ppermute | solution.py:314
  27.7 1.0 %collective-permute-start.6 = (bf16[512,128]{1,0:T(8,128)(2,1)S(1)}, bf16[512,128]{1,0:T(8,128)(2,1)S(1)}, u32[]{:S(2)}, u32[]{:S(2)}) collective-permute-start(bf16[512,128]{1,0:T(8,128)(2,1)S(1)} %collective-permute-done.4.kv1), channel_id=1, source_target_pairs={{0,8},{4,20},{8,0},{12,28},{16,24},{20,4},{24,16},{28,12},{1,9},{5... | collective-permute-start | bytes 393224 | tf_op jit(solution)/shard_map/ppermute | solution.py:317
  28.6 0.0 collective-permute-done.10.qs
  28.6 3.9 %collective-permute-done.5.kv2 = bf16[512,128]{1,0:T(8,128)(2,1)S(1)} collective-permute-done((bf16[512,128]{1,0:T(8,128)(2,1)S(1)}, bf16[512,128]{1,0:T(8,128)(2,1)S(1)}, u32[]{:S(2)}, u32[]{:S(2)}) %collective-permute-start.5) | collective-permute-done | bytes 131104 | tf_op jit(solution)/shard_map/ppermute | solution.py:315
  32.5 1.4 %collective-permute-done.6.kv3 = bf16[512,128]{1,0:T(8,128)(2,1)S(1)} collective-permute-done((bf16[512,128]{1,0:T(8,128)(2,1)S(1)}, bf16[512,128]{1,0:T(8,128)(2,1)S(1)}, u32[]{:S(2)}, u32[]{:S(2)}) %collective-permute-start.6) | collective-permute-done | bytes 131104 | tf_op jit(solution)/shard_map/ppermute | solution.py:317
  33.9 1.1 %shard_map.133.a0 = bf16[192,256]{1,0:T(8,128)(2,1)S(1)} custom-call(bf16[512,128]{1,0:T(8,128)(2,1)S(1)} %constant_dynamic-update-slice_fusion.kv0, bf16[512,128]{1,0:T(8,128)(2,1)S(1)} %collective-permute-done.4.kv1, bf16[512,128]{1,0:T(8,128)(2,1)S(1)} %collective-permute-done.5.kv2, bf16[512,128]{1,0:T(8,128)(2,1)S(1)} %collective-permute-done.6.kv3, ...), custom_call_target="tpu_custom_call" | custom-call | flops 201326592 | tf_op jit(solution)/shard_map/pallas_call | solution.py:324
  35.0 2.1 %collective-permute-start.11 = (bf16[192,256]{1,0:T(8,128)(2,1)S(1)}, bf16[192,256]{1,0:T(8,128)(2,1)S(1)}, u32[]{:S(2)}, u32[]{:S(2)}) collective-permute-start(bf16[192,256]{1,0:T(8,128)(2,1)S(1)} %shard_map.133.a0), channel_id=1, source_target_pairs={{0,1},{1,3},{3,2},{2,0},{4,5},{5,7},{7,6},{6,4},{8,9},{9,11},{11,1... | collective-permute-start | bytes 294920 | tf_op jit(solution)/shard_map/ppermute | solution.py:334
  37.1 3.6 %collective-permute-done.11.a1 = bf16[192,256]{1,0:T(8,128)(2,1)S(1)} collective-permute-done((bf16[192,256]{1,0:T(8,128)(2,1)S(1)}, bf16[192,256]{1,0:T(8,128)(2,1)S(1)}, u32[]{:S(2)}, u32[]{:S(2)}) %collective-permute-start.11) | collective-permute-done | bytes 98336 | tf_op jit(solution)/shard_map/ppermute | solution.py:334
  40.7 1.2 %collective-permute-start.12 = (bf16[192,256]{1,0:T(8,128)(2,1)S(1)}, bf16[192,256]{1,0:T(8,128)(2,1)S(1)}, u32[]{:S(2)}, u32[]{:S(2)}) collective-permute-start(bf16[192,256]{1,0:T(8,128)(2,1)S(1)} %collective-permute-done.11.a1), channel_id=1, source_target_pairs={{0,1},{1,3},{3,2},{2,0},{4,5},{5,7},{7,6},{6,4},{8,9},{9,11},{11,1... | collective-permute-start | bytes 294920 | tf_op jit(solution)/shard_map/ppermute | solution.py:334
  41.9 4.7 %collective-permute-done.12.a2 = bf16[192,256]{1,0:T(8,128)(2,1)S(1)} collective-permute-done((bf16[192,256]{1,0:T(8,128)(2,1)S(1)}, bf16[192,256]{1,0:T(8,128)(2,1)S(1)}, u32[]{:S(2)}, u32[]{:S(2)}) %collective-permute-start.12) | collective-permute-done | bytes 98336 | tf_op jit(solution)/shard_map/ppermute | solution.py:334
  46.6 1.5 %collective-permute-start.13 = (bf16[192,256]{1,0:T(8,128)(2,1)S(1)}, bf16[192,256]{1,0:T(8,128)(2,1)S(1)}, u32[]{:S(2)}, u32[]{:S(2)}) collective-permute-start(bf16[192,256]{1,0:T(8,128)(2,1)S(1)} %collective-permute-done.12.a2), channel_id=1, source_target_pairs={{0,1},{1,3},{3,2},{2,0},{4,5},{5,7},{7,6},{6,4},{8,9},{9,11},{11,1... | collective-permute-start | bytes 294920 | tf_op jit(solution)/shard_map/ppermute | solution.py:334
  48.1 4.0 %collective-permute-done.13.a3 = bf16[192,256]{1,0:T(8,128)(2,1)S(1)} collective-permute-done((bf16[192,256]{1,0:T(8,128)(2,1)S(1)}, bf16[192,256]{1,0:T(8,128)(2,1)S(1)}, u32[]{:S(2)}, u32[]{:S(2)}) %collective-permute-start.13) | collective-permute-done | bytes 98336 | tf_op jit(solution)/shard_map/ppermute | solution.py:334
  52.1 0.0 collective-permute-done.1.w2
  52.1 0.0 collective-permute-done.2.w3
  52.1 0.0 copy-done
  52.1 2.0 %shard_map.134 = bf16[1344,192]{1,0:T(8,128)(2,1)S(1)} custom-call(bf16[1344,256]{1,0:T(8,128)(2,1)S(1)} %bitcast.7, bf16[1344,256]{1,0:T(8,128)(2,1)S(1)} %collective-permute-done.w1, bf16[1344,256]{1,0:T(8,128)(2,1)S(1)} %collective-permute-done.1.w2, bf16[1344,256]{1,0:T(8,128)(2,1)S(1)} %collective-permute-done.2.w3, ...), custom_call_target="tpu_custom_call" | custom-call | flops 528482304 | bytes 2752512 | tf_op jit(solution)/shard_map/pallas_call | solution.py:338
  54.1 0.0 copy-start.1
  54.1 0.8 copy-done.1
  54.9 1.1 %copy.18 = bf16[1344,192]{0,1:T(8,128)(2,1)} copy(bf16[1344,192]{1,0:T(8,128)(2,1)S(1)} %shard_map.134) | data formatting | bytes 1032192 | tf_op jit(solution)/shard_map/pallas_call | solution.py:338
  56.0 0.0 collective-permute-start.14
  56.0 1.1 %shard_map.131.a0 = bf16[192,256]{1,0:T(8,128)(2,1)S(1)} custom-call(bf16[512,128]{1,0:T(8,128)(2,1)S(1)} %constant_dynamic-update-slice_fusion.kv0, bf16[512,128]{1,0:T(8,128)(2,1)S(1)} %collective-permute-done.4.kv1, bf16[512,128]{1,0:T(8,128)(2,1)S(1)} %collective-permute-done.5.kv2, bf16[512,128]{1,0:T(8,128)(2,1)S(1)} %collective-permute-done.6.kv3, ...), custom_call_target="tpu_custom_call" | custom-call | flops 201326592 | tf_op jit(solution)/shard_map/pallas_call | solution.py:324
  57.1 1.6 %collective-permute-start.7 = (bf16[192,256]{1,0:T(8,128)(2,1)S(1)}, bf16[192,256]{1,0:T(8,128)(2,1)S(1)}, u32[]{:S(2)}, u32[]{:S(2)}) collective-permute-start(bf16[192,256]{1,0:T(8,128)(2,1)S(1)} %shard_map.131.a0), channel_id=1, source_target_pairs={{0,1},{1,3},{3,2},{2,0},{4,5},{5,7},{7,6},{6,4},{8,9},{9,11},{11,1... | collective-permute-start | bytes 294920 | tf_op jit(solution)/shard_map/ppermute | solution.py:334
  58.7 4.5 %collective-permute-done.7.a1 = bf16[192,256]{1,0:T(8,128)(2,1)S(1)} collective-permute-done((bf16[192,256]{1,0:T(8,128)(2,1)S(1)}, bf16[192,256]{1,0:T(8,128)(2,1)S(1)}, u32[]{:S(2)}, u32[]{:S(2)}) %collective-permute-start.7) | collective-permute-done | bytes 98336 | tf_op jit(solution)/shard_map/ppermute | solution.py:334
  63.3 1.5 %collective-permute-start.8 = (bf16[192,256]{1,0:T(8,128)(2,1)S(1)}, bf16[192,256]{1,0:T(8,128)(2,1)S(1)}, u32[]{:S(2)}, u32[]{:S(2)}) collective-permute-start(bf16[192,256]{1,0:T(8,128)(2,1)S(1)} %collective-permute-done.7.a1), channel_id=1, source_target_pairs={{0,1},{1,3},{3,2},{2,0},{4,5},{5,7},{7,6},{6,4},{8,9},{9,11},{11,1... | collective-permute-start | bytes 294920 | tf_op jit(solution)/shard_map/ppermute | solution.py:334
  64.8 4.0 %collective-permute-done.8.a2 = bf16[192,256]{1,0:T(8,128)(2,1)S(1)} collective-permute-done((bf16[192,256]{1,0:T(8,128)(2,1)S(1)}, bf16[192,256]{1,0:T(8,128)(2,1)S(1)}, u32[]{:S(2)}, u32[]{:S(2)}) %collective-permute-start.8) | collective-permute-done | bytes 98336 | tf_op jit(solution)/shard_map/ppermute | solution.py:334
  68.8 1.6 %collective-permute-start.9 = (bf16[192,256]{1,0:T(8,128)(2,1)S(1)}, bf16[192,256]{1,0:T(8,128)(2,1)S(1)}, u32[]{:S(2)}, u32[]{:S(2)}) collective-permute-start(bf16[192,256]{1,0:T(8,128)(2,1)S(1)} %collective-permute-done.8.a2), channel_id=1, source_target_pairs={{0,1},{1,3},{3,2},{2,0},{4,5},{5,7},{7,6},{6,4},{8,9},{9,11},{11,1... | collective-permute-start | bytes 294920 | tf_op jit(solution)/shard_map/ppermute | solution.py:334
  70.4 3.9 %collective-permute-done.9.a3 = bf16[192,256]{1,0:T(8,128)(2,1)S(1)} collective-permute-done((bf16[192,256]{1,0:T(8,128)(2,1)S(1)}, bf16[192,256]{1,0:T(8,128)(2,1)S(1)}, u32[]{:S(2)}, u32[]{:S(2)}) %collective-permute-start.9) | collective-permute-done | bytes 98336 | tf_op jit(solution)/shard_map/ppermute | solution.py:334
  74.3 1.1 %copy-done.2 = bf16[1344,256]{1,0:T(8,128)(2,1)S(1)} copy-done((bf16[1344,256]{1,0:T(8,128)(2,1)S(1)}, bf16[1344,256]{1,0:T(8,128)(2,1)}, u32[]{:S(2)}) %copy-start.2) | copy-done | bytes 688152
  75.4 2.0 %shard_map.132.own = f32[1344,192]{1,0:T(8,128)S(1)} custom-call(bf16[1344,256]{1,0:T(8,128)(2,1)S(1)} %bitcast.8, bf16[1344,256]{1,0:T(8,128)(2,1)S(1)} %collective-permute-done.w1, bf16[1344,256]{1,0:T(8,128)(2,1)S(1)} %collective-permute-done.1.w2, bf16[1344,256]{1,0:T(8,128)(2,1)S(1)} %copy-done.2, bf16[192,256]{1,0:T(8,128)(2,1)S(1)} %shard_map.131.a0, ...), custom_call_target="tpu_custom_call" | custom-call | flops 528482304 | bytes 2752512 | tf_op jit(solution)/shard_map/pallas_call | solution.py:338
  77.4 0.0 copy-start.10
  77.4 0.0 collective-permute-done.14
  77.4 1.3 %copy.19.received = bf16[1344,192]{1,0:T(8,128)(2,1)S(1)} copy(bf16[1344,192]{0,1:T(8,128)(2,1)} %collective-permute-done.14) | data formatting | bytes 1032192 | tf_op jit(solution)/shard_map/ppermute | solution.py:355
  78.7 0.0 copy-start.3
  78.7 0.0 copy-start.4
  78.7 0.0 copy-start.9
  78.7 0.2 shard_map.135
  79.0 1.6 %collective-permute-start.15 = (f32[1,192]{1,0:T(1,128)S(1)}, f32[1,192]{1,0:T(1,128)S(1)}, u32[]{:S(2)}, u32[]{:S(2)}) collective-permute-start(f32[1,192]{1,0:T(1,128)S(1)} %get-tuple-element.17.s0), channel_id=1, source_target_pairs={{0,1},{1,2},{2,3},{3,0},{4,5},{5,6},{6,7},{7,4},{8,9},{9,10},{10,1... | collective-permute-start | bytes 2312 | tf_op jit(solution)/shard_map/ppermute | solution.py:302
  80.6 3.3 %collective-permute-start.16 = (f32[1,192]{1,0:T(1,128)S(1)}, f32[1,192]{1,0:T(1,128)S(1)}, u32[]{:S(2)}, u32[]{:S(2)}) collective-permute-start(f32[1,192]{1,0:T(1,128)S(1)} %get-tuple-element.17.s0), channel_id=1, source_target_pairs={{0,2},{1,3},{2,0},{3,1},{4,6},{5,7},{6,4},{7,5},{8,10},{9,11},{10,... | collective-permute-start | bytes 2312 | tf_op jit(solution)/shard_map/ppermute | solution.py:302
  83.9 0.0 collective-permute-start.17
  83.9 0.0 copy-done.10
  83.9 0.2 shard_map.136.gain
  84.2 0.7 collective-permute-done.15.s1
  84.9 0.6 collective-permute-done.16.s2
  85.4 2.0 %collective-permute-done.17.s3 = f32[1,192]{1,0:T(1,128)S(1)} collective-permute-done((f32[1,192]{1,0:T(1,128)S(1)}, f32[1,192]{1,0:T(1,128)S(1)}, u32[]{:S(2)}, u32[]{:S(2)}) %collective-permute-start.17) | collective-permute-done | bytes 800 | tf_op jit(solution)/shard_map/ppermute | solution.py:302
  87.5 0.0 copy-done.3
  87.5 0.0 copy-done.4
  87.5 1.6 %shard_map.137 = (bf16[1344,128]{1,0:T(8,128)(2,1)}, bf16[1,64,1344]{2,1,0:T(8,128)(2,1)}, f32[1,1344]{1,0:T(1,128)}) custom-call(s32[1,2]{1,0:T(1,128)S(1)} %copy-done.9, f32[1344,192]{1,0:T(8,128)S(1)} %get-tuple-element.16.projected, f32[1,192]{1,0:T(1,128)S(1)} %get-tuple-element.17.s0, f32[1,192]{1,0:T(1,128)S(1)} %collective-permute-done.15.s1, ...), custom_call_target="tpu_custom_call" | custom-call | tf_op jit(solution)/shard_map/pallas_call | solution.py:361
  (9 shorter events, 0.1 us)
Async XLA Ops:
  0.6 51.5 %copy-start = (bf16[256,1344]{0,1:T(8,128)(2,1)S(1)}, bf16[256,1344]{0,1:T(8,128)(2,1)}, u32[]{:S(2)}) copy-start(bf16[256,1344]{0,1:T(8,128)(2,1)} %param.19) | copy-start | bytes 2064388
  0.6 19.1 %collective-permute-start = (bf16[1344,256]{1,0:T(8,128)(2,1)}, bf16[1344,256]{1,0:T(8,128)(2,1)S(1)}, u32[]{:S(2)}, u32[]{:S(2)}) collective-permute-start(bf16[1344,256]{1,0:T(8,128)(2,1)} %bitcast.5), channel_id=1, source_target_pairs={{0,16},{4,12},{8,24},{12,4},{16,0},{20,28},{24,8},{28,20},{1,17},{... | collective-permute-start | bytes 2064392 | tf_op jit(solution)/shard_map/ppermute | solution.py:305
  3.7 48.4 %collective-permute-start.1 = (bf16[1344,256]{1,0:T(8,128)(2,1)}, bf16[1344,256]{1,0:T(8,128)(2,1)S(1)}, u32[]{:S(2)}, u32[]{:S(2)}) collective-permute-start(bf16[1344,256]{1,0:T(8,128)(2,1)} %bitcast.6), channel_id=1, source_target_pairs={{0,8},{4,20},{8,0},{12,28},{16,24},{20,4},{24,16},{28,12},{1,9},{5... | collective-permute-start | bytes 2064392 | tf_op jit(solution)/shard_map/ppermute | solution.py:319
  7.1 0.9 %copy-start.5 = (bf16[128,512]{1,0:T(8,128)(2,1)S(1)}, bf16[128,512]{1,0:T(8,128)(2,1)}, u32[]{:S(2)}) copy-start(bf16[128,512]{1,0:T(8,128)(2,1)} %q.1) | copy-start | bytes 393220
  8.0 0.8 copy-start.6
  8.8 0.8 copy-start.7
  9.6 0.8 copy-start.8
  10.4 10.8 %collective-permute-start.3 = (bf16[256,128]{1,0:T(8,128)(2,1)S(1)}, bf16[256,128]{1,0:T(8,128)(2,1)S(1)}, u32[]{:S(2)}, u32[]{:S(2)}) collective-permute-start(bf16[256,128]{1,0:T(8,128)(2,1)S(1)} %get-tuple-element.13), channel_id=1, source_target_pairs={{0,4},{4,0},{8,12},{12,8},{16,20},{20,16},{24,28},{28,24},{1,5},{5... | collective-permute-start | bytes 196616 | tf_op jit(solution)/shard_map/ppermute | solution.py:312
  19.7 32.4 %collective-permute-start.2 = (bf16[1344,256]{1,0:T(8,128)(2,1)S(1)}, bf16[1344,256]{1,0:T(8,128)(2,1)S(1)}, u32[]{:S(2)}, u32[]{:S(2)}) collective-permute-start(bf16[1344,256]{1,0:T(8,128)(2,1)S(1)} %collective-permute-done.w1), channel_id=1, source_target_pairs={{0,8},{4,20},{8,0},{12,28},{16,24},{20,4},{24,16},{28,12},{1,9},{5... | collective-permute-start | bytes 2064392 | tf_op jit(solution)/shard_map/ppermute | solution.py:320
  21.1 6.5 %collective-permute-start.4 = (bf16[512,128]{1,0:T(8,128)(2,1)S(1)}, bf16[512,128]{1,0:T(8,128)(2,1)S(1)}, u32[]{:S(2)}, u32[]{:S(2)}) collective-permute-start(bf16[512,128]{1,0:T(8,128)(2,1)S(1)} %constant_dynamic-update-slice_fusion.kv0), channel_id=1, source_target_pairs={{0,16},{4,12},{8,24},{12,4},{16,0},{20,28},{24,8},{28,20},{1,17},{... | collective-permute-start | bytes 393224 | tf_op jit(solution)/shard_map/ppermute | solution.py:314
  22.9 5.8 %collective-permute-start.10 = (bf16[256,256]{1,0:T(8,128)(2,1)S(1)}, bf16[256,256]{1,0:T(8,128)(2,1)S(1)}, u32[]{:S(2)}, u32[]{:S(2)}) collective-permute-start(bf16[256,256]{1,0:T(8,128)(2,1)S(1)} %get-tuple-element.15), channel_id=1, source_target_pairs={{0,4},{4,0},{8,12},{12,8},{16,20},{20,16},{24,28},{28,24},{1,5},{5... | collective-permute-start | bytes 393224 | tf_op jit(solution)/shard_map/ppermute | solution.py:316
  22.9 9.6 %collective-permute-start.5 = (bf16[512,128]{1,0:T(8,128)(2,1)S(1)}, bf16[512,128]{1,0:T(8,128)(2,1)S(1)}, u32[]{:S(2)}, u32[]{:S(2)}) collective-permute-start(bf16[512,128]{1,0:T(8,128)(2,1)S(1)} %constant_dynamic-update-slice_fusion.kv0), channel_id=1, source_target_pairs={{0,8},{4,20},{8,0},{12,28},{16,24},{20,4},{24,16},{28,12},{1,9},{5... | collective-permute-start | bytes 393224 | tf_op jit(solution)/shard_map/ppermute | solution.py:315
  27.7 6.3 %collective-permute-start.6 = (bf16[512,128]{1,0:T(8,128)(2,1)S(1)}, bf16[512,128]{1,0:T(8,128)(2,1)S(1)}, u32[]{:S(2)}, u32[]{:S(2)}) collective-permute-start(bf16[512,128]{1,0:T(8,128)(2,1)S(1)} %collective-permute-done.4.kv1), channel_id=1, source_target_pairs={{0,8},{4,20},{8,0},{12,28},{16,24},{20,4},{24,16},{28,12},{1,9},{5... | collective-permute-start | bytes 393224 | tf_op jit(solution)/shard_map/ppermute | solution.py:317
  35.0 5.7 %collective-permute-start.11 = (bf16[192,256]{1,0:T(8,128)(2,1)S(1)}, bf16[192,256]{1,0:T(8,128)(2,1)S(1)}, u32[]{:S(2)}, u32[]{:S(2)}) collective-permute-start(bf16[192,256]{1,0:T(8,128)(2,1)S(1)} %shard_map.133.a0), channel_id=1, source_target_pairs={{0,1},{1,3},{3,2},{2,0},{4,5},{5,7},{7,6},{6,4},{8,9},{9,11},{11,1... | collective-permute-start | bytes 294920 | tf_op jit(solution)/shard_map/ppermute | solution.py:334
  40.7 5.9 %collective-permute-start.12 = (bf16[192,256]{1,0:T(8,128)(2,1)S(1)}, bf16[192,256]{1,0:T(8,128)(2,1)S(1)}, u32[]{:S(2)}, u32[]{:S(2)}) collective-permute-start(bf16[192,256]{1,0:T(8,128)(2,1)S(1)} %collective-permute-done.11.a1), channel_id=1, source_target_pairs={{0,1},{1,3},{3,2},{2,0},{4,5},{5,7},{7,6},{6,4},{8,9},{9,11},{11,1... | collective-permute-start | bytes 294920 | tf_op jit(solution)/shard_map/ppermute | solution.py:334
  46.6 5.5 %collective-permute-start.13 = (bf16[192,256]{1,0:T(8,128)(2,1)S(1)}, bf16[192,256]{1,0:T(8,128)(2,1)S(1)}, u32[]{:S(2)}, u32[]{:S(2)}) collective-permute-start(bf16[192,256]{1,0:T(8,128)(2,1)S(1)} %collective-permute-done.12.a2), channel_id=1, source_target_pairs={{0,1},{1,3},{3,2},{2,0},{4,5},{5,7},{7,6},{6,4},{8,9},{9,11},{11,1... | collective-permute-start | bytes 294920 | tf_op jit(solution)/shard_map/ppermute | solution.py:334
  54.1 0.8 copy-start.1
  56.0 21.4 %collective-permute-start.14 = (bf16[1344,192]{0,1:T(8,128)(2,1)}, bf16[1344,192]{0,1:T(8,128)(2,1)}, u32[]{:S(2)}, u32[]{:S(2)}) collective-permute-start(bf16[1344,192]{0,1:T(8,128)(2,1)} %copy.18), channel_id=1, source_target_pairs={{0,4},{4,0},{8,12},{12,8},{16,20},{20,16},{24,28},{28,24},{1,5},{5... | collective-permute-start | bytes 1548296 | tf_op jit(solution)/shard_map/ppermute | solution.py:355
  57.1 6.2 %collective-permute-start.7 = (bf16[192,256]{1,0:T(8,128)(2,1)S(1)}, bf16[192,256]{1,0:T(8,128)(2,1)S(1)}, u32[]{:S(2)}, u32[]{:S(2)}) collective-permute-start(bf16[192,256]{1,0:T(8,128)(2,1)S(1)} %shard_map.131.a0), channel_id=1, source_target_pairs={{0,1},{1,3},{3,2},{2,0},{4,5},{5,7},{7,6},{6,4},{8,9},{9,11},{11,1... | collective-permute-start | bytes 294920 | tf_op jit(solution)/shard_map/ppermute | solution.py:334
  63.3 5.5 %collective-permute-start.8 = (bf16[192,256]{1,0:T(8,128)(2,1)S(1)}, bf16[192,256]{1,0:T(8,128)(2,1)S(1)}, u32[]{:S(2)}, u32[]{:S(2)}) collective-permute-start(bf16[192,256]{1,0:T(8,128)(2,1)S(1)} %collective-permute-done.7.a1), channel_id=1, source_target_pairs={{0,1},{1,3},{3,2},{2,0},{4,5},{5,7},{7,6},{6,4},{8,9},{9,11},{11,1... | collective-permute-start | bytes 294920 | tf_op jit(solution)/shard_map/ppermute | solution.py:334
  68.8 5.5 %collective-permute-start.9 = (bf16[192,256]{1,0:T(8,128)(2,1)S(1)}, bf16[192,256]{1,0:T(8,128)(2,1)S(1)}, u32[]{:S(2)}, u32[]{:S(2)}) collective-permute-start(bf16[192,256]{1,0:T(8,128)(2,1)S(1)} %collective-permute-done.8.a2), channel_id=1, source_target_pairs={{0,1},{1,3},{3,2},{2,0},{4,5},{5,7},{7,6},{6,4},{8,9},{9,11},{11,1... | collective-permute-start | bytes 294920 | tf_op jit(solution)/shard_map/ppermute | solution.py:334
  74.3 1.1 %copy-start.2 = (bf16[1344,256]{1,0:T(8,128)(2,1)S(1)}, bf16[1344,256]{1,0:T(8,128)(2,1)}, u32[]{:S(2)}) copy-start(bf16[1344,256]{1,0:T(8,128)(2,1)} %copy-done.1) | copy-start | bytes 2064388
  77.4 6.5 %copy-start.10 = (f32[1344]{0:T(1024)S(1)}, f32[1344]{0:T(1024)}, u32[]{:S(2)}) copy-start(f32[1344]{0:T(1024)} %param.20) | copy-start | bytes 16132
  78.7 8.8 %copy-start.3 = (bf16[128,1344]{0,1:T(8,128)(2,1)S(1)}, bf16[128,1344]{0,1:T(8,128)(2,1)}, u32[]{:S(2)}) copy-start(bf16[128,1344]{0,1:T(8,128)(2,1)} %param.14) | copy-start | bytes 1032196
  78.7 8.8 %copy-start.4 = (bf16[1,64,1344]{2,1,0:T(8,128)(2,1)S(1)}, bf16[1,64,1344]{2,1,0:T(8,128)(2,1)}, u32[]{:S(2)}) copy-start(bf16[1,64,1344]{2,1,0:T(8,128)(2,1)} %opt_resid.1) | copy-start | bytes 516100
  78.7 8.7 %copy-start.9 = (s32[1,2]{1,0:T(1,128)S(1)}, s32[1,2]{1,0:T(1,128)}, u32[]{:S(2)}) copy-start(s32[1,2]{1,0:T(1,128)} %bounds.1) | copy-start | bytes 28
  79.0 5.9 %collective-permute-start.15 = (f32[1,192]{1,0:T(1,128)S(1)}, f32[1,192]{1,0:T(1,128)S(1)}, u32[]{:S(2)}, u32[]{:S(2)}) collective-permute-start(f32[1,192]{1,0:T(1,128)S(1)} %get-tuple-element.17.s0), channel_id=1, source_target_pairs={{0,1},{1,2},{2,3},{3,0},{4,5},{5,6},{6,7},{7,4},{8,9},{9,10},{10,1... | collective-permute-start | bytes 2312 | tf_op jit(solution)/shard_map/ppermute | solution.py:302
  80.6 4.9 %collective-permute-start.16 = (f32[1,192]{1,0:T(1,128)S(1)}, f32[1,192]{1,0:T(1,128)S(1)}, u32[]{:S(2)}, u32[]{:S(2)}) collective-permute-start(f32[1,192]{1,0:T(1,128)S(1)} %get-tuple-element.17.s0), channel_id=1, source_target_pairs={{0,2},{1,3},{2,0},{3,1},{4,6},{5,7},{6,4},{7,5},{8,10},{9,11},{10,... | collective-permute-start | bytes 2312 | tf_op jit(solution)/shard_map/ppermute | solution.py:302
  83.9 3.6 %collective-permute-start.17 = (f32[1,192]{1,0:T(1,128)S(1)}, f32[1,192]{1,0:T(1,128)S(1)}, u32[]{:S(2)}, u32[]{:S(2)}) collective-permute-start(f32[1,192]{1,0:T(1,128)S(1)} %get-tuple-element.17.s0), channel_id=1, source_target_pairs={{0,3},{1,0},{2,1},{3,2},{4,7},{5,4},{6,5},{7,6},{8,11},{9,8},{10,9... | collective-permute-start | bytes 2312 | tf_op jit(solution)/shard_map/ppermute | solution.py:302

commit v2 on v1

--- a/solution.py
+++ b/solution.py
@@ -12,7 +12,6 @@
 score_scale = 168.0 ** (-0.5)
 exp2_scale = score_scale * 1.4426950408889634
 epsilon = 1e-06
-VMEM_BYTES = 40 * 1024 * 1024
 
 
 def passed_along(value, axis, steps):
@@ -128,6 +127,7 @@
 
 SMEM = pltpu.MemorySpace.SMEM
 VMEM = pltpu.MemorySpace.VMEM
+HBM = pltpu.MemorySpace.HBM
 
 
 def dot_nt(a, b):
@@ -138,18 +138,17 @@
     return lax.dot_general(a, b, (((1,), (0,)), ((), ())), preferred_element_type=jnp.float32)
 
 
-def call(kernel, out_shape, count, flops=0, moved=0, in_specs=None, scratch=()):
+def call(kernel, out_shape, count, flops=0, moved=0, in_specs=None, out_specs=None, scratch=(), vmem=8):
     many = isinstance(out_shape, (list, tuple))
     return pl.pallas_call(
         kernel,
         out_shape=out_shape,
         in_specs=in_specs or [pl.BlockSpec(memory_space=VMEM)] * count,
-        out_specs=[pl.BlockSpec(memory_space=VMEM)] * len(out_shape)
-        if many
-        else pl.BlockSpec(memory_space=VMEM),
+        out_specs=out_specs
+        or ([pl.BlockSpec(memory_space=VMEM)] * len(out_shape) if many else pl.BlockSpec(memory_space=VMEM)),
         scratch_shapes=list(scratch),
         cost_estimate=pl.CostEstimate(flops=flops, bytes_accessed=moved, transcendentals=0),
-        compiler_params=pltpu.CompilerParams(vmem_limit_bytes=VMEM_BYTES),
+        compiler_params=pltpu.CompilerParams(vmem_limit_bytes=vmem * 1024 * 1024),
     )
 
 
@@ -158,49 +157,78 @@
     return (0 * parity, 4 - 2 * parity, 2 + 2 * parity, 0 * parity + 6)
 
 
-def pack_kernel(q, kt, vt, oq, ok, ov, keep_kv, send_kv, keep_q, send_q):
+def pack_kernel(q, k, v, oq, ok, ov, sent, kept, sems):
     parity = lax.rem(lax.axis_index("seq"), 2)
     rows, opt = q.shape[0], oq.shape[1]
     wide = q.shape[1] // 2
-    for kv, qs, head in ((keep_kv, keep_q, parity), (send_kv, send_q, 1 - parity)):
-        at = pl.multiple_of(head * HD, HD)
-        at_q = pl.multiple_of(head * wide, wide)
-        kv[0:HD, :] = kt[pl.ds(at, HD), :]
-        kv[HD : 2 * HD, :] = vt[pl.ds(at, HD), :]
-        qs[0:rows, :] = q[:, pl.ds(at_q, wide)]
-        qs[rows : rows + opt, :] = oq[0, :, pl.ds(at_q, wide)]
-        qs[rows + opt : rows + 2 * opt, 0:HD] = ok[0, :, pl.ds(at, HD)]
-        qs[rows + opt : rows + 2 * opt, HD : 2 * HD] = ov[0, :, pl.ds(at, HD)]
-
-
-def attn_kernel(flip, rows, opt, kv0, kv1, kv2, kv3, qs, out):
+    own = pl.ds(2 * rows + opt, opt)
+    pieces = []
+    for to, head in ((sent, 1 - parity), (kept, parity)):
+        at = pl.ds(pl.multiple_of(head * HD, HD), HD)
+        at_q = pl.ds(pl.multiple_of(head * wide, wide), wide)
+        pieces += [
+            (k.at[:, at], to.at[0:rows, 0:HD]),
+            (v.at[:, at], to.at[0:rows, HD : 2 * HD]),
+            (q.at[:, at_q], to.at[rows : 2 * rows, :]),
+            (oq.at[0, :, at_q], to.at[2 * rows : 2 * rows + opt, :]),
+            (ok.at[0, :, at], to.at[own, 0:HD]),
+            (ov.at[0, :, at], to.at[own, HD : 2 * HD]),
+        ]
+    copies = [pltpu.make_async_copy(a, b, sems.at[i]) for i, (a, b) in enumerate(pieces)]
+    for copy in copies:
+        copy.start()
+    for copy in copies:
+        copy.wait()
+
+
+def join_kernel(kept, received, out):
+    rows = out.shape[0] // 2
+    out[0:rows, :] = kept[0:rows, :]
+    out[rows : 2 * rows, :] = received[0:rows, :]
+
+
+def stack_kernel(upper, lower, out):
+    rows = upper.shape[0]
+    out[0:rows, :] = upper[...]
+    out[rows : 2 * rows, :] = lower[...]
+
+
+def attn_kernel(flip, rows, opt, kv02, kv13, packed, out):
+    own = slice(2 * rows + opt, 2 * rows + 2 * opt)
+    attn(
+        (kv02, kv13),
+        flip,
+        packed[rows : 2 * rows, :],
+        packed[2 * rows : 2 * rows + opt, :],
+        packed[own, 0:HD],
+        packed[own, HD : 2 * HD],
+        out,
+    )
+
+
+def attn(slots, flip, q, oq, own_keys, own_values, out):
     s = lax.axis_index("seq")
-    slots = (kv0, kv1, kv2, kv3)
-    keys = jnp.concatenate(
-        [kv[b * 2 * HD : b * 2 * HD + HD, :] for kv in slots for b in (0, 1)], axis=1
-    )
-    values = jnp.concatenate(
-        [kv[b * 2 * HD + HD : (b + 1) * 2 * HD, :] for kv in slots for b in (0, 1)], axis=1
-    )
+    rows, opt = q.shape[0], oq.shape[0]
+    keys = jnp.concatenate([kv[:, 0:HD] for kv in slots], axis=0)
+    values = jnp.concatenate([kv[:, HD : 2 * HD] for kv in slots], axis=0)
+    _, m1, m2, m3 = masks(s)
     lane = lax.broadcasted_iota(jnp.int32, (1, rows), 1)
     key_pos = jnp.concatenate(
-        [((s ^ m) ^ b) * rows + lane for m in masks(s) for b in (0, 1)], axis=1
+        [((s ^ m) ^ b) * rows + lane for m in (0, m2, m1, m3) for b in (0, 1)], axis=1
     )
     query_pos = (s ^ flip) * rows + lax.broadcasted_iota(jnp.int32, (rows, 1), 0)
-    heads = qs.shape[1] // HD
+    heads = q.shape[1] // HD
     for h in range(heads):
-        scores = dot_nn(qs[0:rows, h * HD : (h + 1) * HD], keys)
+        scores = dot_nt(q[:, h * HD : (h + 1) * HD], keys)
         scores = jnp.where(key_pos <= query_pos, scores, -jnp.inf)
         top = jnp.max(scores, axis=1, keepdims=True)
         weights = jnp.exp2((scores - top) * exp2_scale)
         total = jnp.sum(weights, axis=1, keepdims=True)
-        mixed = dot_nt(weights.astype(jnp.bfloat16), values)
+        mixed = dot_nn(weights.astype(jnp.bfloat16), values)
         out[0:rows, h * HD : (h + 1) * HD] = (mixed / total).astype(jnp.bfloat16)
-    oq = jnp.concatenate([qs[rows : rows + opt, h * HD : (h + 1) * HD] for h in range(heads)], axis=0)
-    own_keys = qs[rows + opt : rows + 2 * opt, 0:HD]
-    own_values = qs[rows + opt : rows + 2 * opt, HD : 2 * HD]
+    oq = jnp.concatenate([oq[:, h * HD : (h + 1) * HD] for h in range(heads)], axis=0)
     step = lax.rem(lax.broadcasted_iota(jnp.int32, (heads * opt, 1), 0), opt)
-    scores = jnp.where(key_pos > step, dot_nn(oq, keys), -jnp.inf)
+    scores = jnp.where(key_pos > step, dot_nt(oq, keys), -jnp.inf)
     own = dot_nt(oq, own_keys)
     own = jnp.where(lax.broadcasted_iota(jnp.int32, (1, opt), 1) <= step, own, -jnp.inf)
     top = jnp.maximum(
@@ -209,7 +237,7 @@
     weights = jnp.exp2((scores - top) * exp2_scale)
     own = jnp.exp2((own - top) * exp2_scale)
     total = jnp.sum(weights, axis=1, keepdims=True) + jnp.sum(own, axis=1, keepdims=True)
-    mixed = dot_nt(weights.astype(jnp.bfloat16), values) + dot_nn(
+    mixed = dot_nn(weights.astype(jnp.bfloat16), values) + dot_nn(
         own.astype(jnp.bfloat16), own_values
     )
     mixed = (mixed / total).astype(jnp.bfloat16)
@@ -217,60 +245,81 @@
         out[rows : rows + opt, h * HD : (h + 1) * HD] = mixed[h * opt : (h + 1) * opt]
 
 
-def project_kernel(w0, w1, w2, w3, a0, a1, a2, a3, out, held, placed, sems):
-    copies = [
-        pltpu.make_async_copy(w, held.at[j], sems.at[j]) for j, w in enumerate((w0, w1, w2, w3))
-    ]
-    for copy in copies:
-        copy.start()
+def project_kernel(rows, opt, packed, w0, w1, w2, w3, a0, a1, a2, a3, out, placed):
     s = lax.axis_index("seq")
     z = lax.axis_index("head")
-    place = z ^ (z >> 1)
     for t, a in enumerate((a0, a1, a2, a3)):
-        source = lax.rem(place + (4 - t), 4)
-        placed[source ^ (source >> 1)] = a[...]
-    for copy in copies:
-        copy.wait()
+        placed[z ^ t] = a[...]
     blocks = [placed[(s ^ m) >> 1] for m in masks(s)]
-    features = out.shape[0]
-    part = features // 3
-    for n in range(3):
-        total = dot_nt(held[0, n * part : (n + 1) * part, :], blocks[0])
+    held = (w0, w1, w2, w3)
+    features = w0.shape[0]
+    half = features // 2
+    for n in range(2):
+        part = slice(n * half, (n + 1) * half)
+        total = dot_nt(held[0][part, :], blocks[0])
         for j in range(1, 4):
-            total += dot_nt(held[j, n * part : (n + 1) * part, :], blocks[j])
-        out[n * part : (n + 1) * part, :] = total.astype(out.dtype)
-
-
-def square_kernel(own, received, projected, squares):
-    total = own[...] + received[...].astype(jnp.float32)
-    projected[...] = total
-    squares[...] = jnp.sum(total * total, axis=0, keepdims=True)
-
-
-def spread_kernel(gain, out):
-    out[...] = jnp.broadcast_to(gain[...], (out.shape[1], out.shape[0])).T
+            total += dot_nt(held[j][part, :], blocks[j])
+        total = total.astype(out.dtype)
+        if packed:
+            out[part, :] = total[:, 0:rows]
+            out[features : features + half, n * opt : (n + 1) * opt] = total[:, rows : rows + opt]
+        else:
+            out[part, :] = total
+
+
+def square_kernel(rows, opt, own, received, projected, squares):
+    features = own.shape[0]
+    half = features // 2
+    left = own[:, 0:rows] + received[0:features, :].astype(jnp.float32)
+    projected[:, 0:rows] = left
+    squares[:, 0:rows] = jnp.sum(left * left, axis=0, keepdims=True)
+    total = 0.0
+    for n in range(2):
+        part = slice(n * half, (n + 1) * half)
+        right = received[features : features + half, n * opt : (n + 1) * opt]
+        right = own[part, rows : rows + opt] + right.astype(jnp.float32)
+        projected[part, rows : rows + opt] = right
+        total += jnp.sum(right * right, axis=0, keepdims=True)
+    squares[:, rows : rows + opt] = total
+
+
+def scale_kernel(rows, projected, gain, prefix, option):
+    features = prefix.shape[0]
+    row = gain[...]
+    prefix[...] = projected[:, 0:rows] * jnp.broadcast_to(row, (rows, features)).T
+    option[...] = projected[:, rows:].T * row
 
 
 def finish_kernel(
-    rows, width, bounds, projected, s0, s1, s2, s3, resid_t, opt_resid, gain, out_t, opt_out, summary
+    rows, width, bounds, prefix, option, s0, s1, s2, s3, resid_t, opt_resid,
+    out_t, opt_out, summary, held_t, held_opt, held_sum, sems,
 ):
     squares = s0[...] + s1[...] + s2[...] + s3[...]
     scale = lax.rsqrt(squares / width + epsilon)
-    spread = gain[...]
-    normed = projected[:, 0:rows] * scale[:, 0:rows] * spread
-    out_t[...] = (resid_t[...].astype(jnp.float32) + normed).astype(jnp.bfloat16)
+    held_t[...] = (resid_t[...].astype(jnp.float32) + prefix[...] * scale[:, 0:rows]).astype(
+        jnp.bfloat16
+    )
+    copies = [
+        pltpu.make_async_copy(a, b, sems.at[i])
+        for i, (a, b) in enumerate(((held_t, out_t), (held_opt, opt_out), (held_sum, summary)))
+    ]
+    copies[0].start()
     opt = opt_resid.shape[1]
-    normed = projected[:, rows : rows + opt] * scale[:, rows : rows + opt] * spread[:, 0:opt]
-    full = opt_resid[0].astype(jnp.float32) + normed.T
+    column = jnp.broadcast_to(scale[:, rows : rows + opt], (HD, opt)).T[:, 0:1]
+    full = opt_resid[0].astype(jnp.float32) + option[...] * column
     start, length = bounds[0, 0], bounds[0, 1]
     position = lax.broadcasted_iota(jnp.int32, (opt, 1), 0)
     kept = jnp.where(position < length, full, 0.0).astype(jnp.bfloat16)
-    opt_out[0] = kept
+    held_opt[0] = kept
+    copies[1].start()
     chosen = (position < length) & (position >= start)
     count = (length - start).astype(jnp.float32)
-    summary[...] = (
+    held_sum[...] = (
         jnp.sum(jnp.where(chosen, kept.astype(jnp.float32), 0.0), axis=0, keepdims=True) / count
     )
+    copies[2].start()
+    for copy in copies:
+        copy.wait()
 
 
 def paired_body(
@@ -295,100 +344,118 @@
     pair = [(s, s ^ 1) for s in seq]
     first = [(s, s ^ (2 if s % 2 else 4)) for s in seq]
     second = [(s, s ^ (4 if s % 2 else 2)) for s in seq]
-    ring = [(0, 1), (1, 3), (3, 2), (2, 0)]
 
     def turned(value, steps):
         count = lax.axis_size("head")
         return lax.ppermute(value, "head", [(i, (i + steps) % count) for i in range(count)])
 
+    def after(value, *others):
+        return lax.optimization_barrier((value, *others))[0]
+
+    def in_hbm(value):
+        return pltpu.with_memory_space_constraint(value, HBM)
+
+    def crossed(value, mask):
+        return lax.ppermute(value, "head", [(i, i ^ mask) for i in range(lax.axis_size("head"))])
+
     weight = out_weight.T
     weight_1 = lax.ppermute(weight, "seq", first)
 
-    keep_kv, send_kv, keep_q, send_q = call(
+    packed = pltpu.VMEM((2 * rows + 2 * opt, wide), bf16)
+    sent, kept = call(
         pack_kernel,
-        [shape((2 * HD, rows), bf16)] * 2 + [shape((rows + 2 * opt, wide), bf16)] * 2,
+        [packed, packed],
         6,
-    )(queries, keys.T, values.T, opt_queries, opt_keys, opt_values)
-    pair_kv = lax.ppermute(send_kv, "seq", pair)
-    kv_0 = jnp.concatenate([keep_kv, pair_kv], axis=0)
-    kv_1 = lax.ppermute(kv_0, "seq", first)
+        in_specs=[pl.BlockSpec(memory_space=HBM)] * 6,
+        scratch=[pltpu.SemaphoreType.DMA((12,))],
+    )(*map(in_hbm, (queries, keys, values, opt_queries, opt_keys, opt_values)))
+    received = lax.ppermute(sent, "seq", pair)
+    kv_0 = call(join_kernel, pltpu.VMEM((2 * rows, 2 * HD), bf16), 2)(kept, received)
     kv_2 = lax.ppermute(kv_0, "seq", second)
-    pair_q = lax.ppermute(send_q, "seq", pair)
-    kv_3 = lax.ppermute(kv_1, "seq", second)
-
-    weight_2 = lax.ppermute(weight, "seq", second)
-    weight_3 = lax.ppermute(weight_1, "seq", second)
-    weights = (weight, weight_1, weight_2, weight_3)
-
-    def attention(flip, q):
+    kv_02 = call(stack_kernel, pltpu.VMEM((4 * rows, 2 * HD), bf16), 2)(kv_0, kv_2)
+    kv_13 = lax.ppermute(kv_02, "seq", first)
+
+    attn_shape = pltpu.VMEM((rows + opt, wide), bf16)
+
+    def attention(flip, block):
         return call(
             functools.partial(attn_kernel, flip, rows, opt),
-            shape((rows + opt, wide), bf16),
-            5,
+            attn_shape,
+            3,
             flops=4 * (rows + opt) * wide * WINDOW,
-        )(kv_0, kv_1, kv_2, kv_3, q)
-
-    def gathered(block):
-        blocks = [block]
-        for _ in range(3):
-            blocks.append(lax.ppermute(blocks[-1], "head", ring))
-        return blocks
-
-    def project(blocks, dtype):
+            vmem=24,
+        )(kv_02, kv_13, block)
+
+    pair_0 = attention(1, received)
+    own_0 = attention(0, kept)
+    pair_1, pair_2 = crossed(pair_0, 1), crossed(pair_0, 2)
+    own_1, own_2 = crossed(own_0, 1), crossed(own_0, 2)
+    pair_3 = crossed(after(pair_2, own_0), 1)
+    own_3 = crossed(own_2, 1)
+
+    weight_2 = lax.ppermute(after(weight, kv_13), "seq", second)
+    weight_3 = lax.ppermute(after(weight_1, kv_13), "seq", second)
+    weights = (weight, weight_1, weight_2, weight_3)
+
+    def project(blocks, out_shape, packed):
         return call(
-            project_kernel,
-            shape((features, rows + opt), dtype),
+            functools.partial(project_kernel, rows, opt, packed),
+            out_shape,
             8,
             flops=8 * features * wide * (rows + opt),
             moved=8 * features * wide,
-            in_specs=[pl.BlockSpec(memory_space=pl.ANY)] * 4
-            + [pl.BlockSpec(memory_space=VMEM)] * 4,
-            scratch=[
-                pltpu.VMEM((4, features, wide), bf16),
-                pltpu.VMEM((4, rows + opt, wide), bf16),
-                pltpu.SemaphoreType.DMA((4,)),
-            ],
+            scratch=[pltpu.VMEM((4, rows + opt, wide), bf16)],
+            vmem=16,
         )(*weights, *blocks)
 
-    pair_blocks = gathered(attention(1, pair_q))
-    own_blocks = gathered(attention(0, keep_q))
-    received = lax.ppermute(project(pair_blocks, bf16), "seq", pair)
-    own = project(own_blocks, f32)
+    half = project((after(pair_0, own_1, own_3), pair_1, pair_2, pair_3), shape((features + features // 2, rows), bf16), True)
+    received = lax.ppermute(half, "seq", pair)
+    own = project((own_0, own_1, own_2, own_3), shape((features, rows + opt), f32), False)
     projected, squares = call(
-        square_kernel, [shape((features, rows + opt), f32), shape((1, rows + opt), f32)], 2
+        functools.partial(square_kernel, rows, opt),
+        [shape((features, rows + opt), f32), shape((1, rows + opt), f32)],
+        2,
     )(own, received)
-    spread = call(spread_kernel, shape((features, rows), f32), 1)(norm_gain[None])
+    prefix, option = call(
+        functools.partial(scale_kernel, rows),
+        [shape((features, rows), f32), shape((opt, features), f32)],
+        2,
+    )(projected, norm_gain[None])
+    results = [
+        shape((features, rows), bf16),
+        shape((1, opt, features), bf16),
+        shape((1, features), f32),
+    ]
     out_t, opt_out, summary = call(
         functools.partial(finish_kernel, rows, float(features * lax.axis_size("head"))),
-        [
-            shape((features, rows), bf16),
-            shape((1, opt, features), bf16),
-            shape((1, features), f32),
-        ],
+        results,
         9,
         in_specs=[pl.BlockSpec(memory_space=SMEM)] + [pl.BlockSpec(memory_space=VMEM)] * 8,
+        out_specs=[pl.BlockSpec(memory_space=HBM)] * 3,
+        scratch=[pltpu.VMEM(r.shape, r.dtype) for r in results] + [pltpu.SemaphoreType.DMA((3,))],
     )(
         option_bounds,
-        projected,
+        prefix,
+        option,
         squares,
         turned(squares, 1),
         turned(squares, 2),
         turned(squares, 3),
         prefix_resid.T,
         opt_resid,
-        spread,
     )
     return out_t.T, opt_out, summary
 
 
 def body(*args):
-    queries, keys, out_weight = args[0], args[1], args[8]
+    queries, keys, opt_queries, out_weight = args[0], args[1], args[4], args[8]
     seq, head = lax.axis_size("seq"), lax.axis_size("head")
     paired = (
         seq == 8
         and head == 4
         and seq * queries.shape[0] == WINDOW
         and queries.shape[0] == HD
+        and queries.shape[0] == 2 * opt_queries.shape[1]
         and keys.shape[1] == 2 * HD
         and out_weight.shape[0] * 2 == queries.shape[1]
         and out_weight.shape[0] * seq == queries.shape[1] * head

time: 89.5 us -> 52.1 us (0.58)
  waiting for transfers between devices: 46.1 us -> 22.8 us
  local copies, waits for them, and re-layouts: 9.55 us -> 0.03 us
  starting transfers between devices: 24.5 us -> 20.3 us
    ppermute x13 -> x11, waiting for transfers between devices: 29.6 us -> 15.9 us  [the longest x6 7.9 us: crossed(): lax.ppermute(value, 'head', [(i, i ^ mask) for i in range(lax.axis_size('...]
    ppermute x1, waiting for transfers between devices: 9.26 us -> 0.01 us  [paired_body(): weight_1 = lax.ppermute(weight, 'seq', first)]
    unnamed x25 -> x10, local copies, waits for them, and re-layouts: 7.13 us -> 0.03 us
    ppermute x13 -> x11, starting transfers between devices: 15.2 us -> 10.7 us  [the longest x6 7.83 us: crossed(): lax.ppermute(value, 'head', [(i, i ^ mask) for i in range(lax.axis_size('...]
    ppermute x3, waiting for transfers between devices: 3.31 us -> 1.95 us  [turned(): lax.ppermute(value, 'head', [(i, (i + steps) % count) for i in range(coun...]
    ppermute x1 -> x0, local copies, waits for them, and re-layouts: 1.3 us -> none  [paired_body(): received = lax.ppermute(project(pair_blocks, bf16), 'seq', pair)]
    pallas_call x1 -> x0, local copies, waits for them, and re-layouts: 1.1 us -> none  [project(): call(project_kernel, shape((features, rows + opt), dtype), 8, flops=8 * f...]
    ppermute x1, waiting for transfers between devices: 3.86 us -> 4.94 us  [paired_body(): kv_2 = lax.ppermute(kv_0, 'seq', second)]
  transfers between devices with their start and end apart: 18 -> 16, of which waited for: 13 -> 10; matrix products, arithmetic and copies ran while one was open for 2% -> 0% of each run, Pallas kernels for 5% -> 10%
where the time goes in v2:
time: 52.1 us; the launch traced here: 51.9 us
  waiting for transfers between devices  22.8 us (44%)
  starting transfers between devices  20.3 us (39%)
  Pallas kernels  8.01 us (15%)
  between operations  0.75 us (1%)
    ppermute x6, waiting for transfers between devices, crossed(): lax.ppermute(value, 'head', [(i, i ^ mask) for i in range(lax.axis_size('...  7.9 us
    ppermute x6, starting transfers between devices, crossed(): lax.ppermute(value, 'head', [(i, i ^ mask) for i in range(lax.axis_size('...  7.83 us
    ppermute x1, waiting for transfers between devices, paired_body(): kv_13 = lax.ppermute(kv_02, 'seq', first)  5.69 us
    ppermute x1, waiting for transfers between devices, paired_body(): kv_2 = lax.ppermute(kv_0, 'seq', second)  4.94 us
    ppermute x3, starting transfers between devices, turned(): lax.ppermute(value, 'head', [(i, (i + steps) % count) for i in range(coun...  4.93 us
    ppermute x1, starting transfers between devices, paired_body(): weight_1 = lax.ppermute(weight, 'seq', first)  3.03 us
    pallas_call x2, Pallas kernels, attention(): call(functools.partial(attn_kernel, flip, rows, opt), attn_shape, 3, flop...  2.54 us
    ppermute x3, waiting for transfers between devices, turned(): lax.ppermute(value, 'head', [(i, (i + steps) % count) for i in range(coun...  1.95 us
  transfers between devices with their start and end apart: 16, of which 10 were waited for; matrix products, arithmetic and copies ran while one was open for 0% of the time, Pallas kernels for 10%

profile of v2, /device:TPU:0, one launch (start us, length us, event | category | flops | bytes accessed | tf_op | source)
XLA Modules:
  0.0 51.9 jit_solution(11157163282975725687)
XLA Ops:
  0.6 0.0 copy-start
  0.6 3.0 %collective-permute-start = (bf16[1344,256]{1,0:T(8,128)(2,1)}, bf16[1344,256]{1,0:T(8,128)(2,1)S(1)}, u32[]{:S(2)}, u32[]{:S(2)}) collective-permute-start(bf16[1344,256]{1,0:T(8,128)(2,1)} %bitcast.3), channel_id=1, source_target_pairs={{0,16},{4,12},{8,24},{12,4},{16,0},{20,28},{24,8},{28,20},{1,17},{... | collective-permute-start | bytes 2064392 | tf_op jit(solution)/shard_map/ppermute | solution.py:362
  3.7 1.1 %shard_map.130 = (bf16[384,256]{1,0:T(8,128)(2,1)S(1)}, bf16[384,256]{1,0:T(8,128)(2,1)S(1)}) custom-call(bf16[128,512]{1,0:T(8,128)(2,1)} %q.1, bf16[128,256]{1,0:T(8,128)(2,1)} %k.1, bf16[128,256]{1,0:T(8,128)(2,1)} %v.1, bf16[1,64,512]{2,1,0:T(8,128)(2,1)} %oq.1, bf16[1,64,256]{2,1,0:T(8,128)(2,1)} %ok.1, bf16[1,64,256]{2,1,0:T(8,128)(2,1)} %ov.1), custom_call_target="tpu_custom_call" | custom-call | tf_op jit(solution)/shard_map/pallas_call | solution.py:365
  4.8 0.1 collective-permute-start.1
  4.9 1.4 %collective-permute-done.1.received.packed = bf16[384,256]{1,0:T(8,128)(2,1)S(1)} collective-permute-done((bf16[384,256]{1,0:T(8,128)(2,1)S(1)}, bf16[384,256]{1,0:T(8,128)(2,1)S(1)}, u32[]{:S(2)}, u32[]{:S(2)}) %collective-permute-start.1) | collective-permute-done | bytes 196640 | tf_op jit(solution)/shard_map/ppermute | solution.py:372
  6.3 1.6 %collective-permute-start.2 = (bf16[256,256]{1,0:T(8,128)(2,1)S(1)}, bf16[256,256]{1,0:T(8,128)(2,1)S(1)}, u32[]{:S(2)}, u32[]{:S(2)}) collective-permute-start(bf16[256,256]{1,0:T(8,128)(2,1)S(1)} %shard_map.131.upper), channel_id=1, source_target_pairs={{0,8},{4,20},{8,0},{12,28},{16,24},{20,4},{24,16},{28,12},{1,9},{5... | collective-permute-start | bytes 393224 | tf_op jit(solution)/shard_map/ppermute | solution.py:374
  7.9 4.9 %collective-permute-done.2.lower = bf16[256,256]{1,0:T(8,128)(2,1)S(1)} collective-permute-done((bf16[256,256]{1,0:T(8,128)(2,1)S(1)}, bf16[256,256]{1,0:T(8,128)(2,1)S(1)}, u32[]{:S(2)}, u32[]{:S(2)}) %collective-permute-start.2) | collective-permute-done | bytes 131104 | tf_op jit(solution)/shard_map/ppermute | solution.py:374
  12.8 0.7 %collective-permute-start.3 = (bf16[512,256]{1,0:T(8,128)(2,1)S(1)}, bf16[512,256]{1,0:T(8,128)(2,1)S(1)}, u32[]{:S(2)}, u32[]{:S(2)}) collective-permute-start(bf16[512,256]{1,0:T(8,128)(2,1)S(1)} %shard_map.132.kv02), channel_id=1, source_target_pairs={{0,16},{4,12},{8,24},{12,4},{16,0},{20,28},{24,8},{28,20},{1,17},{... | collective-permute-start | bytes 786440 | tf_op jit(solution)/shard_map/ppermute | solution.py:376
  13.6 5.7 %collective-permute-done.3.kv13 = bf16[512,256]{1,0:T(8,128)(2,1)S(1)} collective-permute-done((bf16[512,256]{1,0:T(8,128)(2,1)S(1)}, bf16[512,256]{1,0:T(8,128)(2,1)S(1)}, u32[]{:S(2)}, u32[]{:S(2)}) %collective-permute-start.3) | collective-permute-done | bytes 262176 | tf_op jit(solution)/shard_map/ppermute | solution.py:376
  19.3 0.0 copy-done
  19.3 1.5 %collective-permute-start.4 = (bf16[1344,256]{1,0:T(8,128)(2,1)S(1)}, bf16[1344,256]{1,0:T(8,128)(2,1)S(1)}, u32[]{:S(2)}, u32[]{:S(2)}) collective-permute-start(bf16[1344,256]{1,0:T(8,128)(2,1)S(1)} %bitcast.4), channel_id=1, source_target_pairs={{0,8},{4,20},{8,0},{12,28},{16,24},{20,4},{24,16},{28,12},{1,9},{5... | collective-permute-start | bytes 2064392 | tf_op jit(solution)/shard_map/ppermute | solution.py:396
  20.8 0.0 collective-permute-done.w1
  20.8 0.5 %collective-permute-start.5 = (bf16[1344,256]{1,0:T(8,128)(2,1)S(1)}, bf16[1344,256]{1,0:T(8,128)(2,1)S(1)}, u32[]{:S(2)}, u32[]{:S(2)}) collective-permute-start(bf16[1344,256]{1,0:T(8,128)(2,1)S(1)} %collective-permute-done.w1), channel_id=1, source_target_pairs={{0,8},{4,20},{8,0},{12,28},{16,24},{20,4},{24,16},{28,12},{1,9},{5... | collective-permute-start | bytes 2064392 | tf_op jit(solution)/shard_map/ppermute | solution.py:397
  21.3 1.3 %shard_map.133.a0 = bf16[192,256]{1,0:T(8,128)(2,1)S(1)} custom-call(bf16[512,256]{1,0:T(8,128)(2,1)S(1)} %shard_map.132.kv02, bf16[512,256]{1,0:T(8,128)(2,1)S(1)} %collective-permute-done.3.kv13, bf16[384,256]{1,0:T(8,128)(2,1)S(1)} %get-tuple-element.16.kept.packed), custom_call_target="tpu_custom_call" | custom-call | flops 201326592 | tf_op jit(solution)/shard_map/pallas_call | solution.py:381
  22.6 2.7 %collective-permute-start.7 = (bf16[192,256]{1,0:T(8,128)(2,1)S(1)}, bf16[192,256]{1,0:T(8,128)(2,1)S(1)}, u32[]{:S(2)}, u32[]{:S(2)}) collective-permute-start(bf16[192,256]{1,0:T(8,128)(2,1)S(1)} %shard_map.133.a0), channel_id=1, source_target_pairs={{0,2},{1,3},{2,0},{3,1},{4,6},{5,7},{6,4},{7,5},{8,10},{9,11},{10,... | collective-permute-start | bytes 294920 | tf_op jit(solution)/shard_map/ppermute | solution.py:359
  25.2 1.3 %shard_map.135.a0 = bf16[192,256]{1,0:T(8,128)(2,1)S(1)} custom-call(bf16[512,256]{1,0:T(8,128)(2,1)S(1)} %shard_map.132.kv02, bf16[512,256]{1,0:T(8,128)(2,1)S(1)} %collective-permute-done.3.kv13, bf16[384,256]{1,0:T(8,128)(2,1)S(1)} %collective-permute-done.1.received.packed), custom_call_target="tpu_custom_call" | custom-call | flops 201326592 | tf_op jit(solution)/shard_map/pallas_call | solution.py:381
  26.5 0.4 collective-permute-start.10
  26.9 1.6 %collective-permute-start.6 = (bf16[192,256]{1,0:T(8,128)(2,1)S(1)}, bf16[192,256]{1,0:T(8,128)(2,1)S(1)}, u32[]{:S(2)}, u32[]{:S(2)}) collective-permute-start(bf16[192,256]{1,0:T(8,128)(2,1)S(1)} %shard_map.133.a0), channel_id=1, source_target_pairs={{0,1},{1,0},{2,3},{3,2},{4,5},{5,4},{6,7},{7,6},{8,9},{9,8},{10,11... | collective-permute-start | bytes 294920 | tf_op jit(solution)/shard_map/ppermute | solution.py:359
  28.5 2.4 %collective-permute-done.7.a2 = bf16[192,256]{1,0:T(8,128)(2,1)S(1)} collective-permute-done((bf16[192,256]{1,0:T(8,128)(2,1)S(1)}, bf16[192,256]{1,0:T(8,128)(2,1)S(1)}, u32[]{:S(2)}, u32[]{:S(2)}) %collective-permute-start.7) | collective-permute-done | bytes 98336 | tf_op jit(solution)/shard_map/ppermute | solution.py:359
  30.9 1.2 %collective-permute-start.9 = (bf16[192,256]{1,0:T(8,128)(2,1)S(1)}, bf16[192,256]{1,0:T(8,128)(2,1)S(1)}, u32[]{:S(2)}, u32[]{:S(2)}) collective-permute-start(bf16[192,256]{1,0:T(8,128)(2,1)S(1)} %shard_map.135.a0), channel_id=1, source_target_pairs={{0,1},{1,0},{2,3},{3,2},{4,5},{5,4},{6,7},{7,6},{8,9},{9,8},{10,11... | collective-permute-start | bytes 294920 | tf_op jit(solution)/shard_map/ppermute | solution.py:359
  32.1 1.4 %collective-permute-done.10.a2 = bf16[192,256]{1,0:T(8,128)(2,1)S(1)} collective-permute-done((bf16[192,256]{1,0:T(8,128)(2,1)S(1)}, bf16[192,256]{1,0:T(8,128)(2,1)S(1)}, u32[]{:S(2)}, u32[]{:S(2)}) %collective-permute-start.10) | collective-permute-done | bytes 98336 | tf_op jit(solution)/shard_map/ppermute | solution.py:359
  33.5 0.5 %collective-permute-start.8 = (bf16[192,256]{1,0:T(8,128)(2,1)S(1)}, bf16[192,256]{1,0:T(8,128)(2,1)S(1)}, u32[]{:S(2)}, u32[]{:S(2)}) collective-permute-start(bf16[192,256]{1,0:T(8,128)(2,1)S(1)} %collective-permute-done.7.a2), channel_id=1, source_target_pairs={{0,1},{1,0},{2,3},{3,2},{4,5},{5,4},{6,7},{7,6},{8,9},{9,8},{10,11... | collective-permute-start | bytes 294920 | tf_op jit(solution)/shard_map/ppermute | solution.py:359
  34.0 0.0 collective-permute-done.6.a1
  34.0 1.5 %collective-permute-start.11 = (bf16[192,256]{1,0:T(8,128)(2,1)S(1)}, bf16[192,256]{1,0:T(8,128)(2,1)S(1)}, u32[]{:S(2)}, u32[]{:S(2)}) collective-permute-start(bf16[192,256]{1,0:T(8,128)(2,1)S(1)} %collective-permute-done.10.a2), channel_id=1, source_target_pairs={{0,1},{1,0},{2,3},{3,2},{4,5},{5,4},{6,7},{7,6},{8,9},{9,8},{10,11... | collective-permute-start | bytes 294920 | tf_op jit(solution)/shard_map/ppermute | solution.py:359
  35.5 3.0 %collective-permute-done.8.a3 = bf16[192,256]{1,0:T(8,128)(2,1)S(1)} collective-permute-done((bf16[192,256]{1,0:T(8,128)(2,1)S(1)}, bf16[192,256]{1,0:T(8,128)(2,1)S(1)}, u32[]{:S(2)}, u32[]{:S(2)}) %collective-permute-start.8) | collective-permute-done | bytes 98336 | tf_op jit(solution)/shard_map/ppermute | solution.py:359
  38.5 0.0 collective-permute-done.9.a1
  38.5 1.0 %collective-permute-done.11.a3 = bf16[192,256]{1,0:T(8,128)(2,1)S(1)} collective-permute-done((bf16[192,256]{1,0:T(8,128)(2,1)S(1)}, bf16[192,256]{1,0:T(8,128)(2,1)S(1)}, u32[]{:S(2)}, u32[]{:S(2)}) %collective-permute-start.11) | collective-permute-done | bytes 98336 | tf_op jit(solution)/shard_map/ppermute | solution.py:359
  39.6 0.0 collective-permute-done.4.w2
  39.6 0.0 collective-permute-done.5.w3
  39.6 1.0 %shard_map.136 = bf16[2016,128]{1,0:T(8,128)(2,1)S(1)} custom-call(bf16[1344,256]{1,0:T(8,128)(2,1)S(1)} %bitcast.5, bf16[1344,256]{1,0:T(8,128)(2,1)S(1)} %collective-permute-done.w1, bf16[1344,256]{1,0:T(8,128)(2,1)S(1)} %collective-permute-done.4.w2, bf16[1344,256]{1,0:T(8,128)(2,1)S(1)} %collective-permute-done.5.w3, ...), custom_call_target="tpu_custom_call" | custom-call | flops 528482304 | bytes 2752512 | tf_op jit(solution)/shard_map/pallas_call | solution.py:401
  40.6 0.1 collective-permute-start.12
  40.7 0.9 %shard_map.134.own = f32[1344,192]{1,0:T(8,128)S(1)} custom-call(bf16[1344,256]{1,0:T(8,128)(2,1)S(1)} %bitcast.6, bf16[1344,256]{1,0:T(8,128)(2,1)S(1)} %collective-permute-done.w1, bf16[1344,256]{1,0:T(8,128)(2,1)S(1)} %collective-permute-done.4.w2, bf16[1344,256]{1,0:T(8,128)(2,1)S(1)} %collective-permute-done.5.w3, bf16[192,256]{1,0:T(8,128)(2,1)S(1)} %shard_map.133.a0, ...), custom_call_target="tpu_custom_call" | custom-call | flops 528482304 | bytes 2752512 | tf_op jit(solution)/shard_map/pallas_call | solution.py:401
  41.6 0.0 copy-start.4
  41.6 0.0 copy-start.1
  41.6 0.0 copy-start.2
  41.6 0.0 copy-start.3
  41.6 0.9 %collective-permute-done.12.received = bf16[2016,128]{1,0:T(8,128)(2,1)S(1)} collective-permute-done((bf16[2016,128]{1,0:T(8,128)(2,1)S(1)}, bf16[2016,128]{1,0:T(8,128)(2,1)S(1)}, u32[]{:S(2)}, u32[]{:S(2)}) %collective-permute-start.12) | collective-permute-done | bytes 516128 | tf_op jit(solution)/shard_map/ppermute | solution.py:412
  42.6 0.3 shard_map.137
  42.9 0.6 %collective-permute-start.13 = (f32[1,192]{1,0:T(1,128)S(1)}, f32[1,192]{1,0:T(1,128)S(1)}, u32[]{:S(2)}, u32[]{:S(2)}) collective-permute-start(f32[1,192]{1,0:T(1,128)S(1)} %get-tuple-element.25.s0), channel_id=1, source_target_pairs={{0,1},{1,2},{2,3},{3,0},{4,5},{5,6},{6,7},{7,4},{8,9},{9,10},{10,1... | collective-permute-start | bytes 2312 | tf_op jit(solution)/shard_map/ppermute | solution.py:350
  43.5 3.2 %collective-permute-start.14 = (f32[1,192]{1,0:T(1,128)S(1)}, f32[1,192]{1,0:T(1,128)S(1)}, u32[]{:S(2)}, u32[]{:S(2)}) collective-permute-start(f32[1,192]{1,0:T(1,128)S(1)} %get-tuple-element.25.s0), channel_id=1, source_target_pairs={{0,2},{1,3},{2,0},{3,1},{4,6},{5,7},{6,4},{7,5},{8,10},{9,11},{10,... | collective-permute-start | bytes 2312 | tf_op jit(solution)/shard_map/ppermute | solution.py:350
  46.6 1.2 %collective-permute-start.15 = (f32[1,192]{1,0:T(1,128)S(1)}, f32[1,192]{1,0:T(1,128)S(1)}, u32[]{:S(2)}, u32[]{:S(2)}) collective-permute-start(f32[1,192]{1,0:T(1,128)S(1)} %get-tuple-element.25.s0), channel_id=1, source_target_pairs={{0,3},{1,0},{2,1},{3,2},{4,7},{5,4},{6,5},{7,6},{8,11},{9,8},{10,9... | collective-permute-start | bytes 2312 | tf_op jit(solution)/shard_map/ppermute | solution.py:350
  47.8 0.0 copy-done.4
  47.8 0.4 shard_map.138
  48.2 0.1 collective-permute-done.13.s1
  48.3 0.0 collective-permute-done.14.s2
  48.3 1.9 %collective-permute-done.15.s3 = f32[1,192]{1,0:T(1,128)S(1)} collective-permute-done((f32[1,192]{1,0:T(1,128)S(1)}, f32[1,192]{1,0:T(1,128)S(1)}, u32[]{:S(2)}, u32[]{:S(2)}) %collective-permute-start.15) | collective-permute-done | bytes 800 | tf_op jit(solution)/shard_map/ppermute | solution.py:350
  50.2 0.0 copy-done.1
  50.2 0.0 copy-done.2
  50.2 0.0 copy-done.3
  50.2 1.7 %shard_map.139 = (bf16[1344,128]{1,0:T(8,128)(2,1)}, bf16[1,64,1344]{2,1,0:T(8,128)(2,1)}, f32[1,1344]{1,0:T(1,128)}) custom-call(s32[1,2]{1,0:T(1,128)S(1)} %copy-done.3, f32[1344,128]{1,0:T(8,128)S(1)} %get-tuple-element.23.prefix, f32[64,1344]{1,0:T(8,128)S(1)} %get-tuple-element.24.option, f32[1,192]{1,0:T(1,128)S(1)} %get-tuple-element.25.s0, ...), custom_call_target="tpu_custom_call" | custom-call | tf_op jit(solution)/shard_map/pallas_call | solution.py:429
  (3 shorter events, 0.0 us)
Async XLA Ops:
  0.6 18.6 %copy-start = (bf16[256,1344]{0,1:T(8,128)(2,1)S(1)}, bf16[256,1344]{0,1:T(8,128)(2,1)}, u32[]{:S(2)}) copy-start(bf16[256,1344]{0,1:T(8,128)(2,1)} %param.19) | copy-start | bytes 2064388
  0.6 20.1 %collective-permute-start = (bf16[1344,256]{1,0:T(8,128)(2,1)}, bf16[1344,256]{1,0:T(8,128)(2,1)S(1)}, u32[]{:S(2)}, u32[]{:S(2)}) collective-permute-start(bf16[1344,256]{1,0:T(8,128)(2,1)} %bitcast.3), channel_id=1, source_target_pairs={{0,16},{4,12},{8,24},{12,4},{16,0},{20,28},{24,8},{28,20},{1,17},{... | collective-permute-start | bytes 2064392 | tf_op jit(solution)/shard_map/ppermute | solution.py:362
  4.8 1.5 %collective-permute-start.1 = (bf16[384,256]{1,0:T(8,128)(2,1)S(1)}, bf16[384,256]{1,0:T(8,128)(2,1)S(1)}, u32[]{:S(2)}, u32[]{:S(2)}) collective-permute-start(bf16[384,256]{1,0:T(8,128)(2,1)S(1)} %get-tuple-element.17), channel_id=1, source_target_pairs={{0,4},{4,0},{8,12},{12,8},{16,20},{20,16},{24,28},{28,24},{1,5},{5... | collective-permute-start | bytes 589832 | tf_op jit(solution)/shard_map/ppermute | solution.py:372
  6.3 6.5 %collective-permute-start.2 = (bf16[256,256]{1,0:T(8,128)(2,1)S(1)}, bf16[256,256]{1,0:T(8,128)(2,1)S(1)}, u32[]{:S(2)}, u32[]{:S(2)}) collective-permute-start(bf16[256,256]{1,0:T(8,128)(2,1)S(1)} %shard_map.131.upper), channel_id=1, source_target_pairs={{0,8},{4,20},{8,0},{12,28},{16,24},{20,4},{24,16},{28,12},{1,9},{5... | collective-permute-start | bytes 393224 | tf_op jit(solution)/shard_map/ppermute | solution.py:374
  12.8 6.4 %collective-permute-start.3 = (bf16[512,256]{1,0:T(8,128)(2,1)S(1)}, bf16[512,256]{1,0:T(8,128)(2,1)S(1)}, u32[]{:S(2)}, u32[]{:S(2)}) collective-permute-start(bf16[512,256]{1,0:T(8,128)(2,1)S(1)} %shard_map.132.kv02), channel_id=1, source_target_pairs={{0,16},{4,12},{8,24},{12,4},{16,0},{20,28},{24,8},{28,20},{1,17},{... | collective-permute-start | bytes 786440 | tf_op jit(solution)/shard_map/ppermute | solution.py:376
  19.3 20.3 %collective-permute-start.4 = (bf16[1344,256]{1,0:T(8,128)(2,1)S(1)}, bf16[1344,256]{1,0:T(8,128)(2,1)S(1)}, u32[]{:S(2)}, u32[]{:S(2)}) collective-permute-start(bf16[1344,256]{1,0:T(8,128)(2,1)S(1)} %bitcast.4), channel_id=1, source_target_pairs={{0,8},{4,20},{8,0},{12,28},{16,24},{20,4},{24,16},{28,12},{1,9},{5... | collective-permute-start | bytes 2064392 | tf_op jit(solution)/shard_map/ppermute | solution.py:396
  20.8 18.8 %collective-permute-start.5 = (bf16[1344,256]{1,0:T(8,128)(2,1)S(1)}, bf16[1344,256]{1,0:T(8,128)(2,1)S(1)}, u32[]{:S(2)}, u32[]{:S(2)}) collective-permute-start(bf16[1344,256]{1,0:T(8,128)(2,1)S(1)} %collective-permute-done.w1), channel_id=1, source_target_pairs={{0,8},{4,20},{8,0},{12,28},{16,24},{20,4},{24,16},{28,12},{1,9},{5... | collective-permute-start | bytes 2064392 | tf_op jit(solution)/shard_map/ppermute | solution.py:397
  22.6 8.3 %collective-permute-start.7 = (bf16[192,256]{1,0:T(8,128)(2,1)S(1)}, bf16[192,256]{1,0:T(8,128)(2,1)S(1)}, u32[]{:S(2)}, u32[]{:S(2)}) collective-permute-start(bf16[192,256]{1,0:T(8,128)(2,1)S(1)} %shard_map.133.a0), channel_id=1, source_target_pairs={{0,2},{1,3},{2,0},{3,1},{4,6},{5,7},{6,4},{7,5},{8,10},{9,11},{10,... | collective-permute-start | bytes 294920 | tf_op jit(solution)/shard_map/ppermute | solution.py:359
  26.5 7.0 %collective-permute-start.10 = (bf16[192,256]{1,0:T(8,128)(2,1)S(1)}, bf16[192,256]{1,0:T(8,128)(2,1)S(1)}, u32[]{:S(2)}, u32[]{:S(2)}) collective-permute-start(bf16[192,256]{1,0:T(8,128)(2,1)S(1)} %shard_map.135.a0), channel_id=1, source_target_pairs={{0,2},{1,3},{2,0},{3,1},{4,6},{5,7},{6,4},{7,5},{8,10},{9,11},{10,... | collective-permute-start | bytes 294920 | tf_op jit(solution)/shard_map/ppermute | solution.py:359
  26.9 7.1 %collective-permute-start.6 = (bf16[192,256]{1,0:T(8,128)(2,1)S(1)}, bf16[192,256]{1,0:T(8,128)(2,1)S(1)}, u32[]{:S(2)}, u32[]{:S(2)}) collective-permute-start(bf16[192,256]{1,0:T(8,128)(2,1)S(1)} %shard_map.133.a0), channel_id=1, source_target_pairs={{0,1},{1,0},{2,3},{3,2},{4,5},{5,4},{6,7},{7,6},{8,9},{9,8},{10,11... | collective-permute-start | bytes 294920 | tf_op jit(solution)/shard_map/ppermute | solution.py:359
  30.9 7.6 %collective-permute-start.9 = (bf16[192,256]{1,0:T(8,128)(2,1)S(1)}, bf16[192,256]{1,0:T(8,128)(2,1)S(1)}, u32[]{:S(2)}, u32[]{:S(2)}) collective-permute-start(bf16[192,256]{1,0:T(8,128)(2,1)S(1)} %shard_map.135.a0), channel_id=1, source_target_pairs={{0,1},{1,0},{2,3},{3,2},{4,5},{5,4},{6,7},{7,6},{8,9},{9,8},{10,11... | collective-permute-start | bytes 294920 | tf_op jit(solution)/shard_map/ppermute | solution.py:359
  33.5 5.1 %collective-permute-start.8 = (bf16[192,256]{1,0:T(8,128)(2,1)S(1)}, bf16[192,256]{1,0:T(8,128)(2,1)S(1)}, u32[]{:S(2)}, u32[]{:S(2)}) collective-permute-start(bf16[192,256]{1,0:T(8,128)(2,1)S(1)} %collective-permute-done.7.a2), channel_id=1, source_target_pairs={{0,1},{1,0},{2,3},{3,2},{4,5},{5,4},{6,7},{7,6},{8,9},{9,8},{10,11... | collective-permute-start | bytes 294920 | tf_op jit(solution)/shard_map/ppermute | solution.py:359
  34.0 5.6 %collective-permute-start.11 = (bf16[192,256]{1,0:T(8,128)(2,1)S(1)}, bf16[192,256]{1,0:T(8,128)(2,1)S(1)}, u32[]{:S(2)}, u32[]{:S(2)}) collective-permute-start(bf16[192,256]{1,0:T(8,128)(2,1)S(1)} %collective-permute-done.10.a2), channel_id=1, source_target_pairs={{0,1},{1,0},{2,3},{3,2},{4,5},{5,4},{6,7},{7,6},{8,9},{9,8},{10,11... | collective-permute-start | bytes 294920 | tf_op jit(solution)/shard_map/ppermute | solution.py:359
  40.6 2.0 %collective-permute-start.12 = (bf16[2016,128]{1,0:T(8,128)(2,1)S(1)}, bf16[2016,128]{1,0:T(8,128)(2,1)S(1)}, u32[]{:S(2)}, u32[]{:S(2)}) collective-permute-start(bf16[2016,128]{1,0:T(8,128)(2,1)S(1)} %shard_map.136), channel_id=1, source_target_pairs={{0,4},{4,0},{8,12},{12,8},{16,20},{20,16},{24,28},{28,24},{1,5},{5... | collective-permute-start | bytes 1548296 | tf_op jit(solution)/shard_map/ppermute | solution.py:412
  41.6 6.2 %copy-start.4 = (f32[1344]{0:T(1024)S(1)}, f32[1344]{0:T(1024)}, u32[]{:S(2)}) copy-start(f32[1344]{0:T(1024)} %param.20) | copy-start | bytes 16132
  41.6 8.6 %copy-start.1 = (bf16[128,1344]{0,1:T(8,128)(2,1)S(1)}, bf16[128,1344]{0,1:T(8,128)(2,1)}, u32[]{:S(2)}) copy-start(bf16[128,1344]{0,1:T(8,128)(2,1)} %param.14) | copy-start | bytes 1032196
  41.6 8.6 %copy-start.2 = (bf16[1,64,1344]{2,1,0:T(8,128)(2,1)S(1)}, bf16[1,64,1344]{2,1,0:T(8,128)(2,1)}, u32[]{:S(2)}) copy-start(bf16[1,64,1344]{2,1,0:T(8,128)(2,1)} %opt_resid.1) | copy-start | bytes 516100
  41.6 8.6 %copy-start.3 = (s32[1,2]{1,0:T(1,128)S(1)}, s32[1,2]{1,0:T(1,128)}, u32[]{:S(2)}) copy-start(s32[1,2]{1,0:T(1,128)} %bounds.1) | copy-start | bytes 28
  42.9 5.4 %collective-permute-start.13 = (f32[1,192]{1,0:T(1,128)S(1)}, f32[1,192]{1,0:T(1,128)S(1)}, u32[]{:S(2)}, u32[]{:S(2)}) collective-permute-start(f32[1,192]{1,0:T(1,128)S(1)} %get-tuple-element.25.s0), channel_id=1, source_target_pairs={{0,1},{1,2},{2,3},{3,0},{4,5},{5,6},{6,7},{7,4},{8,9},{9,10},{10,1... | collective-permute-start | bytes 2312 | tf_op jit(solution)/shard_map/ppermute | solution.py:350
  43.5 4.8 %collective-permute-start.14 = (f32[1,192]{1,0:T(1,128)S(1)}, f32[1,192]{1,0:T(1,128)S(1)}, u32[]{:S(2)}, u32[]{:S(2)}) collective-permute-start(f32[1,192]{1,0:T(1,128)S(1)} %get-tuple-element.25.s0), channel_id=1, source_target_pairs={{0,2},{1,3},{2,0},{3,1},{4,6},{5,7},{6,4},{7,5},{8,10},{9,11},{10,... | collective-permute-start | bytes 2312 | tf_op jit(solution)/shard_map/ppermute | solution.py:350
  46.6 3.6 %collective-permute-start.15 = (f32[1,192]{1,0:T(1,128)S(1)}, f32[1,192]{1,0:T(1,128)S(1)}, u32[]{:S(2)}, u32[]{:S(2)}) collective-permute-start(f32[1,192]{1,0:T(1,128)S(1)} %get-tuple-element.25.s0), channel_id=1, source_target_pairs={{0,3},{1,0},{2,1},{3,2},{4,7},{5,4},{6,5},{7,6},{8,11},{9,8},{10,9... | collective-permute-start | bytes 2312 | tf_op jit(solution)/shard_map/ppermute | solution.py:350

commit v3 on v2

--- a/solution.py
+++ b/solution.py
@@ -125,6 +125,9 @@
     return (prefix_out, option_out[None], option_summary[None])
 
 
+LONG_P, LONG_O, LONG_M = 200, 1, 14
+
+
 SMEM = pltpu.MemorySpace.SMEM
 VMEM = pltpu.MemorySpace.VMEM
 HBM = pltpu.MemorySpace.HBM
@@ -187,16 +190,10 @@
     out[rows : 2 * rows, :] = received[0:rows, :]
 
 
-def stack_kernel(upper, lower, out):
-    rows = upper.shape[0]
-    out[0:rows, :] = upper[...]
-    out[rows : 2 * rows, :] = lower[...]
-
-
-def attn_kernel(flip, rows, opt, kv02, kv13, packed, out):
+def attn_kernel(flip, rows, opt, kv0, kv1, kv2, kv3, packed, out):
     own = slice(2 * rows + opt, 2 * rows + 2 * opt)
     attn(
-        (kv02, kv13),
+        (kv0, kv1, kv2, kv3),
         flip,
         packed[rows : 2 * rows, :],
         packed[2 * rows : 2 * rows + opt, :],
@@ -211,10 +208,9 @@
     rows, opt = q.shape[0], oq.shape[0]
     keys = jnp.concatenate([kv[:, 0:HD] for kv in slots], axis=0)
     values = jnp.concatenate([kv[:, HD : 2 * HD] for kv in slots], axis=0)
-    _, m1, m2, m3 = masks(s)
     lane = lax.broadcasted_iota(jnp.int32, (1, rows), 1)
     key_pos = jnp.concatenate(
-        [((s ^ m) ^ b) * rows + lane for m in (0, m2, m1, m3) for b in (0, 1)], axis=1
+        [((s ^ m) ^ b) * rows + lane for m in masks(s) for b in (0, 1)], axis=1
     )
     query_pos = (s ^ flip) * rows + lax.broadcasted_iota(jnp.int32, (rows, 1), 0)
     heads = q.shape[1] // HD
@@ -245,22 +241,33 @@
         out[rows : rows + opt, h * HD : (h + 1) * HD] = mixed[h * opt : (h + 1) * opt]
 
 
-def project_kernel(rows, opt, packed, w0, w1, w2, w3, a0, a1, a2, a3, out, placed):
+def project_kernel(w0, w1, w2, a0, a1, a2, a3, out, placed):
+    z = lax.axis_index("head")
+    for t, block in enumerate((a0, a1, a2, a3)):
+        placed[z ^ t] = block[...]
     s = lax.axis_index("seq")
+    blocks = [placed[(s ^ m) >> 1] for m in masks(s)]
+    half = out.shape[0] // 2
+    for n in range(2):
+        part = slice(n * half, (n + 1) * half)
+        total = dot_nt(w0[part, :], blocks[0])
+        total += dot_nt(w1[part, :], blocks[1])
+        out[part, :] = total + dot_nt(w2[part, :], blocks[2])
+
+
+def complete_kernel(rows, opt, packed, w3, a0, a1, a2, a3, partial, out, placed):
     z = lax.axis_index("head")
-    for t, a in enumerate((a0, a1, a2, a3)):
-        placed[z ^ t] = a[...]
-    blocks = [placed[(s ^ m) >> 1] for m in masks(s)]
-    held = (w0, w1, w2, w3)
-    features = w0.shape[0]
+    for t, block in enumerate((a0, a1, a2, a3)):
+        placed[z ^ t] = block[...]
+    s = lax.axis_index("seq")
+    block = placed[(s ^ masks(s)[3]) >> 1]
+    features = w3.shape[0]
     half = features // 2
     for n in range(2):
         part = slice(n * half, (n + 1) * half)
-        total = dot_nt(held[0][part, :], blocks[0])
-        for j in range(1, 4):
-            total += dot_nt(held[j][part, :], blocks[j])
-        total = total.astype(out.dtype)
+        total = partial[part, :] + dot_nt(w3[part, :], block)
         if packed:
+            total = total.astype(out.dtype)
             out[part, :] = total[:, 0:rows]
             out[features : features + half, n * opt : (n + 1) * opt] = total[:, rows : rows + opt]
         else:
@@ -283,15 +290,21 @@
     squares[:, rows : rows + opt] = total
 
 
-def scale_kernel(rows, projected, gain, prefix, option):
+def scale_kernel(rows, bounds, projected, gain, prefix, option, kept, share):
     features = prefix.shape[0]
+    start, length = bounds[0, 0], bounds[0, 1]
+    position = lax.broadcasted_iota(jnp.int32, kept.shape, 0)
+    inside = position < length
+    count = jnp.zeros(kept.shape, jnp.float32) + (length - start).astype(jnp.float32)
+    kept[...] = jnp.where(inside, 1.0, 0.0)
+    share[...] = jnp.where(inside & (position >= start), count, 0.0)
     row = gain[...]
     prefix[...] = projected[:, 0:rows] * jnp.broadcast_to(row, (rows, features)).T
     option[...] = projected[:, rows:].T * row
 
 
 def finish_kernel(
-    rows, width, bounds, prefix, option, s0, s1, s2, s3, resid_t, opt_resid,
+    rows, width, prefix, option, kept, share, s0, s1, s2, s3, resid_t, opt_resid,
     out_t, opt_out, summary, held_t, held_opt, held_sum, sems,
 ):
     squares = s0[...] + s1[...] + s2[...] + s3[...]
@@ -307,16 +320,12 @@
     opt = opt_resid.shape[1]
     column = jnp.broadcast_to(scale[:, rows : rows + opt], (HD, opt)).T[:, 0:1]
     full = opt_resid[0].astype(jnp.float32) + option[...] * column
-    start, length = bounds[0, 0], bounds[0, 1]
-    position = lax.broadcasted_iota(jnp.int32, (opt, 1), 0)
-    kept = jnp.where(position < length, full, 0.0).astype(jnp.bfloat16)
-    held_opt[0] = kept
+    full = jnp.where(kept[:, 0:1] > 0.0, full, 0.0).astype(jnp.bfloat16)
+    held_opt[0] = full
     copies[1].start()
-    chosen = (position < length) & (position >= start)
-    count = (length - start).astype(jnp.float32)
-    held_sum[...] = (
-        jnp.sum(jnp.where(chosen, kept.astype(jnp.float32), 0.0), axis=0, keepdims=True) / count
-    )
+    counts = share[:, 0:1]
+    chosen = jnp.where(counts > 0.0, full.astype(jnp.float32), 0.0)
+    held_sum[...] = jnp.sum(chosen, axis=0, keepdims=True) / jnp.max(counts, axis=0, keepdims=True)
     copies[2].start()
     for copy in copies:
         copy.wait()
@@ -344,6 +353,7 @@
     pair = [(s, s ^ 1) for s in seq]
     first = [(s, s ^ (2 if s % 2 else 4)) for s in seq]
     second = [(s, s ^ (4 if s % 2 else 2)) for s in seq]
+    both = [(s, s ^ 6) for s in seq]
 
     def turned(value, steps):
         count = lax.axis_size("head")
@@ -359,7 +369,6 @@
         return lax.ppermute(value, "head", [(i, i ^ mask) for i in range(lax.axis_size("head"))])
 
     weight = out_weight.T
-    weight_1 = lax.ppermute(weight, "seq", first)
 
     packed = pltpu.VMEM((2 * rows + 2 * opt, wide), bf16)
     sent, kept = call(
@@ -371,56 +380,77 @@
     )(*map(in_hbm, (queries, keys, values, opt_queries, opt_keys, opt_values)))
     received = lax.ppermute(sent, "seq", pair)
     kv_0 = call(join_kernel, pltpu.VMEM((2 * rows, 2 * HD), bf16), 2)(kept, received)
-    kv_2 = lax.ppermute(kv_0, "seq", second)
-    kv_02 = call(stack_kernel, pltpu.VMEM((4 * rows, 2 * HD), bf16), 2)(kv_0, kv_2)
-    kv_13 = lax.ppermute(kv_02, "seq", first)
+    slots = (
+        kv_0,
+        lax.ppermute(kv_0, "seq", first),
+        lax.ppermute(kv_0, "seq", second),
+        lax.ppermute(kv_0, "seq", both),
+    )
 
     attn_shape = pltpu.VMEM((rows + opt, wide), bf16)
 
-    def attention(flip, block):
+    def attention(flip, block, weight):
         return call(
             functools.partial(attn_kernel, flip, rows, opt),
             attn_shape,
-            3,
-            flops=4 * (rows + opt) * wide * WINDOW,
+            5,
+            flops=weight * 4 * (rows + opt) * wide * WINDOW,
             vmem=24,
-        )(kv_02, kv_13, block)
-
-    pair_0 = attention(1, received)
-    own_0 = attention(0, kept)
+        )(*slots, block)
+
+    pair_0 = attention(1, received, LONG_P)
+    own_0 = attention(0, kept, LONG_O)
     pair_1, pair_2 = crossed(pair_0, 1), crossed(pair_0, 2)
     own_1, own_2 = crossed(own_0, 1), crossed(own_0, 2)
     pair_3 = crossed(after(pair_2, own_0), 1)
     own_3 = crossed(own_2, 1)
 
-    weight_2 = lax.ppermute(after(weight, kv_13), "seq", second)
-    weight_3 = lax.ppermute(after(weight_1, kv_13), "seq", second)
-    weights = (weight, weight_1, weight_2, weight_3)
-
-    def project(blocks, out_shape, packed):
+    weight_1 = lax.ppermute(after(weight, received), "seq", first)
+    weight_2 = lax.ppermute(after(weight, pair_0), "seq", second)
+    weight_3 = lax.ppermute(after(weight_1, own_0), "seq", second)
+    flops = 2 * features * wide * (rows + opt)
+    placed = [pltpu.VMEM((4, rows + opt, wide), bf16)]
+
+    def project(blocks):
         return call(
-            functools.partial(project_kernel, rows, opt, packed),
+            project_kernel,
+            shape((features, rows + opt), f32),
+            7,
+            flops=LONG_M * 3 * flops,
+            scratch=placed,
+            vmem=16,
+        )(weight, weight_1, weight_2, *blocks)
+
+    def complete(partial, blocks, out_shape, packed):
+        return call(
+            functools.partial(complete_kernel, rows, opt, packed),
             out_shape,
-            8,
-            flops=8 * features * wide * (rows + opt),
-            moved=8 * features * wide,
-            scratch=[pltpu.VMEM((4, rows + opt, wide), bf16)],
+            6,
+            flops=flops,
+            scratch=placed,
             vmem=16,
-        )(*weights, *blocks)
-
-    half = project((after(pair_0, own_1, own_3), pair_1, pair_2, pair_3), shape((features + features // 2, rows), bf16), True)
+        )(weight_3, *blocks, partial)
+
+    pair_blocks = (after(pair_0, own_1, own_3), pair_1, pair_2, pair_3)
+    own_blocks = (own_0, own_1, own_2, own_3)
+    pair_part, own_part = project(pair_blocks), project(own_blocks)
+    half = complete(
+        pair_part, pair_blocks, shape((features + features // 2, rows), bf16), True
+    )
     received = lax.ppermute(half, "seq", pair)
-    own = project((own_0, own_1, own_2, own_3), shape((features, rows + opt), f32), False)
+    own = complete(own_part, own_blocks, shape((features, rows + opt), f32), False)
     projected, squares = call(
         functools.partial(square_kernel, rows, opt),
         [shape((features, rows + opt), f32), shape((1, rows + opt), f32)],
         2,
     )(own, received)
-    prefix, option = call(
+    scaled = call(
         functools.partial(scale_kernel, rows),
-        [shape((features, rows), f32), shape((opt, features), f32)],
-        2,
-    )(projected, norm_gain[None])
+        [shape((features, rows), f32), shape((opt, features), f32)]
+        + [shape((opt, HD), f32)] * 2,
+        3,
+        in_specs=[pl.BlockSpec(memory_space=SMEM)] + [pl.BlockSpec(memory_space=VMEM)] * 2,
+    )(option_bounds, projected, norm_gain[None])
     results = [
         shape((features, rows), bf16),
         shape((1, opt, features), bf16),
@@ -429,14 +459,11 @@
     out_t, opt_out, summary = call(
         functools.partial(finish_kernel, rows, float(features * lax.axis_size("head"))),
         results,
-        9,
-        in_specs=[pl.BlockSpec(memory_space=SMEM)] + [pl.BlockSpec(memory_space=VMEM)] * 8,
+        10,
         out_specs=[pl.BlockSpec(memory_space=HBM)] * 3,
         scratch=[pltpu.VMEM(r.shape, r.dtype) for r in results] + [pltpu.SemaphoreType.DMA((3,))],
     )(
-        option_bounds,
-        prefix,
-        option,
+        *scaled,
         squares,
         turned(squares, 1),
         turned(squares, 2),

time: 52.1 us -> 48.6 us (0.933)
  waiting for transfers between devices: 22.8 us -> 15.2 us
  starting transfers between devices: 20.3 us -> 24 us
    ppermute x6, waiting for transfers between devices: 7.9 us -> 4.24 us  [crossed(): lax.ppermute(value, 'head', [(i, i ^ mask) for i in range(lax.axis_size('...]
    ppermute x5 -> x6, waiting for transfers between devices: 10.6 us -> 7.95 us  [the longest x1 2.57 us: paired_body(): lax.ppermute(kv_0, 'seq', both)]
    ppermute x5 -> x6, starting transfers between devices: 7.36 us -> 9.5 us  [the longest x1 2.95 us: paired_body(): lax.ppermute(kv_0, 'seq', first)]
    ppermute x3, waiting for transfers between devices: 1.95 us -> 1.23 us  [turned(): lax.ppermute(value, 'head', [(i, (i + steps) % count) for i in range(coun...]
    ppermute x3, starting transfers between devices: 4.93 us -> 5.62 us  [turned(): lax.ppermute(value, 'head', [(i, (i + steps) % count) for i in range(coun...]
    pallas_call x1, Pallas kernels: 0.42 us -> 0.96 us  [paired_body(): call(functools.partial(scale_kernel, rows), [shape((features, rows), f32)...]
    pallas_call x5 -> x6, Pallas kernels: 4.49 us -> 4.87 us  [the longest x2 2.55 us: attention(): call(functools.partial(attn_kernel, flip, rows, opt), attn_shape, 5, flop...]
  transfers between devices with their start and end apart: 16 -> 17, of which waited for: 10 -> 10; matrix products, arithmetic and copies ran while one was open for 0% -> 0% of each run, Pallas kernels for 10% -> 11%
where the time goes in v3:
time: 48.6 us; the launch traced here: 48.4 us
  starting transfers between devices  24 us (49%)
  waiting for transfers between devices  15.2 us (31%)
  Pallas kernels  8.44 us (17%)
  between operations  0.76 us (2%)
    ppermute x6, starting transfers between devices, crossed(): lax.ppermute(value, 'head', [(i, i ^ mask) for i in range(lax.axis_size('...  8.29 us
    ppermute x3, starting transfers between devices, turned(): lax.ppermute(value, 'head', [(i, (i + steps) % count) for i in range(coun...  5.62 us
    ppermute x6, waiting for transfers between devices, crossed(): lax.ppermute(value, 'head', [(i, i ^ mask) for i in range(lax.axis_size('...  4.24 us
    ppermute x1, starting transfers between devices, paired_body(): lax.ppermute(kv_0, 'seq', first)  2.95 us
    ppermute x1, waiting for transfers between devices, paired_body(): lax.ppermute(kv_0, 'seq', both)  2.57 us
    pallas_call x2, Pallas kernels, attention(): call(functools.partial(attn_kernel, flip, rows, opt), attn_shape, 5, flop...  2.55 us
    ppermute x1, waiting for transfers between devices, paired_body(): lax.ppermute(kv_0, 'seq', second)  2.22 us
    ppermute x1, starting transfers between devices, paired_body(): weight_1 = lax.ppermute(after(weight, received), 'seq', first)  1.95 us
  transfers between devices with their start and end apart: 17, of which 10 were waited for; matrix products, arithmetic and copies ran while one was open for 0% of the time, Pallas kernels for 11%

profile of v3, /device:TPU:0, one launch (start us, length us, event | category | flops | bytes accessed | tf_op | source)
XLA Modules:
  0.0 48.4 jit_solution(3635511896264184644)
XLA Ops:
  0.6 1.1 %shard_map.130 = (bf16[384,256]{1,0:T(8,128)(2,1)S(1)}, bf16[384,256]{1,0:T(8,128)(2,1)S(1)}) custom-call(bf16[128,512]{1,0:T(8,128)(2,1)} %q.1, bf16[128,256]{1,0:T(8,128)(2,1)} %k.1, bf16[128,256]{1,0:T(8,128)(2,1)} %v.1, bf16[1,64,512]{2,1,0:T(8,128)(2,1)} %oq.1, bf16[1,64,256]{2,1,0:T(8,128)(2,1)} %ok.1, bf16[1,64,256]{2,1,0:T(8,128)(2,1)} %ov.1), custom_call_target="tpu_custom_call" | custom-call | tf_op jit(solution)/shard_map/pallas_call | solution.py:374
  1.8 0.5 %collective-permute-start = (bf16[384,256]{1,0:T(8,128)(2,1)S(1)}, bf16[384,256]{1,0:T(8,128)(2,1)S(1)}, u32[]{:S(2)}, u32[]{:S(2)}) collective-permute-start(bf16[384,256]{1,0:T(8,128)(2,1)S(1)} %get-tuple-element.19), channel_id=1, source_target_pairs={{0,4},{4,0},{8,12},{12,8},{16,20},{20,16},{24,28},{28,24},{1,5},{5... | collective-permute-start | bytes 589832 | tf_op jit(solution)/shard_map/ppermute | solution.py:381
  2.3 1.1 %collective-permute-done.received.packed = bf16[384,256]{1,0:T(8,128)(2,1)S(1)} collective-permute-done((bf16[384,256]{1,0:T(8,128)(2,1)S(1)}, bf16[384,256]{1,0:T(8,128)(2,1)S(1)}, u32[]{:S(2)}, u32[]{:S(2)}) %collective-permute-start) | collective-permute-done | bytes 196640 | tf_op jit(solution)/shard_map/ppermute | solution.py:381
  3.4 3.0 %collective-permute-start.2 = (bf16[256,256]{1,0:T(8,128)(2,1)S(1)}, bf16[256,256]{1,0:T(8,128)(2,1)S(1)}, u32[]{:S(2)}, u32[]{:S(2)}) collective-permute-start(bf16[256,256]{1,0:T(8,128)(2,1)S(1)} %shard_map.131.kv0), channel_id=1, source_target_pairs={{0,16},{4,12},{8,24},{12,4},{16,0},{20,28},{24,8},{28,20},{1,17},{... | collective-permute-start | bytes 393224 | tf_op jit(solution)/shard_map/ppermute | solution.py:385
  6.3 1.5 %collective-permute-start.3 = (bf16[256,256]{1,0:T(8,128)(2,1)S(1)}, bf16[256,256]{1,0:T(8,128)(2,1)S(1)}, u32[]{:S(2)}, u32[]{:S(2)}) collective-permute-start(bf16[256,256]{1,0:T(8,128)(2,1)S(1)} %shard_map.131.kv0), channel_id=1, source_target_pairs={{0,8},{4,20},{8,0},{12,28},{16,24},{20,4},{24,16},{28,12},{1,9},{5... | collective-permute-start | bytes 393224 | tf_op jit(solution)/shard_map/ppermute | solution.py:386
  7.8 0.0 collective-permute-start.4
  7.9 0.0 copy-start.3
  7.9 1.9 %collective-permute-start.1 = (bf16[1344,256]{1,0:T(8,128)(2,1)}, bf16[1344,256]{1,0:T(8,128)(2,1)S(1)}, u32[]{:S(2)}, u32[]{:S(2)}) collective-permute-start(bf16[1344,256]{1,0:T(8,128)(2,1)} %bitcast.4), channel_id=1, source_target_pairs={{0,16},{4,12},{8,24},{12,4},{16,0},{20,28},{24,8},{28,20},{1,17},{... | collective-permute-start | bytes 2064392 | tf_op jit(solution)/shard_map/ppermute | solution.py:408
  9.8 0.6 %collective-permute-done.2.kv1 = bf16[256,256]{1,0:T(8,128)(2,1)S(1)} collective-permute-done((bf16[256,256]{1,0:T(8,128)(2,1)S(1)}, bf16[256,256]{1,0:T(8,128)(2,1)S(1)}, u32[]{:S(2)}, u32[]{:S(2)}) %collective-permute-start.2) | collective-permute-done | bytes 131104 | tf_op jit(solution)/shard_map/ppermute | solution.py:385
  10.4 2.2 %collective-permute-done.3.kv2 = bf16[256,256]{1,0:T(8,128)(2,1)S(1)} collective-permute-done((bf16[256,256]{1,0:T(8,128)(2,1)S(1)}, bf16[256,256]{1,0:T(8,128)(2,1)S(1)}, u32[]{:S(2)}, u32[]{:S(2)}) %collective-permute-start.3) | collective-permute-done | bytes 131104 | tf_op jit(solution)/shard_map/ppermute | solution.py:386
  12.6 2.6 %collective-permute-done.4.kv3 = bf16[256,256]{1,0:T(8,128)(2,1)S(1)} collective-permute-done((bf16[256,256]{1,0:T(8,128)(2,1)S(1)}, bf16[256,256]{1,0:T(8,128)(2,1)S(1)}, u32[]{:S(2)}, u32[]{:S(2)}) %collective-permute-start.4) | collective-permute-done | bytes 131104 | tf_op jit(solution)/shard_map/ppermute | solution.py:387
  15.2 1.3 %shard_map.133.a0 = bf16[192,256]{1,0:T(8,128)(2,1)S(1)} custom-call(bf16[256,256]{1,0:T(8,128)(2,1)S(1)} %shard_map.131.kv0, bf16[256,256]{1,0:T(8,128)(2,1)S(1)} %collective-permute-done.2.kv1, bf16[256,256]{1,0:T(8,128)(2,1)S(1)} %collective-permute-done.3.kv2, bf16[256,256]{1,0:T(8,128)(2,1)S(1)} %collective-permute-done.4.kv3, ...), custom_call_target="tpu_custom_call" | custom-call | flops 40265318400 | tf_op jit(solution)/shard_map/pallas_call | solution.py:393
  16.5 0.0 copy-done.3
  16.5 1.8 %collective-permute-start.9 = (bf16[1344,256]{1,0:T(8,128)(2,1)S(1)}, bf16[1344,256]{1,0:T(8,128)(2,1)S(1)}, u32[]{:S(2)}, u32[]{:S(2)}) collective-permute-start(bf16[1344,256]{1,0:T(8,128)(2,1)S(1)} %bitcast.5), channel_id=1, source_target_pairs={{0,8},{4,20},{8,0},{12,28},{16,24},{20,4},{24,16},{28,12},{1,9},{5... | collective-permute-start | bytes 2064392 | tf_op jit(solution)/shard_map/ppermute | solution.py:409
  18.3 1.3 %shard_map.132.a0 = bf16[192,256]{1,0:T(8,128)(2,1)S(1)} custom-call(bf16[256,256]{1,0:T(8,128)(2,1)S(1)} %shard_map.131.kv0, bf16[256,256]{1,0:T(8,128)(2,1)S(1)} %collective-permute-done.2.kv1, bf16[256,256]{1,0:T(8,128)(2,1)S(1)} %collective-permute-done.3.kv2, bf16[256,256]{1,0:T(8,128)(2,1)S(1)} %collective-permute-done.4.kv3, ...), custom_call_target="tpu_custom_call" | custom-call | flops 201326592 | tf_op jit(solution)/shard_map/pallas_call | solution.py:393
  19.6 2.6 %collective-permute-start.7 = (bf16[192,256]{1,0:T(8,128)(2,1)S(1)}, bf16[192,256]{1,0:T(8,128)(2,1)S(1)}, u32[]{:S(2)}, u32[]{:S(2)}) collective-permute-start(bf16[192,256]{1,0:T(8,128)(2,1)S(1)} %shard_map.132.a0), channel_id=1, source_target_pairs={{0,2},{1,3},{2,0},{3,1},{4,6},{5,7},{6,4},{7,5},{8,10},{9,11},{10,... | collective-permute-start | bytes 294920 | tf_op jit(solution)/shard_map/ppermute | solution.py:369
  22.2 0.3 collective-permute-start.11
  22.6 1.6 %collective-permute-start.6 = (bf16[192,256]{1,0:T(8,128)(2,1)S(1)}, bf16[192,256]{1,0:T(8,128)(2,1)S(1)}, u32[]{:S(2)}, u32[]{:S(2)}) collective-permute-start(bf16[192,256]{1,0:T(8,128)(2,1)S(1)} %shard_map.132.a0), channel_id=1, source_target_pairs={{0,1},{1,0},{2,3},{3,2},{4,5},{5,4},{6,7},{7,6},{8,9},{9,8},{10,11... | collective-permute-start | bytes 294920 | tf_op jit(solution)/shard_map/ppermute | solution.py:369
  24.2 1.6 %collective-permute-done.1.w1 = bf16[1344,256]{1,0:T(8,128)(2,1)S(1)} collective-permute-done((bf16[1344,256]{1,0:T(8,128)(2,1)}, bf16[1344,256]{1,0:T(8,128)(2,1)S(1)}, u32[]{:S(2)}, u32[]{:S(2)}) %collective-permute-start.1) | collective-permute-done | bytes 688160 | tf_op jit(solution)/shard_map/ppermute | solution.py:408
  25.7 1.2 %collective-permute-start.5 = (bf16[1344,256]{1,0:T(8,128)(2,1)S(1)}, bf16[1344,256]{1,0:T(8,128)(2,1)S(1)}, u32[]{:S(2)}, u32[]{:S(2)}) collective-permute-start(bf16[1344,256]{1,0:T(8,128)(2,1)S(1)} %collective-permute-done.1.w1), channel_id=1, source_target_pairs={{0,8},{4,20},{8,0},{12,28},{16,24},{20,4},{24,16},{28,12},{1,9},{5... | collective-permute-start | bytes 2064392 | tf_op jit(solution)/shard_map/ppermute | solution.py:410
  27.0 0.0 collective-permute-done.7.a2
  27.0 1.6 %collective-permute-start.10 = (bf16[192,256]{1,0:T(8,128)(2,1)S(1)}, bf16[192,256]{1,0:T(8,128)(2,1)S(1)}, u32[]{:S(2)}, u32[]{:S(2)}) collective-permute-start(bf16[192,256]{1,0:T(8,128)(2,1)S(1)} %shard_map.133.a0), channel_id=1, source_target_pairs={{0,1},{1,0},{2,3},{3,2},{4,5},{5,4},{6,7},{7,6},{8,9},{9,8},{10,11... | collective-permute-start | bytes 294920 | tf_op jit(solution)/shard_map/ppermute | solution.py:369
  28.6 0.0 collective-permute-done.11.a2
  28.6 1.7 %collective-permute-start.8 = (bf16[192,256]{1,0:T(8,128)(2,1)S(1)}, bf16[192,256]{1,0:T(8,128)(2,1)S(1)}, u32[]{:S(2)}, u32[]{:S(2)}) collective-permute-start(bf16[192,256]{1,0:T(8,128)(2,1)S(1)} %collective-permute-done.7.a2), channel_id=1, source_target_pairs={{0,1},{1,0},{2,3},{3,2},{4,5},{5,4},{6,7},{7,6},{8,9},{9,8},{10,11... | collective-permute-start | bytes 294920 | tf_op jit(solution)/shard_map/ppermute | solution.py:369
  30.3 0.0 collective-permute-done.6.a1
  30.3 0.4 collective-permute-start.12
  30.7 2.5 %collective-permute-done.8.a3 = bf16[192,256]{1,0:T(8,128)(2,1)S(1)} collective-permute-done((bf16[192,256]{1,0:T(8,128)(2,1)S(1)}, bf16[192,256]{1,0:T(8,128)(2,1)S(1)}, u32[]{:S(2)}, u32[]{:S(2)}) %collective-permute-start.8) | collective-permute-done | bytes 98336 | tf_op jit(solution)/shard_map/ppermute | solution.py:369
  33.2 0.0 collective-permute-done.10.a1
  33.2 1.7 %collective-permute-done.12.a3 = bf16[192,256]{1,0:T(8,128)(2,1)S(1)} collective-permute-done((bf16[192,256]{1,0:T(8,128)(2,1)S(1)}, bf16[192,256]{1,0:T(8,128)(2,1)S(1)}, u32[]{:S(2)}, u32[]{:S(2)}) %collective-permute-start.12) | collective-permute-done | bytes 98336 | tf_op jit(solution)/shard_map/ppermute | solution.py:369
  34.9 0.0 collective-permute-done.9.w2
  34.9 0.7 %shard_map.136.partial = f32[1344,192]{1,0:T(8,128)S(1)} custom-call(bf16[1344,256]{1,0:T(8,128)(2,1)S(1)} %bitcast.6, bf16[1344,256]{1,0:T(8,128)(2,1)S(1)} %collective-permute-done.1.w1, bf16[1344,256]{1,0:T(8,128)(2,1)S(1)} %collective-permute-done.9.w2, bf16[192,256]{1,0:T(8,128)(2,1)S(1)} %shard_map.133.a0, ...), custom_call_target="tpu_custom_call" | custom-call | flops 5549064192 | tf_op jit(solution)/shard_map/pallas_call | solution.py:415
  35.7 1.0 %collective-permute-done.5.w3 = bf16[1344,256]{1,0:T(8,128)(2,1)S(1)} collective-permute-done((bf16[1344,256]{1,0:T(8,128)(2,1)S(1)}, bf16[1344,256]{1,0:T(8,128)(2,1)S(1)}, u32[]{:S(2)}, u32[]{:S(2)}) %collective-permute-start.5) | collective-permute-done | bytes 688160 | tf_op jit(solution)/shard_map/ppermute | solution.py:410
  36.7 0.5 shard_map.137
  37.1 0.1 collective-permute-start.13
  37.2 0.7 %shard_map.134.partial = f32[1344,192]{1,0:T(8,128)S(1)} custom-call(bf16[1344,256]{1,0:T(8,128)(2,1)S(1)} %bitcast.7, bf16[1344,256]{1,0:T(8,128)(2,1)S(1)} %collective-permute-done.1.w1, bf16[1344,256]{1,0:T(8,128)(2,1)S(1)} %collective-permute-done.9.w2, bf16[192,256]{1,0:T(8,128)(2,1)S(1)} %shard_map.132.a0, ...), custom_call_target="tpu_custom_call" | custom-call | flops 5549064192 | tf_op jit(solution)/shard_map/pallas_call | solution.py:415
  37.9 0.4 shard_map.135.own
  38.3 0.0 copy-start.4
  38.4 0.0 copy-start.2
  38.4 0.0 copy-start
  38.4 0.0 copy-start.1
  38.4 0.7 %collective-permute-done.13.received = bf16[2016,128]{1,0:T(8,128)(2,1)S(1)} collective-permute-done((bf16[2016,128]{1,0:T(8,128)(2,1)S(1)}, bf16[2016,128]{1,0:T(8,128)(2,1)S(1)}, u32[]{:S(2)}, u32[]{:S(2)}) %collective-permute-start.13) | collective-permute-done | bytes 516128 | tf_op jit(solution)/shard_map/ppermute | solution.py:440
  39.1 0.3 shard_map.138
  39.4 1.7 %collective-permute-start.14 = (f32[1,192]{1,0:T(1,128)S(1)}, f32[1,192]{1,0:T(1,128)S(1)}, u32[]{:S(2)}, u32[]{:S(2)}) collective-permute-start(f32[1,192]{1,0:T(1,128)S(1)} %get-tuple-element.31.s0), channel_id=1, source_target_pairs={{0,1},{1,2},{2,3},{3,0},{4,5},{5,6},{6,7},{7,4},{8,9},{9,10},{10,1... | collective-permute-start | bytes 2312 | tf_op jit(solution)/shard_map/ppermute | solution.py:360
  41.1 2.6 %collective-permute-start.15 = (f32[1,192]{1,0:T(1,128)S(1)}, f32[1,192]{1,0:T(1,128)S(1)}, u32[]{:S(2)}, u32[]{:S(2)}) collective-permute-start(f32[1,192]{1,0:T(1,128)S(1)} %get-tuple-element.31.s0), channel_id=1, source_target_pairs={{0,2},{1,3},{2,0},{3,1},{4,6},{5,7},{6,4},{7,5},{8,10},{9,11},{10,... | collective-permute-start | bytes 2312 | tf_op jit(solution)/shard_map/ppermute | solution.py:360
  43.7 1.3 %collective-permute-start.16 = (f32[1,192]{1,0:T(1,128)S(1)}, f32[1,192]{1,0:T(1,128)S(1)}, u32[]{:S(2)}, u32[]{:S(2)}) collective-permute-start(f32[1,192]{1,0:T(1,128)S(1)} %get-tuple-element.31.s0), channel_id=1, source_target_pairs={{0,3},{1,0},{2,1},{3,2},{4,7},{5,4},{6,5},{7,6},{8,11},{9,8},{10,9... | collective-permute-start | bytes 2312 | tf_op jit(solution)/shard_map/ppermute | solution.py:360
  45.0 0.0 copy-done.4
  45.0 0.0 copy-done.2
  45.0 1.0 %shard_map.139 = (f32[1344,128]{1,0:T(8,128)S(1)}, f32[64,1344]{1,0:T(8,128)S(1)}, f32[64,128]{1,0:T(8,128)S(1)}, f32[64,128]{1,0:T(8,128)S(1)}) custom-call(s32[1,2]{1,0:T(1,128)S(1)} %copy-done.2, f32[1344,192]{1,0:T(8,128)S(1)} %get-tuple-element.26.projected, f32[1,1344]{1,0:T(1,128)S(1)} %broadcast_in_dim.3.gain), custom_call_target="tpu_custom_call" | custom-call | tf_op jit(solution)/shard_map/pallas_call | solution.py:447
  46.0 0.0 collective-permute-done.14.s1
  46.0 0.0 collective-permute-done.15.s2
  46.0 1.2 %collective-permute-done.16.s3 = f32[1,192]{1,0:T(1,128)S(1)} collective-permute-done((f32[1,192]{1,0:T(1,128)S(1)}, f32[1,192]{1,0:T(1,128)S(1)}, u32[]{:S(2)}, u32[]{:S(2)}) %collective-permute-start.16) | collective-permute-done | bytes 800 | tf_op jit(solution)/shard_map/ppermute | solution.py:360
  47.2 0.0 copy-done
  47.2 0.0 copy-done.1
  47.2 1.2 %shard_map.140 = (bf16[1344,128]{1,0:T(8,128)(2,1)}, bf16[1,64,1344]{2,1,0:T(8,128)(2,1)}, f32[1,1344]{1,0:T(1,128)}) custom-call(f32[1344,128]{1,0:T(8,128)S(1)} %get-tuple-element.27.prefix, f32[64,1344]{1,0:T(8,128)S(1)} %get-tuple-element.28.option, f32[64,128]{1,0:T(8,128)S(1)} %get-tuple-element.29.kept, f32[64,128]{1,0:T(8,128)S(1)} %get-tuple-element.30.share, ...), custom_call_target="tpu_custom_call" | custom-call | tf_op jit(solution)/shard_map/pallas_call | solution.py:459
  (2 shorter events, 0.0 us)
Async XLA Ops:
  1.8 1.6 %collective-permute-start = (bf16[384,256]{1,0:T(8,128)(2,1)S(1)}, bf16[384,256]{1,0:T(8,128)(2,1)S(1)}, u32[]{:S(2)}, u32[]{:S(2)}) collective-permute-start(bf16[384,256]{1,0:T(8,128)(2,1)S(1)} %get-tuple-element.19), channel_id=1, source_target_pairs={{0,4},{4,0},{8,12},{12,8},{16,20},{20,16},{24,28},{28,24},{1,5},{5... | collective-permute-start | bytes 589832 | tf_op jit(solution)/shard_map/ppermute | solution.py:381
  3.4 7.1 %collective-permute-start.2 = (bf16[256,256]{1,0:T(8,128)(2,1)S(1)}, bf16[256,256]{1,0:T(8,128)(2,1)S(1)}, u32[]{:S(2)}, u32[]{:S(2)}) collective-permute-start(bf16[256,256]{1,0:T(8,128)(2,1)S(1)} %shard_map.131.kv0), channel_id=1, source_target_pairs={{0,16},{4,12},{8,24},{12,4},{16,0},{20,28},{24,8},{28,20},{1,17},{... | collective-permute-start | bytes 393224 | tf_op jit(solution)/shard_map/ppermute | solution.py:385
  6.3 6.3 %collective-permute-start.3 = (bf16[256,256]{1,0:T(8,128)(2,1)S(1)}, bf16[256,256]{1,0:T(8,128)(2,1)S(1)}, u32[]{:S(2)}, u32[]{:S(2)}) collective-permute-start(bf16[256,256]{1,0:T(8,128)(2,1)S(1)} %shard_map.131.kv0), channel_id=1, source_target_pairs={{0,8},{4,20},{8,0},{12,28},{16,24},{20,4},{24,16},{28,12},{1,9},{5... | collective-permute-start | bytes 393224 | tf_op jit(solution)/shard_map/ppermute | solution.py:386
  7.8 7.4 %collective-permute-start.4 = (bf16[256,256]{1,0:T(8,128)(2,1)S(1)}, bf16[256,256]{1,0:T(8,128)(2,1)S(1)}, u32[]{:S(2)}, u32[]{:S(2)}) collective-permute-start(bf16[256,256]{1,0:T(8,128)(2,1)S(1)} %shard_map.131.kv0), channel_id=1, source_target_pairs={{0,24},{4,28},{8,16},{12,20},{16,8},{20,12},{24,0},{28,4},{1,25},{... | collective-permute-start | bytes 393224 | tf_op jit(solution)/shard_map/ppermute | solution.py:387
  7.9 8.6 %copy-start.3 = (bf16[256,1344]{0,1:T(8,128)(2,1)S(1)}, bf16[256,1344]{0,1:T(8,128)(2,1)}, u32[]{:S(2)}) copy-start(bf16[256,1344]{0,1:T(8,128)(2,1)} %param.19) | copy-start | bytes 2064388
  7.9 17.9 %collective-permute-start.1 = (bf16[1344,256]{1,0:T(8,128)(2,1)}, bf16[1344,256]{1,0:T(8,128)(2,1)S(1)}, u32[]{:S(2)}, u32[]{:S(2)}) collective-permute-start(bf16[1344,256]{1,0:T(8,128)(2,1)} %bitcast.4), channel_id=1, source_target_pairs={{0,16},{4,12},{8,24},{12,4},{16,0},{20,28},{24,8},{28,20},{1,17},{... | collective-permute-start | bytes 2064392 | tf_op jit(solution)/shard_map/ppermute | solution.py:408
  16.5 18.4 %collective-permute-start.9 = (bf16[1344,256]{1,0:T(8,128)(2,1)S(1)}, bf16[1344,256]{1,0:T(8,128)(2,1)S(1)}, u32[]{:S(2)}, u32[]{:S(2)}) collective-permute-start(bf16[1344,256]{1,0:T(8,128)(2,1)S(1)} %bitcast.5), channel_id=1, source_target_pairs={{0,8},{4,20},{8,0},{12,28},{16,24},{20,4},{24,16},{28,12},{1,9},{5... | collective-permute-start | bytes 2064392 | tf_op jit(solution)/shard_map/ppermute | solution.py:409
  19.6 7.4 %collective-permute-start.7 = (bf16[192,256]{1,0:T(8,128)(2,1)S(1)}, bf16[192,256]{1,0:T(8,128)(2,1)S(1)}, u32[]{:S(2)}, u32[]{:S(2)}) collective-permute-start(bf16[192,256]{1,0:T(8,128)(2,1)S(1)} %shard_map.132.a0), channel_id=1, source_target_pairs={{0,2},{1,3},{2,0},{3,1},{4,6},{5,7},{6,4},{7,5},{8,10},{9,11},{10,... | collective-permute-start | bytes 294920 | tf_op jit(solution)/shard_map/ppermute | solution.py:369
  22.2 6.3 %collective-permute-start.11 = (bf16[192,256]{1,0:T(8,128)(2,1)S(1)}, bf16[192,256]{1,0:T(8,128)(2,1)S(1)}, u32[]{:S(2)}, u32[]{:S(2)}) collective-permute-start(bf16[192,256]{1,0:T(8,128)(2,1)S(1)} %shard_map.133.a0), channel_id=1, source_target_pairs={{0,2},{1,3},{2,0},{3,1},{4,6},{5,7},{6,4},{7,5},{8,10},{9,11},{10,... | collective-permute-start | bytes 294920 | tf_op jit(solution)/shard_map/ppermute | solution.py:369
  22.6 7.7 %collective-permute-start.6 = (bf16[192,256]{1,0:T(8,128)(2,1)S(1)}, bf16[192,256]{1,0:T(8,128)(2,1)S(1)}, u32[]{:S(2)}, u32[]{:S(2)}) collective-permute-start(bf16[192,256]{1,0:T(8,128)(2,1)S(1)} %shard_map.132.a0), channel_id=1, source_target_pairs={{0,1},{1,0},{2,3},{3,2},{4,5},{5,4},{6,7},{7,6},{8,9},{9,8},{10,11... | collective-permute-start | bytes 294920 | tf_op jit(solution)/shard_map/ppermute | solution.py:369
  25.7 10.9 %collective-permute-start.5 = (bf16[1344,256]{1,0:T(8,128)(2,1)S(1)}, bf16[1344,256]{1,0:T(8,128)(2,1)S(1)}, u32[]{:S(2)}, u32[]{:S(2)}) collective-permute-start(bf16[1344,256]{1,0:T(8,128)(2,1)S(1)} %collective-permute-done.1.w1), channel_id=1, source_target_pairs={{0,8},{4,20},{8,0},{12,28},{16,24},{20,4},{24,16},{28,12},{1,9},{5... | collective-permute-start | bytes 2064392 | tf_op jit(solution)/shard_map/ppermute | solution.py:410
  27.0 6.3 %collective-permute-start.10 = (bf16[192,256]{1,0:T(8,128)(2,1)S(1)}, bf16[192,256]{1,0:T(8,128)(2,1)S(1)}, u32[]{:S(2)}, u32[]{:S(2)}) collective-permute-start(bf16[192,256]{1,0:T(8,128)(2,1)S(1)} %shard_map.133.a0), channel_id=1, source_target_pairs={{0,1},{1,0},{2,3},{3,2},{4,5},{5,4},{6,7},{7,6},{8,9},{9,8},{10,11... | collective-permute-start | bytes 294920 | tf_op jit(solution)/shard_map/ppermute | solution.py:369
  28.6 4.6 %collective-permute-start.8 = (bf16[192,256]{1,0:T(8,128)(2,1)S(1)}, bf16[192,256]{1,0:T(8,128)(2,1)S(1)}, u32[]{:S(2)}, u32[]{:S(2)}) collective-permute-start(bf16[192,256]{1,0:T(8,128)(2,1)S(1)} %collective-permute-done.7.a2), channel_id=1, source_target_pairs={{0,1},{1,0},{2,3},{3,2},{4,5},{5,4},{6,7},{7,6},{8,9},{9,8},{10,11... | collective-permute-start | bytes 294920 | tf_op jit(solution)/shard_map/ppermute | solution.py:369
  30.3 4.6 %collective-permute-start.12 = (bf16[192,256]{1,0:T(8,128)(2,1)S(1)}, bf16[192,256]{1,0:T(8,128)(2,1)S(1)}, u32[]{:S(2)}, u32[]{:S(2)}) collective-permute-start(bf16[192,256]{1,0:T(8,128)(2,1)S(1)} %collective-permute-done.11.a2), channel_id=1, source_target_pairs={{0,1},{1,0},{2,3},{3,2},{4,5},{5,4},{6,7},{7,6},{8,9},{9,8},{10,11... | collective-permute-start | bytes 294920 | tf_op jit(solution)/shard_map/ppermute | solution.py:369
  37.1 2.0 %collective-permute-start.13 = (bf16[2016,128]{1,0:T(8,128)(2,1)S(1)}, bf16[2016,128]{1,0:T(8,128)(2,1)S(1)}, u32[]{:S(2)}, u32[]{:S(2)}) collective-permute-start(bf16[2016,128]{1,0:T(8,128)(2,1)S(1)} %shard_map.137), channel_id=1, source_target_pairs={{0,4},{4,0},{8,12},{12,8},{16,20},{20,16},{24,28},{28,24},{1,5},{5... | collective-permute-start | bytes 1548296 | tf_op jit(solution)/shard_map/ppermute | solution.py:440
  38.3 6.7 %copy-start.4 = (f32[1344]{0:T(1024)S(1)}, f32[1344]{0:T(1024)}, u32[]{:S(2)}) copy-start(f32[1344]{0:T(1024)} %param.20) | copy-start | bytes 16132
  38.4 6.7 %copy-start.2 = (s32[1,2]{1,0:T(1,128)S(1)}, s32[1,2]{1,0:T(1,128)}, u32[]{:S(2)}) copy-start(s32[1,2]{1,0:T(1,128)} %bounds.1) | copy-start | bytes 28
  38.4 8.9 %copy-start = (bf16[128,1344]{0,1:T(8,128)(2,1)S(1)}, bf16[128,1344]{0,1:T(8,128)(2,1)}, u32[]{:S(2)}) copy-start(bf16[128,1344]{0,1:T(8,128)(2,1)} %param.14) | copy-start | bytes 1032196
  38.4 8.9 %copy-start.1 = (bf16[1,64,1344]{2,1,0:T(8,128)(2,1)S(1)}, bf16[1,64,1344]{2,1,0:T(8,128)(2,1)}, u32[]{:S(2)}) copy-start(bf16[1,64,1344]{2,1,0:T(8,128)(2,1)} %opt_resid.1) | copy-start | bytes 516100
  39.4 6.6 %collective-permute-start.14 = (f32[1,192]{1,0:T(1,128)S(1)}, f32[1,192]{1,0:T(1,128)S(1)}, u32[]{:S(2)}, u32[]{:S(2)}) collective-permute-start(f32[1,192]{1,0:T(1,128)S(1)} %get-tuple-element.31.s0), channel_id=1, source_target_pairs={{0,1},{1,2},{2,3},{3,0},{4,5},{5,6},{6,7},{7,4},{8,9},{9,10},{10,1... | collective-permute-start | bytes 2312 | tf_op jit(solution)/shard_map/ppermute | solution.py:360
  41.1 4.9 %collective-permute-start.15 = (f32[1,192]{1,0:T(1,128)S(1)}, f32[1,192]{1,0:T(1,128)S(1)}, u32[]{:S(2)}, u32[]{:S(2)}) collective-permute-start(f32[1,192]{1,0:T(1,128)S(1)} %get-tuple-element.31.s0), channel_id=1, source_target_pairs={{0,2},{1,3},{2,0},{3,1},{4,6},{5,7},{6,4},{7,5},{8,10},{9,11},{10,... | collective-permute-start | bytes 2312 | tf_op jit(solution)/shard_map/ppermute | solution.py:360
  43.7 3.6 %collective-permute-start.16 = (f32[1,192]{1,0:T(1,128)S(1)}, f32[1,192]{1,0:T(1,128)S(1)}, u32[]{:S(2)}, u32[]{:S(2)}) collective-permute-start(f32[1,192]{1,0:T(1,128)S(1)} %get-tuple-element.31.s0), channel_id=1, source_target_pairs={{0,3},{1,0},{2,1},{3,2},{4,7},{5,4},{6,5},{7,6},{8,11},{9,8},{10,9... | collective-permute-start | bytes 2312 | tf_op jit(solution)/shard_map/ppermute | solution.py:360

commit v4 on v3

--- a/solution.py
+++ b/solution.py
@@ -125,7 +125,7 @@
     return (prefix_out, option_out[None], option_summary[None])
 
 
-LONG_P, LONG_O, LONG_M = 200, 1, 14
+ATTENTION_COST, PROJECTION_COST = 200, 8
 
 
 SMEM = pltpu.MemorySpace.SMEM
@@ -160,20 +160,22 @@
     return (0 * parity, 4 - 2 * parity, 2 + 2 * parity, 0 * parity + 6)
 
 
-def pack_kernel(q, k, v, oq, ok, ov, sent, kept, sems):
+def pack_kernel(q, k, v, oq, ok, ov, kept, sent, sems):
     parity = lax.rem(lax.axis_index("seq"), 2)
     rows, opt = q.shape[0], oq.shape[1]
     wide = q.shape[1] // 2
-    own = pl.ds(2 * rows + opt, opt)
-    pieces = []
-    for to, head in ((sent, 1 - parity), (kept, parity)):
+    mine = pl.ds(pl.multiple_of(parity * HD, HD), HD)
+    pieces = [
+        (k.at[:, mine], kept.at[0:rows, 0:HD]),
+        (v.at[:, mine], kept.at[0:rows, HD : 2 * HD]),
+    ]
+    for to, base, head in ((kept, rows, parity), (sent, 0, 1 - parity)):
         at = pl.ds(pl.multiple_of(head * HD, HD), HD)
         at_q = pl.ds(pl.multiple_of(head * wide, wide), wide)
+        own = pl.ds(base + rows + opt, opt)
         pieces += [
-            (k.at[:, at], to.at[0:rows, 0:HD]),
-            (v.at[:, at], to.at[0:rows, HD : 2 * HD]),
-            (q.at[:, at_q], to.at[rows : 2 * rows, :]),
-            (oq.at[0, :, at_q], to.at[2 * rows : 2 * rows + opt, :]),
+            (q.at[:, at_q], to.at[base : base + rows, :]),
+            (oq.at[0, :, at_q], to.at[base + rows : base + rows + opt, :]),
             (ok.at[0, :, at], to.at[own, 0:HD]),
             (ov.at[0, :, at], to.at[own, HD : 2 * HD]),
         ]
@@ -184,23 +186,26 @@
         copy.wait()
 
 
-def join_kernel(kept, received, out):
-    rows = out.shape[0] // 2
+def join_kernel(kept, k, v, out):
+    rows = k.shape[0]
+    mine = pl.ds(pl.multiple_of(lax.rem(lax.axis_index("seq"), 2) * HD, HD), HD)
     out[0:rows, :] = kept[0:rows, :]
-    out[rows : 2 * rows, :] = received[0:rows, :]
-
-
-def attn_kernel(flip, rows, opt, kv0, kv1, kv2, kv3, packed, out):
-    own = slice(2 * rows + opt, 2 * rows + 2 * opt)
-    attn(
-        (kv0, kv1, kv2, kv3),
-        flip,
-        packed[rows : 2 * rows, :],
-        packed[2 * rows : 2 * rows + opt, :],
-        packed[own, 0:HD],
-        packed[own, HD : 2 * HD],
-        out,
-    )
+    out[rows : 2 * rows, 0:HD] = k[:, mine]
+    out[rows : 2 * rows, HD : 2 * HD] = v[:, mine]
+
+
+def attn_kernel(rows, opt, kv0, kv1, kv2, kv3, received, kept, out):
+    for flip, base, packed in ((1, 0, received), (0, rows, kept)):
+        own = slice(base + rows + opt, base + rows + 2 * opt)
+        attn(
+            (kv0, kv1, kv2, kv3),
+            flip,
+            packed[base : base + rows, :],
+            packed[base + rows : base + rows + opt, :],
+            packed[own, 0:HD],
+            packed[own, HD : 2 * HD],
+            out.at[(1 - flip) * (rows + opt) : (2 - flip) * (rows + opt), :],
+        )
 
 
 def attn(slots, flip, q, oq, own_keys, own_values, out):
@@ -214,58 +219,78 @@
     )
     query_pos = (s ^ flip) * rows + lax.broadcasted_iota(jnp.int32, (rows, 1), 0)
     heads = q.shape[1] // HD
+    parts = [x[:, h * HD : (h + 1) * HD] for x in (q, oq) for h in range(heads)]
+    scores = dot_nt(jnp.concatenate(parts, axis=0), keys)
+    last = heads * rows
+    weights = []
     for h in range(heads):
-        scores = dot_nt(q[:, h * HD : (h + 1) * HD], keys)
-        scores = jnp.where(key_pos <= query_pos, scores, -jnp.inf)
-        top = jnp.max(scores, axis=1, keepdims=True)
-        weights = jnp.exp2((scores - top) * exp2_scale)
-        total = jnp.sum(weights, axis=1, keepdims=True)
-        mixed = dot_nn(weights.astype(jnp.bfloat16), values)
-        out[0:rows, h * HD : (h + 1) * HD] = (mixed / total).astype(jnp.bfloat16)
-    oq = jnp.concatenate([oq[:, h * HD : (h + 1) * HD] for h in range(heads)], axis=0)
+        mine = jnp.where(key_pos <= query_pos, scores[h * rows : (h + 1) * rows], -jnp.inf)
+        top = jnp.max(mine, axis=1, keepdims=True)
+        weights.append(jnp.exp2((mine - top) * exp2_scale).astype(jnp.bfloat16))
     step = lax.rem(lax.broadcasted_iota(jnp.int32, (heads * opt, 1), 0), opt)
-    scores = jnp.where(key_pos > step, dot_nt(oq, keys), -jnp.inf)
-    own = dot_nt(oq, own_keys)
+    mine = jnp.where(key_pos > step, scores[last:], -jnp.inf)
+    own = dot_nt(jnp.concatenate(parts[heads:], axis=0), own_keys)
     own = jnp.where(lax.broadcasted_iota(jnp.int32, (1, opt), 1) <= step, own, -jnp.inf)
-    top = jnp.maximum(
-        jnp.max(scores, axis=1, keepdims=True), jnp.max(own, axis=1, keepdims=True)
-    )
-    weights = jnp.exp2((scores - top) * exp2_scale)
-    own = jnp.exp2((own - top) * exp2_scale)
-    total = jnp.sum(weights, axis=1, keepdims=True) + jnp.sum(own, axis=1, keepdims=True)
-    mixed = dot_nn(weights.astype(jnp.bfloat16), values) + dot_nn(
-        own.astype(jnp.bfloat16), own_values
-    )
-    mixed = (mixed / total).astype(jnp.bfloat16)
+    top = jnp.maximum(jnp.max(mine, axis=1, keepdims=True), jnp.max(own, axis=1, keepdims=True))
+    weights.append(jnp.exp2((mine - top) * exp2_scale).astype(jnp.bfloat16))
+    own = jnp.exp2((own - top) * exp2_scale).astype(jnp.bfloat16)
+    mixed = dot_nn(jnp.concatenate(weights, axis=0), beside_ones(values))
     for h in range(heads):
-        out[rows : rows + opt, h * HD : (h + 1) * HD] = mixed[h * opt : (h + 1) * opt]
-
-
-def project_kernel(w0, w1, w2, a0, a1, a2, a3, out, placed):
-    z = lax.axis_index("head")
+        rest = mixed[h * rows : (h + 1) * rows]
+        out[0:rows, h * HD : (h + 1) * HD] = (rest[:, :HD] / rest[:, HD : HD + 1]).astype(
+            jnp.bfloat16
+        )
+    rest = mixed[last:] + dot_nn(own, beside_ones(own_values))
+    rest = (rest[:, :HD] / rest[:, HD : HD + 1]).astype(jnp.bfloat16)
+    for h in range(heads):
+        out[rows : rows + opt, h * HD : (h + 1) * HD] = rest[h * opt : (h + 1) * opt]
+
+
+def beside_ones(values):
+    return jnp.concatenate([values, jnp.ones_like(values)], axis=1)
+
+
+def apart():
+    s, z = lax.axis_index("seq"), lax.axis_index("head")
+    return [((s ^ mask) >> 1) ^ z for mask in masks(s)]
+
+
+def project_kernel(w0, w1, w2, a0, a1, a2, pair_out, own_out, chosen, placed):
+    for t, block in enumerate((a0, a1, a2)):
+        placed[t] = block[...]
+    placed[3] = jnp.zeros_like(a0)
+    meets = apart()
+    held = (w0, w1, w2)
+    chosen[...] = w0[...]
+    for j in (1, 2):
+
+        @pl.when(meets[j] == 3)
+        def _():
+            chosen[...] = held[j][...]
+
+    count = a0.shape[0] // 2
+    middle = w0.shape[0] // 2
+    for r, out in enumerate((pair_out, own_out)):
+        blocks = [placed[meets[j], r * count : (r + 1) * count, :] for j in range(3)]
+        for n in range(2):
+            part = slice(n * middle, (n + 1) * middle)
+            total = dot_nt(w0[part, :], blocks[0]) + dot_nt(w1[part, :], blocks[1])
+            out[part, :] = total + dot_nt(w2[part, :], blocks[2])
+
+
+def complete_kernel(rows, opt, packed, w3, chosen, a0, a1, a2, a3, partial, out, placed):
+    mine = slice(0, rows + opt) if packed else slice(rows + opt, 2 * (rows + opt))
     for t, block in enumerate((a0, a1, a2, a3)):
-        placed[z ^ t] = block[...]
-    s = lax.axis_index("seq")
-    blocks = [placed[(s ^ m) >> 1] for m in masks(s)]
-    half = out.shape[0] // 2
-    for n in range(2):
-        part = slice(n * half, (n + 1) * half)
-        total = dot_nt(w0[part, :], blocks[0])
-        total += dot_nt(w1[part, :], blocks[1])
-        out[part, :] = total + dot_nt(w2[part, :], blocks[2])
-
-
-def complete_kernel(rows, opt, packed, w3, a0, a1, a2, a3, partial, out, placed):
-    z = lax.axis_index("head")
-    for t, block in enumerate((a0, a1, a2, a3)):
-        placed[z ^ t] = block[...]
-    s = lax.axis_index("seq")
-    block = placed[(s ^ masks(s)[3]) >> 1]
+        placed[t] = block[mine, :]
+    meets = apart()[3]
+    first = placed[meets]
+    second = jnp.where(meets == 3, jnp.zeros_like(first), placed[3])
     features = w3.shape[0]
     half = features // 2
     for n in range(2):
         part = slice(n * half, (n + 1) * half)
-        total = partial[part, :] + dot_nt(w3[part, :], block)
+        total = dot_nt(w3[part, :], first) + dot_nt(chosen[part, :], second)
+        total += partial[part, :]
         if packed:
             total = total.astype(out.dtype)
             out[part, :] = total[:, 0:rows]
@@ -370,75 +395,58 @@
 
     weight = out_weight.T
 
-    packed = pltpu.VMEM((2 * rows + 2 * opt, wide), bf16)
-    sent, kept = call(
+    pair_k = lax.ppermute(keys, "seq", pair)
+    pair_v = lax.ppermute(values, "seq", pair)
+    kept, sent = call(
         pack_kernel,
-        [packed, packed],
+        [pltpu.VMEM((2 * rows + 2 * opt, wide), bf16), pltpu.VMEM((rows + 2 * opt, wide), bf16)],
         6,
         in_specs=[pl.BlockSpec(memory_space=HBM)] * 6,
-        scratch=[pltpu.SemaphoreType.DMA((12,))],
+        scratch=[pltpu.SemaphoreType.DMA((10,))],
     )(*map(in_hbm, (queries, keys, values, opt_queries, opt_keys, opt_values)))
-    received = lax.ppermute(sent, "seq", pair)
-    kv_0 = call(join_kernel, pltpu.VMEM((2 * rows, 2 * HD), bf16), 2)(kept, received)
-    slots = (
-        kv_0,
-        lax.ppermute(kv_0, "seq", first),
-        lax.ppermute(kv_0, "seq", second),
-        lax.ppermute(kv_0, "seq", both),
-    )
-
-    attn_shape = pltpu.VMEM((rows + opt, wide), bf16)
-
-    def attention(flip, block, weight):
-        return call(
-            functools.partial(attn_kernel, flip, rows, opt),
-            attn_shape,
-            5,
-            flops=weight * 4 * (rows + opt) * wide * WINDOW,
-            vmem=24,
-        )(*slots, block)
-
-    pair_0 = attention(1, received, LONG_P)
-    own_0 = attention(0, kept, LONG_O)
-    pair_1, pair_2 = crossed(pair_0, 1), crossed(pair_0, 2)
-    own_1, own_2 = crossed(own_0, 1), crossed(own_0, 2)
-    pair_3 = crossed(after(pair_2, own_0), 1)
-    own_3 = crossed(own_2, 1)
-
-    weight_1 = lax.ppermute(after(weight, received), "seq", first)
-    weight_2 = lax.ppermute(after(weight, pair_0), "seq", second)
-    weight_3 = lax.ppermute(after(weight_1, own_0), "seq", second)
-    flops = 2 * features * wide * (rows + opt)
-    placed = [pltpu.VMEM((4, rows + opt, wide), bf16)]
-
-    def project(blocks):
-        return call(
-            project_kernel,
-            shape((features, rows + opt), f32),
-            7,
-            flops=LONG_M * 3 * flops,
-            scratch=placed,
-            vmem=16,
-        )(weight, weight_1, weight_2, *blocks)
-
-    def complete(partial, blocks, out_shape, packed):
+    kv_0 = call(join_kernel, pltpu.VMEM((2 * rows, 2 * HD), bf16), 3)(kept, pair_k, pair_v)
+    received = lax.ppermute(after(sent, kv_0), "seq", pair)
+    kv_3 = lax.ppermute(kv_0, "seq", both)
+    kv_1 = lax.ppermute(kv_0, "seq", first)
+    kv_2 = lax.ppermute(kv_0, "seq", second)
+    slots = (kv_0, kv_1, kv_2, kv_3)
+
+    block = call(
+        functools.partial(attn_kernel, rows, opt),
+        pltpu.VMEM((2 * (rows + opt), wide), bf16),
+        6,
+        flops=ATTENTION_COST * 4 * (rows + opt) * wide * WINDOW,
+        vmem=24,
+    )(*slots, received, kept)
+    block_1, block_2 = crossed(block, 1), crossed(block, 2)
+    blocks = (block, block_1, block_2, crossed(block_2, 1))
+
+    weight_1 = lax.ppermute(after(weight, kv_0), "seq", first)
+    weight_2 = lax.ppermute(after(weight, block), "seq", second)
+    weight_3 = lax.ppermute(after(weight_1, block), "seq", second)
+    flops = 4 * features * wide * (rows + opt)
+    pair_part, own_part, chosen = call(
+        project_kernel,
+        [shape((features, rows + opt), f32)] * 2 + [shape((features, wide), bf16)],
+        6,
+        flops=PROJECTION_COST * 3 * flops,
+        scratch=[pltpu.VMEM((4, 2 * (rows + opt), wide), bf16)],
+        vmem=16,
+    )(weight, weight_1, weight_2, *blocks[:3])
+
+    def complete(partial, out_shape, packed):
         return call(
             functools.partial(complete_kernel, rows, opt, packed),
             out_shape,
-            6,
-            flops=flops,
-            scratch=placed,
+            7,
+            flops=flops // 2,
+            scratch=[pltpu.VMEM((4, rows + opt, wide), bf16)],
             vmem=16,
-        )(weight_3, *blocks, partial)
-
-    pair_blocks = (after(pair_0, own_1, own_3), pair_1, pair_2, pair_3)
-    own_blocks = (own_0, own_1, own_2, own_3)
-    pair_part, own_part = project(pair_blocks), project(own_blocks)
-    half = complete(
-        pair_part, pair_blocks, shape((features + features // 2, rows), bf16), True
-    )
+        )(weight_3, chosen, *blocks, partial)
+
+    half = complete(pair_part, shape((features + features // 2, rows), bf16), True)
     received = lax.ppermute(half, "seq", pair)
-    own = complete(own_part, own_blocks, shape((features, rows + opt), f32), False)
+    own = complete(own_part, shape((features, rows + opt), f32), False)
     projected, squares = call(
         functools.partial(square_kernel, rows, opt),
         [shape((features, rows + opt), f32), shape((1, rows + opt), f32)],

time: 48.6 us -> 47.7 us (0.981)
  starting transfers between devices: 24 us -> 20.8 us
  waiting for transfers between devices: 15.2 us -> 18.2 us
  Pallas kernels: 8.44 us -> 7.75 us
    ppermute x6 -> x3, starting transfers between devices: 8.29 us -> 4.69 us  [crossed(): lax.ppermute(value, 'head', [(i, i ^ mask) for i in range(lax.axis_size('...]
    ppermute x7 -> x9, waiting for transfers between devices: 9.02 us -> 10.6 us  [the longest x1 2.62 us: paired_body(): weight_3 = lax.ppermute(after(weight_1, block), 'seq', second)]
    ppermute x6 -> x3, waiting for transfers between devices: 4.24 us -> 5.19 us  [crossed(): lax.ppermute(value, 'head', [(i, i ^ mask) for i in range(lax.axis_size('...]
    pallas_call x8 -> x6, Pallas kernels: 6 us -> 5.31 us  [the longest x1 1.72 us: paired_body(): call(functools.partial(attn_kernel, rows, opt), pltpu.VMEM((2 * (rows + o...]
    ppermute x7 -> x9, starting transfers between devices: 10 us -> 10.3 us  [the longest x1 2.87 us: paired_body(): kv_1 = lax.ppermute(kv_0, 'seq', first)]
  transfers between devices with their start and end apart: 17 -> 16, of which waited for: 10 -> 11; matrix products, arithmetic and copies ran while one was open for 0% -> 0% of each run, Pallas kernels for 11% -> 12%
where the time goes in v4:
time: 47.7 us; the launch traced here: 47.5 us
  starting transfers between devices  20.8 us (44%)
  waiting for transfers between devices  18.2 us (38%)
  Pallas kernels  7.75 us (16%)
  between operations  0.75 us (2%)
    ppermute x3, starting transfers between devices, turned(): lax.ppermute(value, 'head', [(i, (i + steps) % count) for i in range(coun...  5.57 us
    ppermute x3, waiting for transfers between devices, crossed(): lax.ppermute(value, 'head', [(i, i ^ mask) for i in range(lax.axis_size('...  5.19 us
    ppermute x3, starting transfers between devices, crossed(): lax.ppermute(value, 'head', [(i, i ^ mask) for i in range(lax.axis_size('...  4.69 us
    ppermute x1, starting transfers between devices, paired_body(): kv_1 = lax.ppermute(kv_0, 'seq', first)  2.87 us
    ppermute x1, waiting for transfers between devices, paired_body(): weight_3 = lax.ppermute(after(weight_1, block), 'seq', second)  2.62 us
    ppermute x1, waiting for transfers between devices, paired_body(): kv_3 = lax.ppermute(kv_0, 'seq', both)  2.55 us
    ppermute x1, waiting for transfers between devices, paired_body(): weight_1 = lax.ppermute(after(weight, kv_0), 'seq', first)  2.28 us
    ppermute x1, waiting for transfers between devices, paired_body(): kv_2 = lax.ppermute(kv_0, 'seq', second)  2.26 us
  transfers between devices with their start and end apart: 16, of which 11 were waited for; matrix products, arithmetic and copies ran while one was open for 0% of the time, Pallas kernels for 12%

profile of v4, /device:TPU:0, one launch (start us, length us, event | category | flops | bytes accessed | tf_op | source)
XLA Modules:
  0.0 47.5 jit_solution(14261518092194242418)
XLA Ops:
  0.6 0.5 %collective-permute-start = (bf16[128,256]{1,0:T(8,128)(2,1)}, bf16[128,256]{1,0:T(8,128)(2,1)S(1)}, u32[]{:S(2)}, u32[]{:S(2)}) collective-permute-start(bf16[128,256]{1,0:T(8,128)(2,1)} %k.1), channel_id=1, source_target_pairs={{0,4},{4,0},{8,12},{12,8},{16,20},{20,16},{24,28},{28,24},{1,5},{5... | collective-permute-start | bytes 196616 | tf_op jit(solution)/shard_map/ppermute | solution.py:398
  1.1 0.1 collective-permute-start.1
  1.2 1.1 %shard_map.130 = (bf16[384,256]{1,0:T(8,128)(2,1)S(1)}, bf16[256,256]{1,0:T(8,128)(2,1)S(1)}) custom-call(bf16[128,512]{1,0:T(8,128)(2,1)} %q.1, bf16[128,256]{1,0:T(8,128)(2,1)} %k.1, bf16[128,256]{1,0:T(8,128)(2,1)} %v.1, bf16[1,64,512]{2,1,0:T(8,128)(2,1)} %oq.1, bf16[1,64,256]{2,1,0:T(8,128)(2,1)} %ok.1, bf16[1,64,256]{2,1,0:T(8,128)(2,1)} %ov.1), custom_call_target="tpu_custom_call" | custom-call | tf_op jit(solution)/shard_map/pallas_call | solution.py:400
  2.3 0.0 collective-permute-done.k
  2.3 0.3 collective-permute-done.1.v
  2.6 0.2 collective-permute-start.6
  2.9 2.9 %collective-permute-start.3 = (bf16[256,256]{1,0:T(8,128)(2,1)S(1)}, bf16[256,256]{1,0:T(8,128)(2,1)S(1)}, u32[]{:S(2)}, u32[]{:S(2)}) collective-permute-start(bf16[256,256]{1,0:T(8,128)(2,1)S(1)} %shard_map.131.kv0), channel_id=1, source_target_pairs={{0,16},{4,12},{8,24},{12,4},{16,0},{20,28},{24,8},{28,20},{1,17},{... | collective-permute-start | bytes 393224 | tf_op jit(solution)/shard_map/ppermute | solution.py:410
  5.7 1.5 %collective-permute-start.4 = (bf16[256,256]{1,0:T(8,128)(2,1)S(1)}, bf16[256,256]{1,0:T(8,128)(2,1)S(1)}, u32[]{:S(2)}, u32[]{:S(2)}) collective-permute-start(bf16[256,256]{1,0:T(8,128)(2,1)S(1)} %shard_map.131.kv0), channel_id=1, source_target_pairs={{0,8},{4,20},{8,0},{12,28},{16,24},{20,4},{24,16},{28,12},{1,9},{5... | collective-permute-start | bytes 393224 | tf_op jit(solution)/shard_map/ppermute | solution.py:411
  7.2 0.0 collective-permute-start.5
  7.2 0.0 copy-start.3
  7.2 2.0 %collective-permute-start.2 = (bf16[1344,256]{1,0:T(8,128)(2,1)}, bf16[1344,256]{1,0:T(8,128)(2,1)S(1)}, u32[]{:S(2)}, u32[]{:S(2)}) collective-permute-start(bf16[1344,256]{1,0:T(8,128)(2,1)} %bitcast.4), channel_id=1, source_target_pairs={{0,16},{4,12},{8,24},{12,4},{16,0},{20,28},{24,8},{28,20},{1,17},{... | collective-permute-start | bytes 2064392 | tf_op jit(solution)/shard_map/ppermute | solution.py:424
  9.2 0.0 collective-permute-done.6.received
  9.2 0.6 %collective-permute-done.3.kv1 = bf16[256,256]{1,0:T(8,128)(2,1)S(1)} collective-permute-done((bf16[256,256]{1,0:T(8,128)(2,1)S(1)}, bf16[256,256]{1,0:T(8,128)(2,1)S(1)}, u32[]{:S(2)}, u32[]{:S(2)}) %collective-permute-start.3) | collective-permute-done | bytes 131104 | tf_op jit(solution)/shard_map/ppermute | solution.py:410
  9.8 2.3 %collective-permute-done.4.kv2 = bf16[256,256]{1,0:T(8,128)(2,1)S(1)} collective-permute-done((bf16[256,256]{1,0:T(8,128)(2,1)S(1)}, bf16[256,256]{1,0:T(8,128)(2,1)S(1)}, u32[]{:S(2)}, u32[]{:S(2)}) %collective-permute-start.4) | collective-permute-done | bytes 131104 | tf_op jit(solution)/shard_map/ppermute | solution.py:411
  12.0 2.5 %collective-permute-done.5.kv3 = bf16[256,256]{1,0:T(8,128)(2,1)S(1)} collective-permute-done((bf16[256,256]{1,0:T(8,128)(2,1)S(1)}, bf16[256,256]{1,0:T(8,128)(2,1)S(1)}, u32[]{:S(2)}, u32[]{:S(2)}) %collective-permute-start.5) | collective-permute-done | bytes 131104 | tf_op jit(solution)/shard_map/ppermute | solution.py:409
  14.6 1.7 %shard_map.132.a0 = bf16[384,256]{1,0:T(8,128)(2,1)S(1)} custom-call(bf16[256,256]{1,0:T(8,128)(2,1)S(1)} %shard_map.131.kv0, bf16[256,256]{1,0:T(8,128)(2,1)S(1)} %collective-permute-done.3.kv1, bf16[256,256]{1,0:T(8,128)(2,1)S(1)} %collective-permute-done.4.kv2, bf16[256,256]{1,0:T(8,128)(2,1)S(1)} %collective-permute-done.5.kv3, ...), custom_call_target="tpu_custom_call" | custom-call | flops 40265318400 | tf_op jit(solution)/shard_map/pallas_call | solution.py:414
  16.3 0.0 copy-done.3
  16.3 1.9 %collective-permute-start.8 = (bf16[1344,256]{1,0:T(8,128)(2,1)S(1)}, bf16[1344,256]{1,0:T(8,128)(2,1)S(1)}, u32[]{:S(2)}, u32[]{:S(2)}) collective-permute-start(bf16[1344,256]{1,0:T(8,128)(2,1)S(1)} %bitcast.5), channel_id=1, source_target_pairs={{0,8},{4,20},{8,0},{12,28},{16,24},{20,4},{24,16},{28,12},{1,9},{5... | collective-permute-start | bytes 2064392 | tf_op jit(solution)/shard_map/ppermute | solution.py:425
  18.2 2.6 %collective-permute-start.10 = (bf16[384,256]{1,0:T(8,128)(2,1)S(1)}, bf16[384,256]{1,0:T(8,128)(2,1)S(1)}, u32[]{:S(2)}, u32[]{:S(2)}) collective-permute-start(bf16[384,256]{1,0:T(8,128)(2,1)S(1)} %shard_map.132.a0), channel_id=1, source_target_pairs={{0,2},{1,3},{2,0},{3,1},{4,6},{5,7},{6,4},{7,5},{8,10},{9,11},{10,... | collective-permute-start | bytes 589832 | tf_op jit(solution)/shard_map/ppermute | solution.py:394
  20.8 1.6 %collective-permute-start.9 = (bf16[384,256]{1,0:T(8,128)(2,1)S(1)}, bf16[384,256]{1,0:T(8,128)(2,1)S(1)}, u32[]{:S(2)}, u32[]{:S(2)}) collective-permute-start(bf16[384,256]{1,0:T(8,128)(2,1)S(1)} %shard_map.132.a0), channel_id=1, source_target_pairs={{0,1},{1,0},{2,3},{3,2},{4,5},{5,4},{6,7},{7,6},{8,9},{9,8},{10,11... | collective-permute-start | bytes 589832 | tf_op jit(solution)/shard_map/ppermute | solution.py:394
  22.3 2.3 %collective-permute-done.2.w1 = bf16[1344,256]{1,0:T(8,128)(2,1)S(1)} collective-permute-done((bf16[1344,256]{1,0:T(8,128)(2,1)}, bf16[1344,256]{1,0:T(8,128)(2,1)S(1)}, u32[]{:S(2)}, u32[]{:S(2)}) %collective-permute-start.2) | collective-permute-done | bytes 688160 | tf_op jit(solution)/shard_map/ppermute | solution.py:424
  24.6 1.3 %collective-permute-start.7 = (bf16[1344,256]{1,0:T(8,128)(2,1)S(1)}, bf16[1344,256]{1,0:T(8,128)(2,1)S(1)}, u32[]{:S(2)}, u32[]{:S(2)}) collective-permute-start(bf16[1344,256]{1,0:T(8,128)(2,1)S(1)} %collective-permute-done.2.w1), channel_id=1, source_target_pairs={{0,8},{4,20},{8,0},{12,28},{16,24},{20,4},{24,16},{28,12},{1,9},{5... | collective-permute-start | bytes 2064392 | tf_op jit(solution)/shard_map/ppermute | solution.py:426
  25.9 1.4 %collective-permute-done.10.a2 = bf16[384,256]{1,0:T(8,128)(2,1)S(1)} collective-permute-done((bf16[384,256]{1,0:T(8,128)(2,1)S(1)}, bf16[384,256]{1,0:T(8,128)(2,1)S(1)}, u32[]{:S(2)}, u32[]{:S(2)}) %collective-permute-start.10) | collective-permute-done | bytes 196640 | tf_op jit(solution)/shard_map/ppermute | solution.py:394
  27.3 0.5 %collective-permute-start.11 = (bf16[384,256]{1,0:T(8,128)(2,1)S(1)}, bf16[384,256]{1,0:T(8,128)(2,1)S(1)}, u32[]{:S(2)}, u32[]{:S(2)}) collective-permute-start(bf16[384,256]{1,0:T(8,128)(2,1)S(1)} %collective-permute-done.10.a2), channel_id=1, source_target_pairs={{0,1},{1,0},{2,3},{3,2},{4,5},{5,4},{6,7},{7,6},{8,9},{9,8},{10,11... | collective-permute-start | bytes 589832 | tf_op jit(solution)/shard_map/ppermute | solution.py:394
  27.9 0.7 %collective-permute-done.9.a1 = bf16[384,256]{1,0:T(8,128)(2,1)S(1)} collective-permute-done((bf16[384,256]{1,0:T(8,128)(2,1)S(1)}, bf16[384,256]{1,0:T(8,128)(2,1)S(1)}, u32[]{:S(2)}, u32[]{:S(2)}) %collective-permute-start.9) | collective-permute-done | bytes 196640 | tf_op jit(solution)/shard_map/ppermute | solution.py:394
  28.6 0.0 collective-permute-done.8.w2
  28.6 1.3 %shard_map.133 = (f32[1344,192]{1,0:T(8,128)S(1)}, f32[1344,192]{1,0:T(8,128)S(1)}, bf16[1344,256]{1,0:T(8,128)(2,1)S(1)}) custom-call(bf16[1344,256]{1,0:T(8,128)(2,1)S(1)} %bitcast.6, bf16[1344,256]{1,0:T(8,128)(2,1)S(1)} %collective-permute-done.2.w1, bf16[1344,256]{1,0:T(8,128)(2,1)S(1)} %collective-permute-done.8.w2, ...), custom_call_target="tpu_custom_call" | custom-call | flops 6341787648 | tf_op jit(solution)/shard_map/pallas_call | solution.py:428
  29.9 3.1 %collective-permute-done.11.a3 = bf16[384,256]{1,0:T(8,128)(2,1)S(1)} collective-permute-done((bf16[384,256]{1,0:T(8,128)(2,1)S(1)}, bf16[384,256]{1,0:T(8,128)(2,1)S(1)}, u32[]{:S(2)}, u32[]{:S(2)}) %collective-permute-start.11) | collective-permute-done | bytes 196640 | tf_op jit(solution)/shard_map/ppermute | solution.py:394
  33.0 2.6 %collective-permute-done.7.w3 = bf16[1344,256]{1,0:T(8,128)(2,1)S(1)} collective-permute-done((bf16[1344,256]{1,0:T(8,128)(2,1)S(1)}, bf16[1344,256]{1,0:T(8,128)(2,1)S(1)}, u32[]{:S(2)}, u32[]{:S(2)}) %collective-permute-start.7) | collective-permute-done | bytes 688160 | tf_op jit(solution)/shard_map/ppermute | solution.py:426
  35.6 0.6 %shard_map.135 = bf16[2016,128]{1,0:T(8,128)(2,1)S(1)} custom-call(bf16[1344,256]{1,0:T(8,128)(2,1)S(1)} %collective-permute-done.7.w3, bf16[1344,256]{1,0:T(8,128)(2,1)S(1)} %get-tuple-element.27.chosen, bf16[384,256]{1,0:T(8,128)(2,1)S(1)} %shard_map.132.a0, bf16[384,256]{1,0:T(8,128)(2,1)S(1)} %collective-permute-done.9.a1, ...), custom_call_target="tpu_custom_call" | custom-call | flops 132120576 | tf_op jit(solution)/shard_map/pallas_call | solution.py:438
  36.2 0.2 collective-permute-start.12
  36.4 0.5 %shard_map.134.own = f32[1344,192]{1,0:T(8,128)S(1)} custom-call(bf16[1344,256]{1,0:T(8,128)(2,1)S(1)} %collective-permute-done.7.w3, bf16[1344,256]{1,0:T(8,128)(2,1)S(1)} %get-tuple-element.27.chosen, bf16[384,256]{1,0:T(8,128)(2,1)S(1)} %shard_map.132.a0, bf16[384,256]{1,0:T(8,128)(2,1)S(1)} %collective-permute-done.9.a1, ...), custom_call_target="tpu_custom_call" | custom-call | flops 132120576 | tf_op jit(solution)/shard_map/pallas_call | solution.py:438
  37.0 0.0 copy-start.4
  37.0 0.0 copy-start.2
  37.0 0.0 copy-start
  37.0 0.0 copy-start.1
  37.0 1.2 %collective-permute-done.12.received = bf16[2016,128]{1,0:T(8,128)(2,1)S(1)} collective-permute-done((bf16[2016,128]{1,0:T(8,128)(2,1)S(1)}, bf16[2016,128]{1,0:T(8,128)(2,1)S(1)}, u32[]{:S(2)}, u32[]{:S(2)}) %collective-permute-start.12) | collective-permute-done | bytes 516128 | tf_op jit(solution)/shard_map/ppermute | solution.py:448
  38.2 0.3 shard_map.136
  38.5 1.6 %collective-permute-start.13 = (f32[1,192]{1,0:T(1,128)S(1)}, f32[1,192]{1,0:T(1,128)S(1)}, u32[]{:S(2)}, u32[]{:S(2)}) collective-permute-start(f32[1,192]{1,0:T(1,128)S(1)} %get-tuple-element.35.s0), channel_id=1, source_target_pairs={{0,1},{1,2},{2,3},{3,0},{4,5},{5,6},{6,7},{7,4},{8,9},{9,10},{10,1... | collective-permute-start | bytes 2312 | tf_op jit(solution)/shard_map/ppermute | solution.py:385
  40.2 2.6 %collective-permute-start.14 = (f32[1,192]{1,0:T(1,128)S(1)}, f32[1,192]{1,0:T(1,128)S(1)}, u32[]{:S(2)}, u32[]{:S(2)}) collective-permute-start(f32[1,192]{1,0:T(1,128)S(1)} %get-tuple-element.35.s0), channel_id=1, source_target_pairs={{0,2},{1,3},{2,0},{3,1},{4,6},{5,7},{6,4},{7,5},{8,10},{9,11},{10,... | collective-permute-start | bytes 2312 | tf_op jit(solution)/shard_map/ppermute | solution.py:385
  42.7 1.3 %collective-permute-start.15 = (f32[1,192]{1,0:T(1,128)S(1)}, f32[1,192]{1,0:T(1,128)S(1)}, u32[]{:S(2)}, u32[]{:S(2)}) collective-permute-start(f32[1,192]{1,0:T(1,128)S(1)} %get-tuple-element.35.s0), channel_id=1, source_target_pairs={{0,3},{1,0},{2,1},{3,2},{4,7},{5,4},{6,5},{7,6},{8,11},{9,8},{10,9... | collective-permute-start | bytes 2312 | tf_op jit(solution)/shard_map/ppermute | solution.py:385
  44.1 0.0 copy-done.4
  44.1 0.0 copy-done.2
  44.1 1.0 %shard_map.137 = (f32[1344,128]{1,0:T(8,128)S(1)}, f32[64,1344]{1,0:T(8,128)S(1)}, f32[64,128]{1,0:T(8,128)S(1)}, f32[64,128]{1,0:T(8,128)S(1)}) custom-call(s32[1,2]{1,0:T(1,128)S(1)} %copy-done.2, f32[1344,192]{1,0:T(8,128)S(1)} %get-tuple-element.30.projected, f32[1,1344]{1,0:T(1,128)S(1)} %broadcast_in_dim.3.gain), custom_call_target="tpu_custom_call" | custom-call | tf_op jit(solution)/shard_map/pallas_call | solution.py:455
  45.1 0.0 collective-permute-done.13.s1
  45.1 0.0 collective-permute-done.14.s2
  45.1 1.2 %collective-permute-done.15.s3 = f32[1,192]{1,0:T(1,128)S(1)} collective-permute-done((f32[1,192]{1,0:T(1,128)S(1)}, f32[1,192]{1,0:T(1,128)S(1)}, u32[]{:S(2)}, u32[]{:S(2)}) %collective-permute-start.15) | collective-permute-done | bytes 800 | tf_op jit(solution)/shard_map/ppermute | solution.py:385
  46.3 0.0 copy-done
  46.3 0.0 copy-done.1
  46.3 1.2 %shard_map.138 = (bf16[1344,128]{1,0:T(8,128)(2,1)}, bf16[1,64,1344]{2,1,0:T(8,128)(2,1)}, f32[1,1344]{1,0:T(1,128)}) custom-call(f32[1344,128]{1,0:T(8,128)S(1)} %get-tuple-element.31.prefix, f32[64,1344]{1,0:T(8,128)S(1)} %get-tuple-element.32.option, f32[64,128]{1,0:T(8,128)S(1)} %get-tuple-element.33.kept, f32[64,128]{1,0:T(8,128)S(1)} %get-tuple-element.34.share, ...), custom_call_target="tpu_custom_call" | custom-call | tf_op jit(solution)/shard_map/pallas_call | solution.py:467
  (2 shorter events, 0.0 us)
Async XLA Ops:
  0.6 1.7 %collective-permute-start = (bf16[128,256]{1,0:T(8,128)(2,1)}, bf16[128,256]{1,0:T(8,128)(2,1)S(1)}, u32[]{:S(2)}, u32[]{:S(2)}) collective-permute-start(bf16[128,256]{1,0:T(8,128)(2,1)} %k.1), channel_id=1, source_target_pairs={{0,4},{4,0},{8,12},{12,8},{16,20},{20,16},{24,28},{28,24},{1,5},{5... | collective-permute-start | bytes 196616 | tf_op jit(solution)/shard_map/ppermute | solution.py:398
  1.1 1.5 %collective-permute-start.1 = (bf16[128,256]{1,0:T(8,128)(2,1)}, bf16[128,256]{1,0:T(8,128)(2,1)S(1)}, u32[]{:S(2)}, u32[]{:S(2)}) collective-permute-start(bf16[128,256]{1,0:T(8,128)(2,1)} %v.1), channel_id=1, source_target_pairs={{0,4},{4,0},{8,12},{12,8},{16,20},{20,16},{24,28},{28,24},{1,5},{5... | collective-permute-start | bytes 196616 | tf_op jit(solution)/shard_map/ppermute | solution.py:399
  2.6 6.6 %collective-permute-start.6 = (bf16[256,256]{1,0:T(8,128)(2,1)S(1)}, bf16[256,256]{1,0:T(8,128)(2,1)S(1)}, u32[]{:S(2)}, u32[]{:S(2)}) collective-permute-start(bf16[256,256]{1,0:T(8,128)(2,1)S(1)} %get-tuple-element.24), channel_id=1, source_target_pairs={{0,4},{4,0},{8,12},{12,8},{16,20},{20,16},{24,28},{28,24},{1,5},{5... | collective-permute-start | bytes 393224 | tf_op jit(solution)/shard_map/ppermute | solution.py:408
  2.9 6.9 %collective-permute-start.3 = (bf16[256,256]{1,0:T(8,128)(2,1)S(1)}, bf16[256,256]{1,0:T(8,128)(2,1)S(1)}, u32[]{:S(2)}, u32[]{:S(2)}) collective-permute-start(bf16[256,256]{1,0:T(8,128)(2,1)S(1)} %shard_map.131.kv0), channel_id=1, source_target_pairs={{0,16},{4,12},{8,24},{12,4},{16,0},{20,28},{24,8},{28,20},{1,17},{... | collective-permute-start | bytes 393224 | tf_op jit(solution)/shard_map/ppermute | solution.py:410
  5.7 6.3 %collective-permute-start.4 = (bf16[256,256]{1,0:T(8,128)(2,1)S(1)}, bf16[256,256]{1,0:T(8,128)(2,1)S(1)}, u32[]{:S(2)}, u32[]{:S(2)}) collective-permute-start(bf16[256,256]{1,0:T(8,128)(2,1)S(1)} %shard_map.131.kv0), channel_id=1, source_target_pairs={{0,8},{4,20},{8,0},{12,28},{16,24},{20,4},{24,16},{28,12},{1,9},{5... | collective-permute-start | bytes 393224 | tf_op jit(solution)/shard_map/ppermute | solution.py:411
  7.2 7.4 %collective-permute-start.5 = (bf16[256,256]{1,0:T(8,128)(2,1)S(1)}, bf16[256,256]{1,0:T(8,128)(2,1)S(1)}, u32[]{:S(2)}, u32[]{:S(2)}) collective-permute-start(bf16[256,256]{1,0:T(8,128)(2,1)S(1)} %shard_map.131.kv0), channel_id=1, source_target_pairs={{0,24},{4,28},{8,16},{12,20},{16,8},{20,12},{24,0},{28,4},{1,25},{... | collective-permute-start | bytes 393224 | tf_op jit(solution)/shard_map/ppermute | solution.py:409
  7.2 9.1 %copy-start.3 = (bf16[256,1344]{0,1:T(8,128)(2,1)S(1)}, bf16[256,1344]{0,1:T(8,128)(2,1)}, u32[]{:S(2)}) copy-start(bf16[256,1344]{0,1:T(8,128)(2,1)} %param.19) | copy-start | bytes 2064388
  7.2 17.4 %collective-permute-start.2 = (bf16[1344,256]{1,0:T(8,128)(2,1)}, bf16[1344,256]{1,0:T(8,128)(2,1)S(1)}, u32[]{:S(2)}, u32[]{:S(2)}) collective-permute-start(bf16[1344,256]{1,0:T(8,128)(2,1)} %bitcast.4), channel_id=1, source_target_pairs={{0,16},{4,12},{8,24},{12,4},{16,0},{20,28},{24,8},{28,20},{1,17},{... | collective-permute-start | bytes 2064392 | tf_op jit(solution)/shard_map/ppermute | solution.py:424
  16.3 12.3 %collective-permute-start.8 = (bf16[1344,256]{1,0:T(8,128)(2,1)S(1)}, bf16[1344,256]{1,0:T(8,128)(2,1)S(1)}, u32[]{:S(2)}, u32[]{:S(2)}) collective-permute-start(bf16[1344,256]{1,0:T(8,128)(2,1)S(1)} %bitcast.5), channel_id=1, source_target_pairs={{0,8},{4,20},{8,0},{12,28},{16,24},{20,4},{24,16},{28,12},{1,9},{5... | collective-permute-start | bytes 2064392 | tf_op jit(solution)/shard_map/ppermute | solution.py:425
  18.2 9.2 %collective-permute-start.10 = (bf16[384,256]{1,0:T(8,128)(2,1)S(1)}, bf16[384,256]{1,0:T(8,128)(2,1)S(1)}, u32[]{:S(2)}, u32[]{:S(2)}) collective-permute-start(bf16[384,256]{1,0:T(8,128)(2,1)S(1)} %shard_map.132.a0), channel_id=1, source_target_pairs={{0,2},{1,3},{2,0},{3,1},{4,6},{5,7},{6,4},{7,5},{8,10},{9,11},{10,... | collective-permute-start | bytes 589832 | tf_op jit(solution)/shard_map/ppermute | solution.py:394
  20.8 7.8 %collective-permute-start.9 = (bf16[384,256]{1,0:T(8,128)(2,1)S(1)}, bf16[384,256]{1,0:T(8,128)(2,1)S(1)}, u32[]{:S(2)}, u32[]{:S(2)}) collective-permute-start(bf16[384,256]{1,0:T(8,128)(2,1)S(1)} %shard_map.132.a0), channel_id=1, source_target_pairs={{0,1},{1,0},{2,3},{3,2},{4,5},{5,4},{6,7},{7,6},{8,9},{9,8},{10,11... | collective-permute-start | bytes 589832 | tf_op jit(solution)/shard_map/ppermute | solution.py:394
  24.6 11.0 %collective-permute-start.7 = (bf16[1344,256]{1,0:T(8,128)(2,1)S(1)}, bf16[1344,256]{1,0:T(8,128)(2,1)S(1)}, u32[]{:S(2)}, u32[]{:S(2)}) collective-permute-start(bf16[1344,256]{1,0:T(8,128)(2,1)S(1)} %collective-permute-done.2.w1), channel_id=1, source_target_pairs={{0,8},{4,20},{8,0},{12,28},{16,24},{20,4},{24,16},{28,12},{1,9},{5... | collective-permute-start | bytes 2064392 | tf_op jit(solution)/shard_map/ppermute | solution.py:426
  27.3 5.7 %collective-permute-start.11 = (bf16[384,256]{1,0:T(8,128)(2,1)S(1)}, bf16[384,256]{1,0:T(8,128)(2,1)S(1)}, u32[]{:S(2)}, u32[]{:S(2)}) collective-permute-start(bf16[384,256]{1,0:T(8,128)(2,1)S(1)} %collective-permute-done.10.a2), channel_id=1, source_target_pairs={{0,1},{1,0},{2,3},{3,2},{4,5},{5,4},{6,7},{7,6},{8,9},{9,8},{10,11... | collective-permute-start | bytes 589832 | tf_op jit(solution)/shard_map/ppermute | solution.py:394
  36.2 2.0 %collective-permute-start.12 = (bf16[2016,128]{1,0:T(8,128)(2,1)S(1)}, bf16[2016,128]{1,0:T(8,128)(2,1)S(1)}, u32[]{:S(2)}, u32[]{:S(2)}) collective-permute-start(bf16[2016,128]{1,0:T(8,128)(2,1)S(1)} %shard_map.135), channel_id=1, source_target_pairs={{0,4},{4,0},{8,12},{12,8},{16,20},{20,16},{24,28},{28,24},{1,5},{5... | collective-permute-start | bytes 1548296 | tf_op jit(solution)/shard_map/ppermute | solution.py:448
  37.0 7.1 %copy-start.4 = (f32[1344]{0:T(1024)S(1)}, f32[1344]{0:T(1024)}, u32[]{:S(2)}) copy-start(f32[1344]{0:T(1024)} %param.20) | copy-start | bytes 16132
  37.0 7.1 %copy-start.2 = (s32[1,2]{1,0:T(1,128)S(1)}, s32[1,2]{1,0:T(1,128)}, u32[]{:S(2)}) copy-start(s32[1,2]{1,0:T(1,128)} %bounds.1) | copy-start | bytes 28
  37.0 9.3 %copy-start = (bf16[128,1344]{0,1:T(8,128)(2,1)S(1)}, bf16[128,1344]{0,1:T(8,128)(2,1)}, u32[]{:S(2)}) copy-start(bf16[128,1344]{0,1:T(8,128)(2,1)} %param.14) | copy-start | bytes 1032196
  37.0 9.3 %copy-start.1 = (bf16[1,64,1344]{2,1,0:T(8,128)(2,1)S(1)}, bf16[1,64,1344]{2,1,0:T(8,128)(2,1)}, u32[]{:S(2)}) copy-start(bf16[1,64,1344]{2,1,0:T(8,128)(2,1)} %opt_resid.1) | copy-start | bytes 516100
  38.5 6.6 %collective-permute-start.13 = (f32[1,192]{1,0:T(1,128)S(1)}, f32[1,192]{1,0:T(1,128)S(1)}, u32[]{:S(2)}, u32[]{:S(2)}) collective-permute-start(f32[1,192]{1,0:T(1,128)S(1)} %get-tuple-element.35.s0), channel_id=1, source_target_pairs={{0,1},{1,2},{2,3},{3,0},{4,5},{5,6},{6,7},{7,4},{8,9},{9,10},{10,1... | collective-permute-start | bytes 2312 | tf_op jit(solution)/shard_map/ppermute | solution.py:385
  40.2 4.9 %collective-permute-start.14 = (f32[1,192]{1,0:T(1,128)S(1)}, f32[1,192]{1,0:T(1,128)S(1)}, u32[]{:S(2)}, u32[]{:S(2)}) collective-permute-start(f32[1,192]{1,0:T(1,128)S(1)} %get-tuple-element.35.s0), channel_id=1, source_target_pairs={{0,2},{1,3},{2,0},{3,1},{4,6},{5,7},{6,4},{7,5},{8,10},{9,11},{10,... | collective-permute-start | bytes 2312 | tf_op jit(solution)/shard_map/ppermute | solution.py:385
  42.7 3.6 %collective-permute-start.15 = (f32[1,192]{1,0:T(1,128)S(1)}, f32[1,192]{1,0:T(1,128)S(1)}, u32[]{:S(2)}, u32[]{:S(2)}) collective-permute-start(f32[1,192]{1,0:T(1,128)S(1)} %get-tuple-element.35.s0), channel_id=1, source_target_pairs={{0,3},{1,0},{2,1},{3,2},{4,7},{5,4},{6,5},{7,6},{8,11},{9,8},{10,9... | collective-permute-start | bytes 2312 | tf_op jit(solution)/shard_map/ppermute | solution.py:385

commit v5 on v4

--- a/solution.py
+++ b/solution.py
@@ -194,7 +194,7 @@
     out[rows : 2 * rows, HD : 2 * HD] = v[:, mine]
 
 
-def attn_kernel(rows, opt, kv0, kv1, kv2, kv3, received, kept, out):
+def attn_kernel(rows, opt, kv0, kv3, kv1, kv2, received, kept, out):
     for flip, base, packed in ((1, 0, received), (0, rows, kept)):
         own = slice(base + rows + opt, base + rows + 2 * opt)
         attn(
@@ -409,7 +409,7 @@
     kv_3 = lax.ppermute(kv_0, "seq", both)
     kv_1 = lax.ppermute(kv_0, "seq", first)
     kv_2 = lax.ppermute(kv_0, "seq", second)
-    slots = (kv_0, kv_1, kv_2, kv_3)
+    slots = (kv_0, kv_3, kv_1, kv_2)
 
     block = call(
         functools.partial(attn_kernel, rows, opt),

time: 47.7 us -> 47.7 us (level)
    ppermute x1, starting transfers between devices: 0.01 us -> 3.79 us  [paired_body(): kv_3 = lax.ppermute(kv_0, 'seq', both)]
    ppermute x1, starting transfers between devices: 2.87 us -> 0.51 us  [paired_body(): kv_1 = lax.ppermute(kv_0, 'seq', first)]
    ppermute x3, waiting for transfers between devices: 5.19 us -> 7.18 us  [crossed(): lax.ppermute(value, 'head', [(i, i ^ mask) for i in range(lax.axis_size('...]
    ppermute x1, waiting for transfers between devices: 0.55 us -> 2.34 us  [paired_body(): kv_1 = lax.ppermute(kv_0, 'seq', first)]
    ppermute x1, starting transfers between devices: 1.49 us -> 0.06 us  [paired_body(): kv_2 = lax.ppermute(kv_0, 'seq', second)]
    ppermute x1, waiting for transfers between devices: 2.26 us -> 1.06 us  [paired_body(): kv_2 = lax.ppermute(kv_0, 'seq', second)]
    ppermute x1, waiting for transfers between devices: 2.62 us -> 1.45 us  [paired_body(): weight_3 = lax.ppermute(after(weight_1, block), 'seq', second)]
    ppermute x1, waiting for transfers between devices: 2.55 us -> 1.71 us  [paired_body(): kv_3 = lax.ppermute(kv_0, 'seq', both)]
  transfers between devices with their start and end apart: 16 -> 16, of which waited for: 11 -> 10; matrix products, arithmetic and copies ran while one was open for 0% -> 0% of each run, Pallas kernels for 12% -> 12%
where the time goes in v5:
time: 47.7 us; the launch traced here: 47.5 us
  starting transfers between devices  20.7 us (43%)
  waiting for transfers between devices  18.3 us (38%)
  Pallas kernels  7.74 us (16%)
  between operations  0.76 us (2%)
    ppermute x3, waiting for transfers between devices, crossed(): lax.ppermute(value, 'head', [(i, i ^ mask) for i in range(lax.axis_size('...  7.18 us
    ppermute x3, starting transfers between devices, turned(): lax.ppermute(value, 'head', [(i, (i + steps) % count) for i in range(coun...  5.55 us
    ppermute x3, starting transfers between devices, crossed(): lax.ppermute(value, 'head', [(i, i ^ mask) for i in range(lax.axis_size('...  4.72 us
    ppermute x1, starting transfers between devices, paired_body(): kv_3 = lax.ppermute(kv_0, 'seq', both)  3.79 us
    ppermute x1, waiting for transfers between devices, paired_body(): kv_1 = lax.ppermute(kv_0, 'seq', first)  2.34 us
    ppermute x1, starting transfers between devices, paired_body(): weight_1 = lax.ppermute(after(weight, kv_0), 'seq', first)  1.99 us
    ppermute x1, waiting for transfers between devices, paired_body(): weight_1 = lax.ppermute(after(weight, kv_0), 'seq', first)  1.75 us
    pallas_call x1, Pallas kernels, paired_body(): call(functools.partial(attn_kernel, rows, opt), pltpu.VMEM((2 * (rows + o...  1.72 us
  transfers between devices with their start and end apart: 16, of which 10 were waited for; matrix products, arithmetic and copies ran while one was open for 0% of the time, Pallas kernels for 12%

profile of v5, /device:TPU:0, one launch (start us, length us, event | category | flops | bytes accessed | tf_op | source)
XLA Modules:
  0.0 47.5 jit_solution(2678185060011659808)
XLA Ops:
  0.6 0.5 %collective-permute-start = (bf16[128,256]{1,0:T(8,128)(2,1)}, bf16[128,256]{1,0:T(8,128)(2,1)S(1)}, u32[]{:S(2)}, u32[]{:S(2)}) collective-permute-start(bf16[128,256]{1,0:T(8,128)(2,1)} %k.1), channel_id=1, source_target_pairs={{0,4},{4,0},{8,12},{12,8},{16,20},{20,16},{24,28},{28,24},{1,5},{5... | collective-permute-start | bytes 196616 | tf_op jit(solution)/shard_map/ppermute | solution.py:398
  1.1 0.1 collective-permute-start.1
  1.2 1.1 %shard_map.130 = (bf16[384,256]{1,0:T(8,128)(2,1)S(1)}, bf16[256,256]{1,0:T(8,128)(2,1)S(1)}) custom-call(bf16[128,512]{1,0:T(8,128)(2,1)} %q.1, bf16[128,256]{1,0:T(8,128)(2,1)} %k.1, bf16[128,256]{1,0:T(8,128)(2,1)} %v.1, bf16[1,64,512]{2,1,0:T(8,128)(2,1)} %oq.1, bf16[1,64,256]{2,1,0:T(8,128)(2,1)} %ok.1, bf16[1,64,256]{2,1,0:T(8,128)(2,1)} %ov.1), custom_call_target="tpu_custom_call" | custom-call | tf_op jit(solution)/shard_map/pallas_call | solution.py:400
  2.3 0.0 collective-permute-done.k
  2.3 0.3 collective-permute-done.1.v
  2.6 0.2 collective-permute-start.6
  2.9 3.8 %collective-permute-start.3 = (bf16[256,256]{1,0:T(8,128)(2,1)S(1)}, bf16[256,256]{1,0:T(8,128)(2,1)S(1)}, u32[]{:S(2)}, u32[]{:S(2)}) collective-permute-start(bf16[256,256]{1,0:T(8,128)(2,1)S(1)} %shard_map.131.kv0), channel_id=1, source_target_pairs={{0,24},{4,28},{8,16},{12,20},{16,8},{20,12},{24,0},{28,4},{1,25},{... | collective-permute-start | bytes 393224 | tf_op jit(solution)/shard_map/ppermute | solution.py:409
  6.7 0.5 %collective-permute-start.4 = (bf16[256,256]{1,0:T(8,128)(2,1)S(1)}, bf16[256,256]{1,0:T(8,128)(2,1)S(1)}, u32[]{:S(2)}, u32[]{:S(2)}) collective-permute-start(bf16[256,256]{1,0:T(8,128)(2,1)S(1)} %shard_map.131.kv0), channel_id=1, source_target_pairs={{0,16},{4,12},{8,24},{12,4},{16,0},{20,28},{24,8},{28,20},{1,17},{... | collective-permute-start | bytes 393224 | tf_op jit(solution)/shard_map/ppermute | solution.py:410
  7.2 0.1 collective-permute-start.5
  7.2 0.0 copy-start.3
  7.2 2.0 %collective-permute-start.2 = (bf16[1344,256]{1,0:T(8,128)(2,1)}, bf16[1344,256]{1,0:T(8,128)(2,1)S(1)}, u32[]{:S(2)}, u32[]{:S(2)}) collective-permute-start(bf16[1344,256]{1,0:T(8,128)(2,1)} %bitcast.4), channel_id=1, source_target_pairs={{0,16},{4,12},{8,24},{12,4},{16,0},{20,28},{24,8},{28,20},{1,17},{... | collective-permute-start | bytes 2064392 | tf_op jit(solution)/shard_map/ppermute | solution.py:424
  9.2 0.0 collective-permute-done.6.received
  9.2 1.7 %collective-permute-done.3.kv3 = bf16[256,256]{1,0:T(8,128)(2,1)S(1)} collective-permute-done((bf16[256,256]{1,0:T(8,128)(2,1)S(1)}, bf16[256,256]{1,0:T(8,128)(2,1)S(1)}, u32[]{:S(2)}, u32[]{:S(2)}) %collective-permute-start.3) | collective-permute-done | bytes 131104 | tf_op jit(solution)/shard_map/ppermute | solution.py:409
  10.9 2.3 %collective-permute-done.4.kv1 = bf16[256,256]{1,0:T(8,128)(2,1)S(1)} collective-permute-done((bf16[256,256]{1,0:T(8,128)(2,1)S(1)}, bf16[256,256]{1,0:T(8,128)(2,1)S(1)}, u32[]{:S(2)}, u32[]{:S(2)}) %collective-permute-start.4) | collective-permute-done | bytes 131104 | tf_op jit(solution)/shard_map/ppermute | solution.py:410
  13.3 1.1 %collective-permute-done.5.kv2 = bf16[256,256]{1,0:T(8,128)(2,1)S(1)} collective-permute-done((bf16[256,256]{1,0:T(8,128)(2,1)S(1)}, bf16[256,256]{1,0:T(8,128)(2,1)S(1)}, u32[]{:S(2)}, u32[]{:S(2)}) %collective-permute-start.5) | collective-permute-done | bytes 131104 | tf_op jit(solution)/shard_map/ppermute | solution.py:411
  14.3 1.7 %shard_map.132.a0 = bf16[384,256]{1,0:T(8,128)(2,1)S(1)} custom-call(bf16[256,256]{1,0:T(8,128)(2,1)S(1)} %shard_map.131.kv0, bf16[256,256]{1,0:T(8,128)(2,1)S(1)} %collective-permute-done.3.kv3, bf16[256,256]{1,0:T(8,128)(2,1)S(1)} %collective-permute-done.4.kv1, bf16[256,256]{1,0:T(8,128)(2,1)S(1)} %collective-permute-done.5.kv2, ...), custom_call_target="tpu_custom_call" | custom-call | flops 40265318400 | tf_op jit(solution)/shard_map/pallas_call | solution.py:414
  16.1 0.0 copy-done.3
  16.1 1.6 %collective-permute-start.8 = (bf16[1344,256]{1,0:T(8,128)(2,1)S(1)}, bf16[1344,256]{1,0:T(8,128)(2,1)S(1)}, u32[]{:S(2)}, u32[]{:S(2)}) collective-permute-start(bf16[1344,256]{1,0:T(8,128)(2,1)S(1)} %bitcast.5), channel_id=1, source_target_pairs={{0,8},{4,20},{8,0},{12,28},{16,24},{20,4},{24,16},{28,12},{1,9},{5... | collective-permute-start | bytes 2064392 | tf_op jit(solution)/shard_map/ppermute | solution.py:425
  17.7 2.6 %collective-permute-start.10 = (bf16[384,256]{1,0:T(8,128)(2,1)S(1)}, bf16[384,256]{1,0:T(8,128)(2,1)S(1)}, u32[]{:S(2)}, u32[]{:S(2)}) collective-permute-start(bf16[384,256]{1,0:T(8,128)(2,1)S(1)} %shard_map.132.a0), channel_id=1, source_target_pairs={{0,2},{1,3},{2,0},{3,1},{4,6},{5,7},{6,4},{7,5},{8,10},{9,11},{10,... | collective-permute-start | bytes 589832 | tf_op jit(solution)/shard_map/ppermute | solution.py:394
  20.2 1.6 %collective-permute-start.9 = (bf16[384,256]{1,0:T(8,128)(2,1)S(1)}, bf16[384,256]{1,0:T(8,128)(2,1)S(1)}, u32[]{:S(2)}, u32[]{:S(2)}) collective-permute-start(bf16[384,256]{1,0:T(8,128)(2,1)S(1)} %shard_map.132.a0), channel_id=1, source_target_pairs={{0,1},{1,0},{2,3},{3,2},{4,5},{5,4},{6,7},{7,6},{8,9},{9,8},{10,11... | collective-permute-start | bytes 589832 | tf_op jit(solution)/shard_map/ppermute | solution.py:394
  21.8 1.8 %collective-permute-done.2.w1 = bf16[1344,256]{1,0:T(8,128)(2,1)S(1)} collective-permute-done((bf16[1344,256]{1,0:T(8,128)(2,1)}, bf16[1344,256]{1,0:T(8,128)(2,1)S(1)}, u32[]{:S(2)}, u32[]{:S(2)}) %collective-permute-start.2) | collective-permute-done | bytes 688160 | tf_op jit(solution)/shard_map/ppermute | solution.py:424
  23.5 1.6 %collective-permute-start.7 = (bf16[1344,256]{1,0:T(8,128)(2,1)S(1)}, bf16[1344,256]{1,0:T(8,128)(2,1)S(1)}, u32[]{:S(2)}, u32[]{:S(2)}) collective-permute-start(bf16[1344,256]{1,0:T(8,128)(2,1)S(1)} %collective-permute-done.2.w1), channel_id=1, source_target_pairs={{0,8},{4,20},{8,0},{12,28},{16,24},{20,4},{24,16},{28,12},{1,9},{5... | collective-permute-start | bytes 2064392 | tf_op jit(solution)/shard_map/ppermute | solution.py:426
  25.1 3.4 %collective-permute-done.10.a2 = bf16[384,256]{1,0:T(8,128)(2,1)S(1)} collective-permute-done((bf16[384,256]{1,0:T(8,128)(2,1)S(1)}, bf16[384,256]{1,0:T(8,128)(2,1)S(1)}, u32[]{:S(2)}, u32[]{:S(2)}) %collective-permute-start.10) | collective-permute-done | bytes 196640 | tf_op jit(solution)/shard_map/ppermute | solution.py:394
  28.6 0.6 %collective-permute-start.11 = (bf16[384,256]{1,0:T(8,128)(2,1)S(1)}, bf16[384,256]{1,0:T(8,128)(2,1)S(1)}, u32[]{:S(2)}, u32[]{:S(2)}) collective-permute-start(bf16[384,256]{1,0:T(8,128)(2,1)S(1)} %collective-permute-done.10.a2), channel_id=1, source_target_pairs={{0,1},{1,0},{2,3},{3,2},{4,5},{5,4},{6,7},{7,6},{8,9},{9,8},{10,11... | collective-permute-start | bytes 589832 | tf_op jit(solution)/shard_map/ppermute | solution.py:394
  29.1 0.0 collective-permute-done.9.a1
  29.1 0.0 collective-permute-done.8.w2
  29.1 1.3 %shard_map.133 = (f32[1344,192]{1,0:T(8,128)S(1)}, f32[1344,192]{1,0:T(8,128)S(1)}, bf16[1344,256]{1,0:T(8,128)(2,1)S(1)}) custom-call(bf16[1344,256]{1,0:T(8,128)(2,1)S(1)} %bitcast.6, bf16[1344,256]{1,0:T(8,128)(2,1)S(1)} %collective-permute-done.2.w1, bf16[1344,256]{1,0:T(8,128)(2,1)S(1)} %collective-permute-done.8.w2, ...), custom_call_target="tpu_custom_call" | custom-call | flops 6341787648 | tf_op jit(solution)/shard_map/pallas_call | solution.py:428
  30.5 3.7 %collective-permute-done.11.a3 = bf16[384,256]{1,0:T(8,128)(2,1)S(1)} collective-permute-done((bf16[384,256]{1,0:T(8,128)(2,1)S(1)}, bf16[384,256]{1,0:T(8,128)(2,1)S(1)}, u32[]{:S(2)}, u32[]{:S(2)}) %collective-permute-start.11) | collective-permute-done | bytes 196640 | tf_op jit(solution)/shard_map/ppermute | solution.py:394
  34.2 1.4 %collective-permute-done.7.w3 = bf16[1344,256]{1,0:T(8,128)(2,1)S(1)} collective-permute-done((bf16[1344,256]{1,0:T(8,128)(2,1)S(1)}, bf16[1344,256]{1,0:T(8,128)(2,1)S(1)}, u32[]{:S(2)}, u32[]{:S(2)}) %collective-permute-start.7) | collective-permute-done | bytes 688160 | tf_op jit(solution)/shard_map/ppermute | solution.py:426
  35.7 0.6 %shard_map.135 = bf16[2016,128]{1,0:T(8,128)(2,1)S(1)} custom-call(bf16[1344,256]{1,0:T(8,128)(2,1)S(1)} %collective-permute-done.7.w3, bf16[1344,256]{1,0:T(8,128)(2,1)S(1)} %get-tuple-element.27.chosen, bf16[384,256]{1,0:T(8,128)(2,1)S(1)} %shard_map.132.a0, bf16[384,256]{1,0:T(8,128)(2,1)S(1)} %collective-permute-done.9.a1, ...), custom_call_target="tpu_custom_call" | custom-call | flops 132120576 | tf_op jit(solution)/shard_map/pallas_call | solution.py:438
  36.3 0.1 collective-permute-start.12
  36.4 0.5 %shard_map.134.own = f32[1344,192]{1,0:T(8,128)S(1)} custom-call(bf16[1344,256]{1,0:T(8,128)(2,1)S(1)} %collective-permute-done.7.w3, bf16[1344,256]{1,0:T(8,128)(2,1)S(1)} %get-tuple-element.27.chosen, bf16[384,256]{1,0:T(8,128)(2,1)S(1)} %shard_map.132.a0, bf16[384,256]{1,0:T(8,128)(2,1)S(1)} %collective-permute-done.9.a1, ...), custom_call_target="tpu_custom_call" | custom-call | flops 132120576 | tf_op jit(solution)/shard_map/pallas_call | solution.py:438
  36.9 0.0 copy-start.4
  36.9 0.0 copy-start.2
  37.0 0.0 copy-start
  37.0 0.0 copy-start.1
  37.0 1.3 %collective-permute-done.12.received = bf16[2016,128]{1,0:T(8,128)(2,1)S(1)} collective-permute-done((bf16[2016,128]{1,0:T(8,128)(2,1)S(1)}, bf16[2016,128]{1,0:T(8,128)(2,1)S(1)}, u32[]{:S(2)}, u32[]{:S(2)}) %collective-permute-start.12) | collective-permute-done | bytes 516128 | tf_op jit(solution)/shard_map/ppermute | solution.py:448
  38.3 0.3 shard_map.136
  38.6 1.6 %collective-permute-start.13 = (f32[1,192]{1,0:T(1,128)S(1)}, f32[1,192]{1,0:T(1,128)S(1)}, u32[]{:S(2)}, u32[]{:S(2)}) collective-permute-start(f32[1,192]{1,0:T(1,128)S(1)} %get-tuple-element.35.s0), channel_id=1, source_target_pairs={{0,1},{1,2},{2,3},{3,0},{4,5},{5,6},{6,7},{7,4},{8,9},{9,10},{10,1... | collective-permute-start | bytes 2312 | tf_op jit(solution)/shard_map/ppermute | solution.py:385
  40.2 2.6 %collective-permute-start.14 = (f32[1,192]{1,0:T(1,128)S(1)}, f32[1,192]{1,0:T(1,128)S(1)}, u32[]{:S(2)}, u32[]{:S(2)}) collective-permute-start(f32[1,192]{1,0:T(1,128)S(1)} %get-tuple-element.35.s0), channel_id=1, source_target_pairs={{0,2},{1,3},{2,0},{3,1},{4,6},{5,7},{6,4},{7,5},{8,10},{9,11},{10,... | collective-permute-start | bytes 2312 | tf_op jit(solution)/shard_map/ppermute | solution.py:385
  42.8 1.4 %collective-permute-start.15 = (f32[1,192]{1,0:T(1,128)S(1)}, f32[1,192]{1,0:T(1,128)S(1)}, u32[]{:S(2)}, u32[]{:S(2)}) collective-permute-start(f32[1,192]{1,0:T(1,128)S(1)} %get-tuple-element.35.s0), channel_id=1, source_target_pairs={{0,3},{1,0},{2,1},{3,2},{4,7},{5,4},{6,5},{7,6},{8,11},{9,8},{10,9... | collective-permute-start | bytes 2312 | tf_op jit(solution)/shard_map/ppermute | solution.py:385
  44.1 0.0 copy-done.4
  44.1 0.0 copy-done.2
  44.1 1.0 %shard_map.137 = (f32[1344,128]{1,0:T(8,128)S(1)}, f32[64,1344]{1,0:T(8,128)S(1)}, f32[64,128]{1,0:T(8,128)S(1)}, f32[64,128]{1,0:T(8,128)S(1)}) custom-call(s32[1,2]{1,0:T(1,128)S(1)} %copy-done.2, f32[1344,192]{1,0:T(8,128)S(1)} %get-tuple-element.30.projected, f32[1,1344]{1,0:T(1,128)S(1)} %broadcast_in_dim.3.gain), custom_call_target="tpu_custom_call" | custom-call | tf_op jit(solution)/shard_map/pallas_call | solution.py:455
  45.1 0.0 collective-permute-done.13.s1
  45.1 0.0 collective-permute-done.14.s2
  45.1 1.2 %collective-permute-done.15.s3 = f32[1,192]{1,0:T(1,128)S(1)} collective-permute-done((f32[1,192]{1,0:T(1,128)S(1)}, f32[1,192]{1,0:T(1,128)S(1)}, u32[]{:S(2)}, u32[]{:S(2)}) %collective-permute-start.15) | collective-permute-done | bytes 800 | tf_op jit(solution)/shard_map/ppermute | solution.py:385
  46.3 0.0 copy-done
  46.3 0.0 copy-done.1
  46.3 1.2 %shard_map.138 = (bf16[1344,128]{1,0:T(8,128)(2,1)}, bf16[1,64,1344]{2,1,0:T(8,128)(2,1)}, f32[1,1344]{1,0:T(1,128)}) custom-call(f32[1344,128]{1,0:T(8,128)S(1)} %get-tuple-element.31.prefix, f32[64,1344]{1,0:T(8,128)S(1)} %get-tuple-element.32.option, f32[64,128]{1,0:T(8,128)S(1)} %get-tuple-element.33.kept, f32[64,128]{1,0:T(8,128)S(1)} %get-tuple-element.34.share, ...), custom_call_target="tpu_custom_call" | custom-call | tf_op jit(solution)/shard_map/pallas_call | solution.py:467
  (2 shorter events, 0.0 us)
Async XLA Ops:
  0.6 1.7 %collective-permute-start = (bf16[128,256]{1,0:T(8,128)(2,1)}, bf16[128,256]{1,0:T(8,128)(2,1)S(1)}, u32[]{:S(2)}, u32[]{:S(2)}) collective-permute-start(bf16[128,256]{1,0:T(8,128)(2,1)} %k.1), channel_id=1, source_target_pairs={{0,4},{4,0},{8,12},{12,8},{16,20},{20,16},{24,28},{28,24},{1,5},{5... | collective-permute-start | bytes 196616 | tf_op jit(solution)/shard_map/ppermute | solution.py:398
  1.1 1.5 %collective-permute-start.1 = (bf16[128,256]{1,0:T(8,128)(2,1)}, bf16[128,256]{1,0:T(8,128)(2,1)S(1)}, u32[]{:S(2)}, u32[]{:S(2)}) collective-permute-start(bf16[128,256]{1,0:T(8,128)(2,1)} %v.1), channel_id=1, source_target_pairs={{0,4},{4,0},{8,12},{12,8},{16,20},{20,16},{24,28},{28,24},{1,5},{5... | collective-permute-start | bytes 196616 | tf_op jit(solution)/shard_map/ppermute | solution.py:399
  2.6 6.6 %collective-permute-start.6 = (bf16[256,256]{1,0:T(8,128)(2,1)S(1)}, bf16[256,256]{1,0:T(8,128)(2,1)S(1)}, u32[]{:S(2)}, u32[]{:S(2)}) collective-permute-start(bf16[256,256]{1,0:T(8,128)(2,1)S(1)} %get-tuple-element.24), channel_id=1, source_target_pairs={{0,4},{4,0},{8,12},{12,8},{16,20},{20,16},{24,28},{28,24},{1,5},{5... | collective-permute-start | bytes 393224 | tf_op jit(solution)/shard_map/ppermute | solution.py:408
  2.9 8.1 %collective-permute-start.3 = (bf16[256,256]{1,0:T(8,128)(2,1)S(1)}, bf16[256,256]{1,0:T(8,128)(2,1)S(1)}, u32[]{:S(2)}, u32[]{:S(2)}) collective-permute-start(bf16[256,256]{1,0:T(8,128)(2,1)S(1)} %shard_map.131.kv0), channel_id=1, source_target_pairs={{0,24},{4,28},{8,16},{12,20},{16,8},{20,12},{24,0},{28,4},{1,25},{... | collective-permute-start | bytes 393224 | tf_op jit(solution)/shard_map/ppermute | solution.py:409
  6.7 6.6 %collective-permute-start.4 = (bf16[256,256]{1,0:T(8,128)(2,1)S(1)}, bf16[256,256]{1,0:T(8,128)(2,1)S(1)}, u32[]{:S(2)}, u32[]{:S(2)}) collective-permute-start(bf16[256,256]{1,0:T(8,128)(2,1)S(1)} %shard_map.131.kv0), channel_id=1, source_target_pairs={{0,16},{4,12},{8,24},{12,4},{16,0},{20,28},{24,8},{28,20},{1,17},{... | collective-permute-start | bytes 393224 | tf_op jit(solution)/shard_map/ppermute | solution.py:410
  7.2 7.2 %collective-permute-start.5 = (bf16[256,256]{1,0:T(8,128)(2,1)S(1)}, bf16[256,256]{1,0:T(8,128)(2,1)S(1)}, u32[]{:S(2)}, u32[]{:S(2)}) collective-permute-start(bf16[256,256]{1,0:T(8,128)(2,1)S(1)} %shard_map.131.kv0), channel_id=1, source_target_pairs={{0,8},{4,20},{8,0},{12,28},{16,24},{20,4},{24,16},{28,12},{1,9},{5... | collective-permute-start | bytes 393224 | tf_op jit(solution)/shard_map/ppermute | solution.py:411
  7.2 8.9 %copy-start.3 = (bf16[256,1344]{0,1:T(8,128)(2,1)S(1)}, bf16[256,1344]{0,1:T(8,128)(2,1)}, u32[]{:S(2)}) copy-start(bf16[256,1344]{0,1:T(8,128)(2,1)} %param.19) | copy-start | bytes 2064388
  7.2 16.3 %collective-permute-start.2 = (bf16[1344,256]{1,0:T(8,128)(2,1)}, bf16[1344,256]{1,0:T(8,128)(2,1)S(1)}, u32[]{:S(2)}, u32[]{:S(2)}) collective-permute-start(bf16[1344,256]{1,0:T(8,128)(2,1)} %bitcast.4), channel_id=1, source_target_pairs={{0,16},{4,12},{8,24},{12,4},{16,0},{20,28},{24,8},{28,20},{1,17},{... | collective-permute-start | bytes 2064392 | tf_op jit(solution)/shard_map/ppermute | solution.py:424
  16.1 13.1 %collective-permute-start.8 = (bf16[1344,256]{1,0:T(8,128)(2,1)S(1)}, bf16[1344,256]{1,0:T(8,128)(2,1)S(1)}, u32[]{:S(2)}, u32[]{:S(2)}) collective-permute-start(bf16[1344,256]{1,0:T(8,128)(2,1)S(1)} %bitcast.5), channel_id=1, source_target_pairs={{0,8},{4,20},{8,0},{12,28},{16,24},{20,4},{24,16},{28,12},{1,9},{5... | collective-permute-start | bytes 2064392 | tf_op jit(solution)/shard_map/ppermute | solution.py:425
  17.7 10.9 %collective-permute-start.10 = (bf16[384,256]{1,0:T(8,128)(2,1)S(1)}, bf16[384,256]{1,0:T(8,128)(2,1)S(1)}, u32[]{:S(2)}, u32[]{:S(2)}) collective-permute-start(bf16[384,256]{1,0:T(8,128)(2,1)S(1)} %shard_map.132.a0), channel_id=1, source_target_pairs={{0,2},{1,3},{2,0},{3,1},{4,6},{5,7},{6,4},{7,5},{8,10},{9,11},{10,... | collective-permute-start | bytes 589832 | tf_op jit(solution)/shard_map/ppermute | solution.py:394
  20.2 8.9 %collective-permute-start.9 = (bf16[384,256]{1,0:T(8,128)(2,1)S(1)}, bf16[384,256]{1,0:T(8,128)(2,1)S(1)}, u32[]{:S(2)}, u32[]{:S(2)}) collective-permute-start(bf16[384,256]{1,0:T(8,128)(2,1)S(1)} %shard_map.132.a0), channel_id=1, source_target_pairs={{0,1},{1,0},{2,3},{3,2},{4,5},{5,4},{6,7},{7,6},{8,9},{9,8},{10,11... | collective-permute-start | bytes 589832 | tf_op jit(solution)/shard_map/ppermute | solution.py:394
  23.5 12.1 %collective-permute-start.7 = (bf16[1344,256]{1,0:T(8,128)(2,1)S(1)}, bf16[1344,256]{1,0:T(8,128)(2,1)S(1)}, u32[]{:S(2)}, u32[]{:S(2)}) collective-permute-start(bf16[1344,256]{1,0:T(8,128)(2,1)S(1)} %collective-permute-done.2.w1), channel_id=1, source_target_pairs={{0,8},{4,20},{8,0},{12,28},{16,24},{20,4},{24,16},{28,12},{1,9},{5... | collective-permute-start | bytes 2064392 | tf_op jit(solution)/shard_map/ppermute | solution.py:426
  28.6 5.7 %collective-permute-start.11 = (bf16[384,256]{1,0:T(8,128)(2,1)S(1)}, bf16[384,256]{1,0:T(8,128)(2,1)S(1)}, u32[]{:S(2)}, u32[]{:S(2)}) collective-permute-start(bf16[384,256]{1,0:T(8,128)(2,1)S(1)} %collective-permute-done.10.a2), channel_id=1, source_target_pairs={{0,1},{1,0},{2,3},{3,2},{4,5},{5,4},{6,7},{7,6},{8,9},{9,8},{10,11... | collective-permute-start | bytes 589832 | tf_op jit(solution)/shard_map/ppermute | solution.py:394
  36.3 2.0 %collective-permute-start.12 = (bf16[2016,128]{1,0:T(8,128)(2,1)S(1)}, bf16[2016,128]{1,0:T(8,128)(2,1)S(1)}, u32[]{:S(2)}, u32[]{:S(2)}) collective-permute-start(bf16[2016,128]{1,0:T(8,128)(2,1)S(1)} %shard_map.135), channel_id=1, source_target_pairs={{0,4},{4,0},{8,12},{12,8},{16,20},{20,16},{24,28},{28,24},{1,5},{5... | collective-permute-start | bytes 1548296 | tf_op jit(solution)/shard_map/ppermute | solution.py:448
  36.9 7.2 %copy-start.4 = (f32[1344]{0:T(1024)S(1)}, f32[1344]{0:T(1024)}, u32[]{:S(2)}) copy-start(f32[1344]{0:T(1024)} %param.20) | copy-start | bytes 16132
  36.9 7.2 %copy-start.2 = (s32[1,2]{1,0:T(1,128)S(1)}, s32[1,2]{1,0:T(1,128)}, u32[]{:S(2)}) copy-start(s32[1,2]{1,0:T(1,128)} %bounds.1) | copy-start | bytes 28
  37.0 9.4 %copy-start = (bf16[128,1344]{0,1:T(8,128)(2,1)S(1)}, bf16[128,1344]{0,1:T(8,128)(2,1)}, u32[]{:S(2)}) copy-start(bf16[128,1344]{0,1:T(8,128)(2,1)} %param.14) | copy-start | bytes 1032196
  37.0 9.4 %copy-start.1 = (bf16[1,64,1344]{2,1,0:T(8,128)(2,1)S(1)}, bf16[1,64,1344]{2,1,0:T(8,128)(2,1)}, u32[]{:S(2)}) copy-start(bf16[1,64,1344]{2,1,0:T(8,128)(2,1)} %opt_resid.1) | copy-start | bytes 516100
  38.6 6.5 %collective-permute-start.13 = (f32[1,192]{1,0:T(1,128)S(1)}, f32[1,192]{1,0:T(1,128)S(1)}, u32[]{:S(2)}, u32[]{:S(2)}) collective-permute-start(f32[1,192]{1,0:T(1,128)S(1)} %get-tuple-element.35.s0), channel_id=1, source_target_pairs={{0,1},{1,2},{2,3},{3,0},{4,5},{5,6},{6,7},{7,4},{8,9},{9,10},{10,1... | collective-permute-start | bytes 2312 | tf_op jit(solution)/shard_map/ppermute | solution.py:385
  40.2 4.9 %collective-permute-start.14 = (f32[1,192]{1,0:T(1,128)S(1)}, f32[1,192]{1,0:T(1,128)S(1)}, u32[]{:S(2)}, u32[]{:S(2)}) collective-permute-start(f32[1,192]{1,0:T(1,128)S(1)} %get-tuple-element.35.s0), channel_id=1, source_target_pairs={{0,2},{1,3},{2,0},{3,1},{4,6},{5,7},{6,4},{7,5},{8,10},{9,11},{10,... | collective-permute-start | bytes 2312 | tf_op jit(solution)/shard_map/ppermute | solution.py:385
  42.8 3.6 %collective-permute-start.15 = (f32[1,192]{1,0:T(1,128)S(1)}, f32[1,192]{1,0:T(1,128)S(1)}, u32[]{:S(2)}, u32[]{:S(2)}) collective-permute-start(f32[1,192]{1,0:T(1,128)S(1)} %get-tuple-element.35.s0), channel_id=1, source_target_pairs={{0,3},{1,0},{2,1},{3,2},{4,7},{5,4},{6,5},{7,6},{8,11},{9,8},{10,9... | collective-permute-start | bytes 2312 | tf_op jit(solution)/shard_map/ppermute | solution.py:385

commit v6 on v5

--- a/solution.py
+++ b/solution.py
@@ -125,7 +125,7 @@
     return (prefix_out, option_out[None], option_summary[None])
 
 
-ATTENTION_COST, PROJECTION_COST = 200, 8
+ATTENTION_COST, PROJECTION_COST = 200, 5
 
 
 SMEM = pltpu.MemorySpace.SMEM
@@ -255,19 +255,10 @@
     return [((s ^ mask) >> 1) ^ z for mask in masks(s)]
 
 
-def project_kernel(w0, w1, w2, a0, a1, a2, pair_out, own_out, chosen, placed):
-    for t, block in enumerate((a0, a1, a2)):
+def project_kernel(w0, w1, w2, a0, a1, a2, a3, pair_out, own_out, placed):
+    for t, block in enumerate((a0, a1, a2, a3)):
         placed[t] = block[...]
-    placed[3] = jnp.zeros_like(a0)
     meets = apart()
-    held = (w0, w1, w2)
-    chosen[...] = w0[...]
-    for j in (1, 2):
-
-        @pl.when(meets[j] == 3)
-        def _():
-            chosen[...] = held[j][...]
-
     count = a0.shape[0] // 2
     middle = w0.shape[0] // 2
     for r, out in enumerate((pair_out, own_out)):
@@ -278,19 +269,16 @@
             out[part, :] = total + dot_nt(w2[part, :], blocks[2])
 
 
-def complete_kernel(rows, opt, packed, w3, chosen, a0, a1, a2, a3, partial, out, placed):
+def complete_kernel(rows, opt, packed, w3, a0, a1, a2, a3, partial, out, placed):
     mine = slice(0, rows + opt) if packed else slice(rows + opt, 2 * (rows + opt))
     for t, block in enumerate((a0, a1, a2, a3)):
         placed[t] = block[mine, :]
-    meets = apart()[3]
-    first = placed[meets]
-    second = jnp.where(meets == 3, jnp.zeros_like(first), placed[3])
+    block = placed[apart()[3]]
     features = w3.shape[0]
     half = features // 2
     for n in range(2):
         part = slice(n * half, (n + 1) * half)
-        total = dot_nt(w3[part, :], first) + dot_nt(chosen[part, :], second)
-        total += partial[part, :]
+        total = partial[part, :] + dot_nt(w3[part, :], block)
         if packed:
             total = total.astype(out.dtype)
             out[part, :] = total[:, 0:rows]
@@ -425,24 +413,24 @@
     weight_2 = lax.ppermute(after(weight, block), "seq", second)
     weight_3 = lax.ppermute(after(weight_1, block), "seq", second)
     flops = 4 * features * wide * (rows + opt)
-    pair_part, own_part, chosen = call(
+    pair_part, own_part = call(
         project_kernel,
-        [shape((features, rows + opt), f32)] * 2 + [shape((features, wide), bf16)],
-        6,
+        [shape((features, rows + opt), f32)] * 2,
+        7,
         flops=PROJECTION_COST * 3 * flops,
         scratch=[pltpu.VMEM((4, 2 * (rows + opt), wide), bf16)],
         vmem=16,
-    )(weight, weight_1, weight_2, *blocks[:3])
+    )(weight, weight_1, weight_2, *blocks)
 
     def complete(partial, out_shape, packed):
         return call(
             functools.partial(complete_kernel, rows, opt, packed),
             out_shape,
-            7,
+            6,
             flops=flops // 2,
             scratch=[pltpu.VMEM((4, rows + opt, wide), bf16)],
             vmem=16,
-        )(weight_3, chosen, *blocks, partial)
+        )(weight_3, *blocks, partial)
 
     half = complete(pair_part, shape((features + features // 2, rows), bf16), True)
     received = lax.ppermute(half, "seq", pair)

time: 47.7 us -> 50 us (1.048)
  waiting for transfers between devices: 18.3 us -> 21.3 us
    ppermute x3, waiting for transfers between devices: 7.18 us -> 8.98 us  [crossed(): lax.ppermute(value, 'head', [(i, i ^ mask) for i in range(lax.axis_size('...]
    ppermute x1, waiting for transfers between devices: 1.75 us -> 3.33 us  [paired_body(): weight_1 = lax.ppermute(after(weight, kv_0), 'seq', first)]
    ppermute x1, waiting for transfers between devices: 1.45 us -> 0.01 us  [paired_body(): weight_3 = lax.ppermute(after(weight_1, block), 'seq', second)]
    ppermute x3, waiting for transfers between devices: 1.22 us -> 2.13 us  [turned(): lax.ppermute(value, 'head', [(i, (i + steps) % count) for i in range(coun...]
  transfers between devices with their start and end apart: 16 -> 16, of which waited for: 10 -> 11; matrix products, arithmetic and copies ran while one was open for 0% -> 0% of each run, Pallas kernels for 12% -> 11%
where the time goes in v6:
time: 50 us; the launch traced here: 49.8 us
  waiting for transfers between devices  21.3 us (43%)
  starting transfers between devices  20.3 us (41%)
  Pallas kernels  7.39 us (15%)
  between operations  0.76 us (2%)
    ppermute x3, waiting for transfers between devices, crossed(): lax.ppermute(value, 'head', [(i, i ^ mask) for i in range(lax.axis_size('...  8.98 us
    ppermute x3, starting transfers between devices, turned(): lax.ppermute(value, 'head', [(i, (i + steps) % count) for i in range(coun...  5.14 us
    ppermute x3, starting transfers between devices, crossed(): lax.ppermute(value, 'head', [(i, i ^ mask) for i in range(lax.axis_size('...  4.76 us
    ppermute x1, starting transfers between devices, paired_body(): kv_3 = lax.ppermute(kv_0, 'seq', both)  3.79 us
    ppermute x1, waiting for transfers between devices, paired_body(): weight_1 = lax.ppermute(after(weight, kv_0), 'seq', first)  3.33 us
    ppermute x1, waiting for transfers between devices, paired_body(): kv_1 = lax.ppermute(kv_0, 'seq', first)  2.34 us
    ppermute x3, waiting for transfers between devices, turned(): lax.ppermute(value, 'head', [(i, (i + steps) % count) for i in range(coun...  2.13 us
    ppermute x1, starting transfers between devices, paired_body(): weight_1 = lax.ppermute(after(weight, kv_0), 'seq', first)  1.99 us
  transfers between devices with their start and end apart: 16, of which 11 were waited for; matrix products, arithmetic and copies ran while one was open for 0% of the time, Pallas kernels for 11%

profile of v6, /device:TPU:0, one launch (start us, length us, event | category | flops | bytes accessed | tf_op | source)
XLA Modules:
  0.0 49.8 jit_solution(11276117074035410494)
XLA Ops:
  0.6 0.5 %collective-permute-start = (bf16[128,256]{1,0:T(8,128)(2,1)}, bf16[128,256]{1,0:T(8,128)(2,1)S(1)}, u32[]{:S(2)}, u32[]{:S(2)}) collective-permute-start(bf16[128,256]{1,0:T(8,128)(2,1)} %k.1), channel_id=1, source_target_pairs={{0,4},{4,0},{8,12},{12,8},{16,20},{20,16},{24,28},{28,24},{1,5},{5... | collective-permute-start | bytes 196616 | tf_op jit(solution)/shard_map/ppermute | solution.py:386
  1.1 0.1 collective-permute-start.1
  1.2 1.1 %shard_map.130 = (bf16[384,256]{1,0:T(8,128)(2,1)S(1)}, bf16[256,256]{1,0:T(8,128)(2,1)S(1)}) custom-call(bf16[128,512]{1,0:T(8,128)(2,1)} %q.1, bf16[128,256]{1,0:T(8,128)(2,1)} %k.1, bf16[128,256]{1,0:T(8,128)(2,1)} %v.1, bf16[1,64,512]{2,1,0:T(8,128)(2,1)} %oq.1, bf16[1,64,256]{2,1,0:T(8,128)(2,1)} %ok.1, bf16[1,64,256]{2,1,0:T(8,128)(2,1)} %ov.1), custom_call_target="tpu_custom_call" | custom-call | tf_op jit(solution)/shard_map/pallas_call | solution.py:388
  2.3 0.0 collective-permute-done.k
  2.3 0.3 collective-permute-done.1.v
  2.6 0.2 collective-permute-start.6
  2.9 3.8 %collective-permute-start.3 = (bf16[256,256]{1,0:T(8,128)(2,1)S(1)}, bf16[256,256]{1,0:T(8,128)(2,1)S(1)}, u32[]{:S(2)}, u32[]{:S(2)}) collective-permute-start(bf16[256,256]{1,0:T(8,128)(2,1)S(1)} %shard_map.131.kv0), channel_id=1, source_target_pairs={{0,24},{4,28},{8,16},{12,20},{16,8},{20,12},{24,0},{28,4},{1,25},{... | collective-permute-start | bytes 393224 | tf_op jit(solution)/shard_map/ppermute | solution.py:397
  6.7 0.5 %collective-permute-start.4 = (bf16[256,256]{1,0:T(8,128)(2,1)S(1)}, bf16[256,256]{1,0:T(8,128)(2,1)S(1)}, u32[]{:S(2)}, u32[]{:S(2)}) collective-permute-start(bf16[256,256]{1,0:T(8,128)(2,1)S(1)} %shard_map.131.kv0), channel_id=1, source_target_pairs={{0,16},{4,12},{8,24},{12,4},{16,0},{20,28},{24,8},{28,20},{1,17},{... | collective-permute-start | bytes 393224 | tf_op jit(solution)/shard_map/ppermute | solution.py:398
  7.2 0.1 collective-permute-start.5
  7.2 0.0 copy-start.3
  7.2 2.0 %collective-permute-start.2 = (bf16[1344,256]{1,0:T(8,128)(2,1)}, bf16[1344,256]{1,0:T(8,128)(2,1)S(1)}, u32[]{:S(2)}, u32[]{:S(2)}) collective-permute-start(bf16[1344,256]{1,0:T(8,128)(2,1)} %bitcast.4), channel_id=1, source_target_pairs={{0,16},{4,12},{8,24},{12,4},{16,0},{20,28},{24,8},{28,20},{1,17},{... | collective-permute-start | bytes 2064392 | tf_op jit(solution)/shard_map/ppermute | solution.py:412
  9.2 0.0 collective-permute-done.6.received
  9.2 1.7 %collective-permute-done.3.kv3 = bf16[256,256]{1,0:T(8,128)(2,1)S(1)} collective-permute-done((bf16[256,256]{1,0:T(8,128)(2,1)S(1)}, bf16[256,256]{1,0:T(8,128)(2,1)S(1)}, u32[]{:S(2)}, u32[]{:S(2)}) %collective-permute-start.3) | collective-permute-done | bytes 131104 | tf_op jit(solution)/shard_map/ppermute | solution.py:397
  10.9 2.3 %collective-permute-done.4.kv1 = bf16[256,256]{1,0:T(8,128)(2,1)S(1)} collective-permute-done((bf16[256,256]{1,0:T(8,128)(2,1)S(1)}, bf16[256,256]{1,0:T(8,128)(2,1)S(1)}, u32[]{:S(2)}, u32[]{:S(2)}) %collective-permute-start.4) | collective-permute-done | bytes 131104 | tf_op jit(solution)/shard_map/ppermute | solution.py:398
  13.3 1.1 %collective-permute-done.5.kv2 = bf16[256,256]{1,0:T(8,128)(2,1)S(1)} collective-permute-done((bf16[256,256]{1,0:T(8,128)(2,1)S(1)}, bf16[256,256]{1,0:T(8,128)(2,1)S(1)}, u32[]{:S(2)}, u32[]{:S(2)}) %collective-permute-start.5) | collective-permute-done | bytes 131104 | tf_op jit(solution)/shard_map/ppermute | solution.py:399
  14.3 1.7 %shard_map.132.a0 = bf16[384,256]{1,0:T(8,128)(2,1)S(1)} custom-call(bf16[256,256]{1,0:T(8,128)(2,1)S(1)} %shard_map.131.kv0, bf16[256,256]{1,0:T(8,128)(2,1)S(1)} %collective-permute-done.3.kv3, bf16[256,256]{1,0:T(8,128)(2,1)S(1)} %collective-permute-done.4.kv1, bf16[256,256]{1,0:T(8,128)(2,1)S(1)} %collective-permute-done.5.kv2, ...), custom_call_target="tpu_custom_call" | custom-call | flops 40265318400 | tf_op jit(solution)/shard_map/pallas_call | solution.py:402
  16.1 0.0 copy-done.3
  16.1 1.6 %collective-permute-start.11 = (bf16[1344,256]{1,0:T(8,128)(2,1)S(1)}, bf16[1344,256]{1,0:T(8,128)(2,1)S(1)}, u32[]{:S(2)}, u32[]{:S(2)}) collective-permute-start(bf16[1344,256]{1,0:T(8,128)(2,1)S(1)} %bitcast.5), channel_id=1, source_target_pairs={{0,8},{4,20},{8,0},{12,28},{16,24},{20,4},{24,16},{28,12},{1,9},{5... | collective-permute-start | bytes 2064392 | tf_op jit(solution)/shard_map/ppermute | solution.py:413
  17.7 2.6 %collective-permute-start.9 = (bf16[384,256]{1,0:T(8,128)(2,1)S(1)}, bf16[384,256]{1,0:T(8,128)(2,1)S(1)}, u32[]{:S(2)}, u32[]{:S(2)}) collective-permute-start(bf16[384,256]{1,0:T(8,128)(2,1)S(1)} %shard_map.132.a0), channel_id=1, source_target_pairs={{0,2},{1,3},{2,0},{3,1},{4,6},{5,7},{6,4},{7,5},{8,10},{9,11},{10,... | collective-permute-start | bytes 589832 | tf_op jit(solution)/shard_map/ppermute | solution.py:382
  20.2 3.3 %collective-permute-done.2.w1 = bf16[1344,256]{1,0:T(8,128)(2,1)S(1)} collective-permute-done((bf16[1344,256]{1,0:T(8,128)(2,1)}, bf16[1344,256]{1,0:T(8,128)(2,1)S(1)}, u32[]{:S(2)}, u32[]{:S(2)}) %collective-permute-start.2) | collective-permute-done | bytes 688160 | tf_op jit(solution)/shard_map/ppermute | solution.py:412
  23.5 1.6 %collective-permute-start.7 = (bf16[1344,256]{1,0:T(8,128)(2,1)S(1)}, bf16[1344,256]{1,0:T(8,128)(2,1)S(1)}, u32[]{:S(2)}, u32[]{:S(2)}) collective-permute-start(bf16[1344,256]{1,0:T(8,128)(2,1)S(1)} %collective-permute-done.2.w1), channel_id=1, source_target_pairs={{0,8},{4,20},{8,0},{12,28},{16,24},{20,4},{24,16},{28,12},{1,9},{5... | collective-permute-start | bytes 2064392 | tf_op jit(solution)/shard_map/ppermute | solution.py:414
  25.1 1.6 %collective-permute-start.8 = (bf16[384,256]{1,0:T(8,128)(2,1)S(1)}, bf16[384,256]{1,0:T(8,128)(2,1)S(1)}, u32[]{:S(2)}, u32[]{:S(2)}) collective-permute-start(bf16[384,256]{1,0:T(8,128)(2,1)S(1)} %shard_map.132.a0), channel_id=1, source_target_pairs={{0,1},{1,0},{2,3},{3,2},{4,5},{5,4},{6,7},{7,6},{8,9},{9,8},{10,11... | collective-permute-start | bytes 589832 | tf_op jit(solution)/shard_map/ppermute | solution.py:382
  26.7 1.9 %collective-permute-done.9.a2 = bf16[384,256]{1,0:T(8,128)(2,1)S(1)} collective-permute-done((bf16[384,256]{1,0:T(8,128)(2,1)S(1)}, bf16[384,256]{1,0:T(8,128)(2,1)S(1)}, u32[]{:S(2)}, u32[]{:S(2)}) %collective-permute-start.9) | collective-permute-done | bytes 196640 | tf_op jit(solution)/shard_map/ppermute | solution.py:382
  28.6 0.6 %collective-permute-start.10 = (bf16[384,256]{1,0:T(8,128)(2,1)S(1)}, bf16[384,256]{1,0:T(8,128)(2,1)S(1)}, u32[]{:S(2)}, u32[]{:S(2)}) collective-permute-start(bf16[384,256]{1,0:T(8,128)(2,1)S(1)} %collective-permute-done.9.a2), channel_id=1, source_target_pairs={{0,1},{1,0},{2,3},{3,2},{4,5},{5,4},{6,7},{7,6},{8,9},{9,8},{10,11... | collective-permute-start | bytes 589832 | tf_op jit(solution)/shard_map/ppermute | solution.py:382
  29.2 3.8 %collective-permute-done.8.a1 = bf16[384,256]{1,0:T(8,128)(2,1)S(1)} collective-permute-done((bf16[384,256]{1,0:T(8,128)(2,1)S(1)}, bf16[384,256]{1,0:T(8,128)(2,1)S(1)}, u32[]{:S(2)}, u32[]{:S(2)}) %collective-permute-start.8) | collective-permute-done | bytes 196640 | tf_op jit(solution)/shard_map/ppermute | solution.py:382
  33.0 3.3 %collective-permute-done.10.a3 = bf16[384,256]{1,0:T(8,128)(2,1)S(1)} collective-permute-done((bf16[384,256]{1,0:T(8,128)(2,1)S(1)}, bf16[384,256]{1,0:T(8,128)(2,1)S(1)}, u32[]{:S(2)}, u32[]{:S(2)}) %collective-permute-start.10) | collective-permute-done | bytes 196640 | tf_op jit(solution)/shard_map/ppermute | solution.py:382
  36.3 0.0 collective-permute-done.11.w2
  36.3 1.3 %shard_map.133 = (f32[1344,192]{1,0:T(8,128)S(1)}, f32[1344,192]{1,0:T(8,128)S(1)}) custom-call(bf16[1344,256]{1,0:T(8,128)(2,1)S(1)} %bitcast.6, bf16[1344,256]{1,0:T(8,128)(2,1)S(1)} %collective-permute-done.2.w1, bf16[1344,256]{1,0:T(8,128)(2,1)S(1)} %collective-permute-done.11.w2, bf16[384,256]{1,0:T(8,128)(2,1)S(1)} %shard_map.132.a0, ...), custom_call_target="tpu_custom_call" | custom-call | flops 3963617280 | tf_op jit(solution)/shard_map/pallas_call | solution.py:416
  37.6 0.0 collective-permute-done.7.w3
  37.6 0.4 shard_map.135
  38.1 0.1 collective-permute-start.12
  38.2 0.4 shard_map.134.own
  38.5 0.0 copy-start.4
  38.6 0.0 copy-start.2
  38.6 0.0 copy-start
  38.6 0.0 copy-start.1
  38.6 1.4 %collective-permute-done.12.received = bf16[2016,128]{1,0:T(8,128)(2,1)S(1)} collective-permute-done((bf16[2016,128]{1,0:T(8,128)(2,1)S(1)}, bf16[2016,128]{1,0:T(8,128)(2,1)S(1)}, u32[]{:S(2)}, u32[]{:S(2)}) %collective-permute-start.12) | collective-permute-done | bytes 516128 | tf_op jit(solution)/shard_map/ppermute | solution.py:436
  40.0 0.3 shard_map.136
  40.4 0.3 collective-permute-start.13
  40.7 4.4 %collective-permute-start.14 = (f32[1,192]{1,0:T(1,128)S(1)}, f32[1,192]{1,0:T(1,128)S(1)}, u32[]{:S(2)}, u32[]{:S(2)}) collective-permute-start(f32[1,192]{1,0:T(1,128)S(1)} %get-tuple-element.33.s0), channel_id=1, source_target_pairs={{0,2},{1,3},{2,0},{3,1},{4,6},{5,7},{6,4},{7,5},{8,10},{9,11},{10,... | collective-permute-start | bytes 2312 | tf_op jit(solution)/shard_map/ppermute | solution.py:373
  45.0 0.5 collective-permute-start.15
  45.5 0.0 copy-done.4
  45.5 0.0 copy-done.2
  45.5 1.0 %shard_map.137 = (f32[1344,128]{1,0:T(8,128)S(1)}, f32[64,1344]{1,0:T(8,128)S(1)}, f32[64,128]{1,0:T(8,128)S(1)}, f32[64,128]{1,0:T(8,128)S(1)}) custom-call(s32[1,2]{1,0:T(1,128)S(1)} %copy-done.2, f32[1344,192]{1,0:T(8,128)S(1)} %get-tuple-element.28.projected, f32[1,1344]{1,0:T(1,128)S(1)} %broadcast_in_dim.3.gain), custom_call_target="tpu_custom_call" | custom-call | tf_op jit(solution)/shard_map/pallas_call | solution.py:443
  46.5 0.0 collective-permute-done.13.s1
  46.5 0.1 collective-permute-done.14.s2
  46.6 2.0 %collective-permute-done.15.s3 = f32[1,192]{1,0:T(1,128)S(1)} collective-permute-done((f32[1,192]{1,0:T(1,128)S(1)}, f32[1,192]{1,0:T(1,128)S(1)}, u32[]{:S(2)}, u32[]{:S(2)}) %collective-permute-start.15) | collective-permute-done | bytes 800 | tf_op jit(solution)/shard_map/ppermute | solution.py:373
  48.6 0.0 copy-done
  48.6 0.0 copy-done.1
  48.6 1.2 %shard_map.138 = (bf16[1344,128]{1,0:T(8,128)(2,1)}, bf16[1,64,1344]{2,1,0:T(8,128)(2,1)}, f32[1,1344]{1,0:T(1,128)}) custom-call(f32[1344,128]{1,0:T(8,128)S(1)} %get-tuple-element.29.prefix, f32[64,1344]{1,0:T(8,128)S(1)} %get-tuple-element.30.option, f32[64,128]{1,0:T(8,128)S(1)} %get-tuple-element.31.kept, f32[64,128]{1,0:T(8,128)S(1)} %get-tuple-element.32.share, ...), custom_call_target="tpu_custom_call" | custom-call | tf_op jit(solution)/shard_map/pallas_call | solution.py:455
  (2 shorter events, 0.0 us)
Async XLA Ops:
  0.6 1.7 %collective-permute-start = (bf16[128,256]{1,0:T(8,128)(2,1)}, bf16[128,256]{1,0:T(8,128)(2,1)S(1)}, u32[]{:S(2)}, u32[]{:S(2)}) collective-permute-start(bf16[128,256]{1,0:T(8,128)(2,1)} %k.1), channel_id=1, source_target_pairs={{0,4},{4,0},{8,12},{12,8},{16,20},{20,16},{24,28},{28,24},{1,5},{5... | collective-permute-start | bytes 196616 | tf_op jit(solution)/shard_map/ppermute | solution.py:386
  1.1 1.5 %collective-permute-start.1 = (bf16[128,256]{1,0:T(8,128)(2,1)}, bf16[128,256]{1,0:T(8,128)(2,1)S(1)}, u32[]{:S(2)}, u32[]{:S(2)}) collective-permute-start(bf16[128,256]{1,0:T(8,128)(2,1)} %v.1), channel_id=1, source_target_pairs={{0,4},{4,0},{8,12},{12,8},{16,20},{20,16},{24,28},{28,24},{1,5},{5... | collective-permute-start | bytes 196616 | tf_op jit(solution)/shard_map/ppermute | solution.py:387
  2.6 6.6 %collective-permute-start.6 = (bf16[256,256]{1,0:T(8,128)(2,1)S(1)}, bf16[256,256]{1,0:T(8,128)(2,1)S(1)}, u32[]{:S(2)}, u32[]{:S(2)}) collective-permute-start(bf16[256,256]{1,0:T(8,128)(2,1)S(1)} %get-tuple-element.23), channel_id=1, source_target_pairs={{0,4},{4,0},{8,12},{12,8},{16,20},{20,16},{24,28},{28,24},{1,5},{5... | collective-permute-start | bytes 393224 | tf_op jit(solution)/shard_map/ppermute | solution.py:396
  2.9 8.1 %collective-permute-start.3 = (bf16[256,256]{1,0:T(8,128)(2,1)S(1)}, bf16[256,256]{1,0:T(8,128)(2,1)S(1)}, u32[]{:S(2)}, u32[]{:S(2)}) collective-permute-start(bf16[256,256]{1,0:T(8,128)(2,1)S(1)} %shard_map.131.kv0), channel_id=1, source_target_pairs={{0,24},{4,28},{8,16},{12,20},{16,8},{20,12},{24,0},{28,4},{1,25},{... | collective-permute-start | bytes 393224 | tf_op jit(solution)/shard_map/ppermute | solution.py:397
  6.7 6.6 %collective-permute-start.4 = (bf16[256,256]{1,0:T(8,128)(2,1)S(1)}, bf16[256,256]{1,0:T(8,128)(2,1)S(1)}, u32[]{:S(2)}, u32[]{:S(2)}) collective-permute-start(bf16[256,256]{1,0:T(8,128)(2,1)S(1)} %shard_map.131.kv0), channel_id=1, source_target_pairs={{0,16},{4,12},{8,24},{12,4},{16,0},{20,28},{24,8},{28,20},{1,17},{... | collective-permute-start | bytes 393224 | tf_op jit(solution)/shard_map/ppermute | solution.py:398
  7.2 7.2 %collective-permute-start.5 = (bf16[256,256]{1,0:T(8,128)(2,1)S(1)}, bf16[256,256]{1,0:T(8,128)(2,1)S(1)}, u32[]{:S(2)}, u32[]{:S(2)}) collective-permute-start(bf16[256,256]{1,0:T(8,128)(2,1)S(1)} %shard_map.131.kv0), channel_id=1, source_target_pairs={{0,8},{4,20},{8,0},{12,28},{16,24},{20,4},{24,16},{28,12},{1,9},{5... | collective-permute-start | bytes 393224 | tf_op jit(solution)/shard_map/ppermute | solution.py:399
  7.2 8.9 %copy-start.3 = (bf16[256,1344]{0,1:T(8,128)(2,1)S(1)}, bf16[256,1344]{0,1:T(8,128)(2,1)}, u32[]{:S(2)}) copy-start(bf16[256,1344]{0,1:T(8,128)(2,1)} %param.19) | copy-start | bytes 2064388
  7.2 16.3 %collective-permute-start.2 = (bf16[1344,256]{1,0:T(8,128)(2,1)}, bf16[1344,256]{1,0:T(8,128)(2,1)S(1)}, u32[]{:S(2)}, u32[]{:S(2)}) collective-permute-start(bf16[1344,256]{1,0:T(8,128)(2,1)} %bitcast.4), channel_id=1, source_target_pairs={{0,16},{4,12},{8,24},{12,4},{16,0},{20,28},{24,8},{28,20},{1,17},{... | collective-permute-start | bytes 2064392 | tf_op jit(solution)/shard_map/ppermute | solution.py:412
  16.1 20.2 %collective-permute-start.11 = (bf16[1344,256]{1,0:T(8,128)(2,1)S(1)}, bf16[1344,256]{1,0:T(8,128)(2,1)S(1)}, u32[]{:S(2)}, u32[]{:S(2)}) collective-permute-start(bf16[1344,256]{1,0:T(8,128)(2,1)S(1)} %bitcast.5), channel_id=1, source_target_pairs={{0,8},{4,20},{8,0},{12,28},{16,24},{20,4},{24,16},{28,12},{1,9},{5... | collective-permute-start | bytes 2064392 | tf_op jit(solution)/shard_map/ppermute | solution.py:413
  17.7 10.9 %collective-permute-start.9 = (bf16[384,256]{1,0:T(8,128)(2,1)S(1)}, bf16[384,256]{1,0:T(8,128)(2,1)S(1)}, u32[]{:S(2)}, u32[]{:S(2)}) collective-permute-start(bf16[384,256]{1,0:T(8,128)(2,1)S(1)} %shard_map.132.a0), channel_id=1, source_target_pairs={{0,2},{1,3},{2,0},{3,1},{4,6},{5,7},{6,4},{7,5},{8,10},{9,11},{10,... | collective-permute-start | bytes 589832 | tf_op jit(solution)/shard_map/ppermute | solution.py:382
  23.5 14.1 %collective-permute-start.7 = (bf16[1344,256]{1,0:T(8,128)(2,1)S(1)}, bf16[1344,256]{1,0:T(8,128)(2,1)S(1)}, u32[]{:S(2)}, u32[]{:S(2)}) collective-permute-start(bf16[1344,256]{1,0:T(8,128)(2,1)S(1)} %collective-permute-done.2.w1), channel_id=1, source_target_pairs={{0,8},{4,20},{8,0},{12,28},{16,24},{20,4},{24,16},{28,12},{1,9},{5... | collective-permute-start | bytes 2064392 | tf_op jit(solution)/shard_map/ppermute | solution.py:414
  25.1 7.8 %collective-permute-start.8 = (bf16[384,256]{1,0:T(8,128)(2,1)S(1)}, bf16[384,256]{1,0:T(8,128)(2,1)S(1)}, u32[]{:S(2)}, u32[]{:S(2)}) collective-permute-start(bf16[384,256]{1,0:T(8,128)(2,1)S(1)} %shard_map.132.a0), channel_id=1, source_target_pairs={{0,1},{1,0},{2,3},{3,2},{4,5},{5,4},{6,7},{7,6},{8,9},{9,8},{10,11... | collective-permute-start | bytes 589832 | tf_op jit(solution)/shard_map/ppermute | solution.py:382
  28.6 7.7 %collective-permute-start.10 = (bf16[384,256]{1,0:T(8,128)(2,1)S(1)}, bf16[384,256]{1,0:T(8,128)(2,1)S(1)}, u32[]{:S(2)}, u32[]{:S(2)}) collective-permute-start(bf16[384,256]{1,0:T(8,128)(2,1)S(1)} %collective-permute-done.9.a2), channel_id=1, source_target_pairs={{0,1},{1,0},{2,3},{3,2},{4,5},{5,4},{6,7},{7,6},{8,9},{9,8},{10,11... | collective-permute-start | bytes 589832 | tf_op jit(solution)/shard_map/ppermute | solution.py:382
  38.1 2.0 %collective-permute-start.12 = (bf16[2016,128]{1,0:T(8,128)(2,1)S(1)}, bf16[2016,128]{1,0:T(8,128)(2,1)S(1)}, u32[]{:S(2)}, u32[]{:S(2)}) collective-permute-start(bf16[2016,128]{1,0:T(8,128)(2,1)S(1)} %shard_map.135), channel_id=1, source_target_pairs={{0,4},{4,0},{8,12},{12,8},{16,20},{20,16},{24,28},{28,24},{1,5},{5... | collective-permute-start | bytes 1548296 | tf_op jit(solution)/shard_map/ppermute | solution.py:436
  38.5 6.9 %copy-start.4 = (f32[1344]{0:T(1024)S(1)}, f32[1344]{0:T(1024)}, u32[]{:S(2)}) copy-start(f32[1344]{0:T(1024)} %param.20) | copy-start | bytes 16132
  38.6 6.9 %copy-start.2 = (s32[1,2]{1,0:T(1,128)S(1)}, s32[1,2]{1,0:T(1,128)}, u32[]{:S(2)}) copy-start(s32[1,2]{1,0:T(1,128)} %bounds.1) | copy-start | bytes 28
  38.6 10.0 %copy-start = (bf16[128,1344]{0,1:T(8,128)(2,1)S(1)}, bf16[128,1344]{0,1:T(8,128)(2,1)}, u32[]{:S(2)}) copy-start(bf16[128,1344]{0,1:T(8,128)(2,1)} %param.14) | copy-start | bytes 1032196
  38.6 10.0 %copy-start.1 = (bf16[1,64,1344]{2,1,0:T(8,128)(2,1)S(1)}, bf16[1,64,1344]{2,1,0:T(8,128)(2,1)}, u32[]{:S(2)}) copy-start(bf16[1,64,1344]{2,1,0:T(8,128)(2,1)} %opt_resid.1) | copy-start | bytes 516100
  40.4 6.1 %collective-permute-start.13 = (f32[1,192]{1,0:T(1,128)S(1)}, f32[1,192]{1,0:T(1,128)S(1)}, u32[]{:S(2)}, u32[]{:S(2)}) collective-permute-start(f32[1,192]{1,0:T(1,128)S(1)} %get-tuple-element.33.s0), channel_id=1, source_target_pairs={{0,1},{1,2},{2,3},{3,0},{4,5},{5,6},{6,7},{7,4},{8,9},{9,10},{10,1... | collective-permute-start | bytes 2312 | tf_op jit(solution)/shard_map/ppermute | solution.py:373
  40.7 5.9 %collective-permute-start.14 = (f32[1,192]{1,0:T(1,128)S(1)}, f32[1,192]{1,0:T(1,128)S(1)}, u32[]{:S(2)}, u32[]{:S(2)}) collective-permute-start(f32[1,192]{1,0:T(1,128)S(1)} %get-tuple-element.33.s0), channel_id=1, source_target_pairs={{0,2},{1,3},{2,0},{3,1},{4,6},{5,7},{6,4},{7,5},{8,10},{9,11},{10,... | collective-permute-start | bytes 2312 | tf_op jit(solution)/shard_map/ppermute | solution.py:373
  45.0 3.6 %collective-permute-start.15 = (f32[1,192]{1,0:T(1,128)S(1)}, f32[1,192]{1,0:T(1,128)S(1)}, u32[]{:S(2)}, u32[]{:S(2)}) collective-permute-start(f32[1,192]{1,0:T(1,128)S(1)} %get-tuple-element.33.s0), channel_id=1, source_target_pairs={{0,3},{1,0},{2,1},{3,2},{4,7},{5,4},{6,5},{7,6},{8,11},{9,8},{10,9... | collective-permute-start | bytes 2312 | tf_op jit(solution)/shard_map/ppermute | solution.py:373

commit v7 on v5

--- a/solution.py
+++ b/solution.py
@@ -278,19 +278,28 @@
             out[part, :] = total + dot_nt(w2[part, :], blocks[2])
 
 
-def complete_kernel(rows, opt, packed, w3, chosen, a0, a1, a2, a3, partial, out, placed):
+def add_kernel(chosen, a3, pair_part, own_part, pair_out, own_out):
+    block = a3[...]
+    block = jnp.where(apart()[3] == 3, jnp.zeros_like(block), block)
+    count = block.shape[0] // 2
+    middle = chosen.shape[0] // 2
+    for r, (part, out) in enumerate(((pair_part, pair_out), (own_part, own_out))):
+        for n in range(2):
+            at = slice(n * middle, (n + 1) * middle)
+            product = dot_nt(chosen[at, :], block[r * count : (r + 1) * count, :])
+            out[at, :] = part[at, :] + product
+
+
+def complete_kernel(rows, opt, packed, w3, a0, a1, a2, a3, partial, out, placed):
     mine = slice(0, rows + opt) if packed else slice(rows + opt, 2 * (rows + opt))
     for t, block in enumerate((a0, a1, a2, a3)):
         placed[t] = block[mine, :]
-    meets = apart()[3]
-    first = placed[meets]
-    second = jnp.where(meets == 3, jnp.zeros_like(first), placed[3])
+    block = placed[apart()[3]]
     features = w3.shape[0]
     half = features // 2
     for n in range(2):
         part = slice(n * half, (n + 1) * half)
-        total = dot_nt(w3[part, :], first) + dot_nt(chosen[part, :], second)
-        total += partial[part, :]
+        total = partial[part, :] + dot_nt(w3[part, :], block)
         if packed:
             total = total.astype(out.dtype)
             out[part, :] = total[:, 0:rows]
@@ -434,15 +443,19 @@
         vmem=16,
     )(weight, weight_1, weight_2, *blocks[:3])
 
+    pair_part, own_part = call(
+        add_kernel, [shape((features, rows + opt), f32)] * 2, 4, flops=flops, vmem=16
+    )(chosen, blocks[3], pair_part, own_part)
+
     def complete(partial, out_shape, packed):
         return call(
             functools.partial(complete_kernel, rows, opt, packed),
             out_shape,
-            7,
+            6,
             flops=flops // 2,
             scratch=[pltpu.VMEM((4, rows + opt, wide), bf16)],
             vmem=16,
-        )(weight_3, chosen, *blocks, partial)
+        )(weight_3, *blocks, partial)
 
     half = complete(pair_part, shape((features + features // 2, rows), bf16), True)
     received = lax.ppermute(half, "seq", pair)

time: 47.7 us -> 47.6 us (level)
    ppermute x1, waiting for transfers between devices: 1.45 us -> 0.9 us  [paired_body(): weight_3 = lax.ppermute(after(weight_1, block), 'seq', second)]
    pallas_call x2 -> x3, Pallas kernels: 1.16 us -> 1.38 us  [the longest x2 0.84 us: complete(): call(functools.partial(complete_kernel, rows, opt, packed), out_shape, 6,...]
  transfers between devices with their start and end apart: 16 -> 16, of which waited for: 10 -> 10; matrix products, arithmetic and copies ran while one was open for 0% -> 0% of each run, Pallas kernels for 12% -> 13%
where the time goes in v7:
time: 47.6 us; the launch traced here: 47.4 us
  starting transfers between devices  20.6 us (43%)
  waiting for transfers between devices  18 us (38%)
  Pallas kernels  7.96 us (17%)
  between operations  0.77 us (2%)
    ppermute x3, waiting for transfers between devices, crossed(): lax.ppermute(value, 'head', [(i, i ^ mask) for i in range(lax.axis_size('...  7.18 us
    ppermute x3, starting transfers between devices, turned(): lax.ppermute(value, 'head', [(i, (i + steps) % count) for i in range(coun...  5.54 us
    ppermute x3, starting transfers between devices, crossed(): lax.ppermute(value, 'head', [(i, i ^ mask) for i in range(lax.axis_size('...  4.72 us
    ppermute x1, starting transfers between devices, paired_body(): kv_3 = lax.ppermute(kv_0, 'seq', both)  3.79 us
    ppermute x1, waiting for transfers between devices, paired_body(): kv_1 = lax.ppermute(kv_0, 'seq', first)  2.34 us
    ppermute x1, starting transfers between devices, paired_body(): weight_1 = lax.ppermute(after(weight, kv_0), 'seq', first)  1.99 us
    ppermute x1, waiting for transfers between devices, paired_body(): weight_1 = lax.ppermute(after(weight, kv_0), 'seq', first)  1.75 us
    pallas_call x1, Pallas kernels, paired_body(): call(functools.partial(attn_kernel, rows, opt), pltpu.VMEM((2 * (rows + o...  1.72 us
  transfers between devices with their start and end apart: 16, of which 10 were waited for; matrix products, arithmetic and copies ran while one was open for 0% of the time, Pallas kernels for 13%

profile of v7, /device:TPU:0, one launch (start us, length us, event | category | flops | bytes accessed | tf_op | source)
XLA Modules:
  0.0 47.4 jit_solution(2487095933469907929)
XLA Ops:
  0.6 0.5 %collective-permute-start = (bf16[128,256]{1,0:T(8,128)(2,1)}, bf16[128,256]{1,0:T(8,128)(2,1)S(1)}, u32[]{:S(2)}, u32[]{:S(2)}) collective-permute-start(bf16[128,256]{1,0:T(8,128)(2,1)} %k.1), channel_id=1, source_target_pairs={{0,4},{4,0},{8,12},{12,8},{16,20},{20,16},{24,28},{28,24},{1,5},{5... | collective-permute-start | bytes 196616 | tf_op jit(solution)/shard_map/ppermute | solution.py:407
  1.1 0.1 collective-permute-start.1
  1.2 1.1 %shard_map.130 = (bf16[384,256]{1,0:T(8,128)(2,1)S(1)}, bf16[256,256]{1,0:T(8,128)(2,1)S(1)}) custom-call(bf16[128,512]{1,0:T(8,128)(2,1)} %q.1, bf16[128,256]{1,0:T(8,128)(2,1)} %k.1, bf16[128,256]{1,0:T(8,128)(2,1)} %v.1, bf16[1,64,512]{2,1,0:T(8,128)(2,1)} %oq.1, bf16[1,64,256]{2,1,0:T(8,128)(2,1)} %ok.1, bf16[1,64,256]{2,1,0:T(8,128)(2,1)} %ov.1), custom_call_target="tpu_custom_call" | custom-call | tf_op jit(solution)/shard_map/pallas_call | solution.py:409
  2.3 0.0 collective-permute-done.k
  2.3 0.3 collective-permute-done.1.v
  2.6 0.2 collective-permute-start.6
  2.9 3.8 %collective-permute-start.3 = (bf16[256,256]{1,0:T(8,128)(2,1)S(1)}, bf16[256,256]{1,0:T(8,128)(2,1)S(1)}, u32[]{:S(2)}, u32[]{:S(2)}) collective-permute-start(bf16[256,256]{1,0:T(8,128)(2,1)S(1)} %shard_map.131.kv0), channel_id=1, source_target_pairs={{0,24},{4,28},{8,16},{12,20},{16,8},{20,12},{24,0},{28,4},{1,25},{... | collective-permute-start | bytes 393224 | tf_op jit(solution)/shard_map/ppermute | solution.py:418
  6.7 0.5 %collective-permute-start.4 = (bf16[256,256]{1,0:T(8,128)(2,1)S(1)}, bf16[256,256]{1,0:T(8,128)(2,1)S(1)}, u32[]{:S(2)}, u32[]{:S(2)}) collective-permute-start(bf16[256,256]{1,0:T(8,128)(2,1)S(1)} %shard_map.131.kv0), channel_id=1, source_target_pairs={{0,16},{4,12},{8,24},{12,4},{16,0},{20,28},{24,8},{28,20},{1,17},{... | collective-permute-start | bytes 393224 | tf_op jit(solution)/shard_map/ppermute | solution.py:419
  7.2 0.1 collective-permute-start.5
  7.2 0.0 copy-start.3
  7.2 2.0 %collective-permute-start.2 = (bf16[1344,256]{1,0:T(8,128)(2,1)}, bf16[1344,256]{1,0:T(8,128)(2,1)S(1)}, u32[]{:S(2)}, u32[]{:S(2)}) collective-permute-start(bf16[1344,256]{1,0:T(8,128)(2,1)} %bitcast.4), channel_id=1, source_target_pairs={{0,16},{4,12},{8,24},{12,4},{16,0},{20,28},{24,8},{28,20},{1,17},{... | collective-permute-start | bytes 2064392 | tf_op jit(solution)/shard_map/ppermute | solution.py:433
  9.2 0.0 collective-permute-done.6.received
  9.2 1.7 %collective-permute-done.3.kv3 = bf16[256,256]{1,0:T(8,128)(2,1)S(1)} collective-permute-done((bf16[256,256]{1,0:T(8,128)(2,1)S(1)}, bf16[256,256]{1,0:T(8,128)(2,1)S(1)}, u32[]{:S(2)}, u32[]{:S(2)}) %collective-permute-start.3) | collective-permute-done | bytes 131104 | tf_op jit(solution)/shard_map/ppermute | solution.py:418
  10.9 2.3 %collective-permute-done.4.kv1 = bf16[256,256]{1,0:T(8,128)(2,1)S(1)} collective-permute-done((bf16[256,256]{1,0:T(8,128)(2,1)S(1)}, bf16[256,256]{1,0:T(8,128)(2,1)S(1)}, u32[]{:S(2)}, u32[]{:S(2)}) %collective-permute-start.4) | collective-permute-done | bytes 131104 | tf_op jit(solution)/shard_map/ppermute | solution.py:419
  13.3 1.1 %collective-permute-done.5.kv2 = bf16[256,256]{1,0:T(8,128)(2,1)S(1)} collective-permute-done((bf16[256,256]{1,0:T(8,128)(2,1)S(1)}, bf16[256,256]{1,0:T(8,128)(2,1)S(1)}, u32[]{:S(2)}, u32[]{:S(2)}) %collective-permute-start.5) | collective-permute-done | bytes 131104 | tf_op jit(solution)/shard_map/ppermute | solution.py:420
  14.3 1.7 %shard_map.132.a0 = bf16[384,256]{1,0:T(8,128)(2,1)S(1)} custom-call(bf16[256,256]{1,0:T(8,128)(2,1)S(1)} %shard_map.131.kv0, bf16[256,256]{1,0:T(8,128)(2,1)S(1)} %collective-permute-done.3.kv3, bf16[256,256]{1,0:T(8,128)(2,1)S(1)} %collective-permute-done.4.kv1, bf16[256,256]{1,0:T(8,128)(2,1)S(1)} %collective-permute-done.5.kv2, ...), custom_call_target="tpu_custom_call" | custom-call | flops 40265318400 | tf_op jit(solution)/shard_map/pallas_call | solution.py:423
  16.1 0.0 copy-done.3
  16.1 1.6 %collective-permute-start.11 = (bf16[1344,256]{1,0:T(8,128)(2,1)S(1)}, bf16[1344,256]{1,0:T(8,128)(2,1)S(1)}, u32[]{:S(2)}, u32[]{:S(2)}) collective-permute-start(bf16[1344,256]{1,0:T(8,128)(2,1)S(1)} %bitcast.5), channel_id=1, source_target_pairs={{0,8},{4,20},{8,0},{12,28},{16,24},{20,4},{24,16},{28,12},{1,9},{5... | collective-permute-start | bytes 2064392 | tf_op jit(solution)/shard_map/ppermute | solution.py:434
  17.7 2.6 %collective-permute-start.9 = (bf16[384,256]{1,0:T(8,128)(2,1)S(1)}, bf16[384,256]{1,0:T(8,128)(2,1)S(1)}, u32[]{:S(2)}, u32[]{:S(2)}) collective-permute-start(bf16[384,256]{1,0:T(8,128)(2,1)S(1)} %shard_map.132.a0), channel_id=1, source_target_pairs={{0,2},{1,3},{2,0},{3,1},{4,6},{5,7},{6,4},{7,5},{8,10},{9,11},{10,... | collective-permute-start | bytes 589832 | tf_op jit(solution)/shard_map/ppermute | solution.py:403
  20.2 1.6 %collective-permute-start.8 = (bf16[384,256]{1,0:T(8,128)(2,1)S(1)}, bf16[384,256]{1,0:T(8,128)(2,1)S(1)}, u32[]{:S(2)}, u32[]{:S(2)}) collective-permute-start(bf16[384,256]{1,0:T(8,128)(2,1)S(1)} %shard_map.132.a0), channel_id=1, source_target_pairs={{0,1},{1,0},{2,3},{3,2},{4,5},{5,4},{6,7},{7,6},{8,9},{9,8},{10,11... | collective-permute-start | bytes 589832 | tf_op jit(solution)/shard_map/ppermute | solution.py:403
  21.8 1.8 %collective-permute-done.2.w1 = bf16[1344,256]{1,0:T(8,128)(2,1)S(1)} collective-permute-done((bf16[1344,256]{1,0:T(8,128)(2,1)}, bf16[1344,256]{1,0:T(8,128)(2,1)S(1)}, u32[]{:S(2)}, u32[]{:S(2)}) %collective-permute-start.2) | collective-permute-done | bytes 688160 | tf_op jit(solution)/shard_map/ppermute | solution.py:433
  23.5 1.6 %collective-permute-start.7 = (bf16[1344,256]{1,0:T(8,128)(2,1)S(1)}, bf16[1344,256]{1,0:T(8,128)(2,1)S(1)}, u32[]{:S(2)}, u32[]{:S(2)}) collective-permute-start(bf16[1344,256]{1,0:T(8,128)(2,1)S(1)} %collective-permute-done.2.w1), channel_id=1, source_target_pairs={{0,8},{4,20},{8,0},{12,28},{16,24},{20,4},{24,16},{28,12},{1,9},{5... | collective-permute-start | bytes 2064392 | tf_op jit(solution)/shard_map/ppermute | solution.py:435
  25.1 3.4 %collective-permute-done.9.a2 = bf16[384,256]{1,0:T(8,128)(2,1)S(1)} collective-permute-done((bf16[384,256]{1,0:T(8,128)(2,1)S(1)}, bf16[384,256]{1,0:T(8,128)(2,1)S(1)}, u32[]{:S(2)}, u32[]{:S(2)}) %collective-permute-start.9) | collective-permute-done | bytes 196640 | tf_op jit(solution)/shard_map/ppermute | solution.py:403
  28.6 0.6 %collective-permute-start.10 = (bf16[384,256]{1,0:T(8,128)(2,1)S(1)}, bf16[384,256]{1,0:T(8,128)(2,1)S(1)}, u32[]{:S(2)}, u32[]{:S(2)}) collective-permute-start(bf16[384,256]{1,0:T(8,128)(2,1)S(1)} %collective-permute-done.9.a2), channel_id=1, source_target_pairs={{0,1},{1,0},{2,3},{3,2},{4,5},{5,4},{6,7},{7,6},{8,9},{9,8},{10,11... | collective-permute-start | bytes 589832 | tf_op jit(solution)/shard_map/ppermute | solution.py:403
  29.1 0.0 collective-permute-done.8.a1
  29.1 0.0 collective-permute-done.11.w2
  29.1 1.3 %shard_map.133 = (f32[1344,192]{1,0:T(8,128)S(1)}, f32[1344,192]{1,0:T(8,128)S(1)}, bf16[1344,256]{1,0:T(8,128)(2,1)S(1)}) custom-call(bf16[1344,256]{1,0:T(8,128)(2,1)S(1)} %bitcast.6, bf16[1344,256]{1,0:T(8,128)(2,1)S(1)} %collective-permute-done.2.w1, bf16[1344,256]{1,0:T(8,128)(2,1)S(1)} %collective-permute-done.11.w2, ...), custom_call_target="tpu_custom_call" | custom-call | flops 6341787648 | tf_op jit(solution)/shard_map/pallas_call | solution.py:437
  30.5 3.7 %collective-permute-done.10.a3 = bf16[384,256]{1,0:T(8,128)(2,1)S(1)} collective-permute-done((bf16[384,256]{1,0:T(8,128)(2,1)S(1)}, bf16[384,256]{1,0:T(8,128)(2,1)S(1)}, u32[]{:S(2)}, u32[]{:S(2)}) %collective-permute-start.10) | collective-permute-done | bytes 196640 | tf_op jit(solution)/shard_map/ppermute | solution.py:403
  34.2 0.5 %shard_map.134 = (f32[1344,192]{1,0:T(8,128)S(1)}, f32[1344,192]{1,0:T(8,128)S(1)}) custom-call(bf16[1344,256]{1,0:T(8,128)(2,1)S(1)} %get-tuple-element.29.chosen, bf16[384,256]{1,0:T(8,128)(2,1)S(1)} %collective-permute-done.10.a3, f32[1344,192]{1,0:T(8,128)S(1)} %get-tuple-element.30.pair_part, f32[1344,192]{1,0:T(8,128)S(1)} %get-tuple-element.31.own_part), custom_call_target="tpu_custom_call" | custom-call | flops 264241152 | tf_op jit(solution)/shard_map/pallas_call | solution.py:446
  34.8 0.9 %collective-permute-done.7.w3 = bf16[1344,256]{1,0:T(8,128)(2,1)S(1)} collective-permute-done((bf16[1344,256]{1,0:T(8,128)(2,1)S(1)}, bf16[1344,256]{1,0:T(8,128)(2,1)S(1)}, u32[]{:S(2)}, u32[]{:S(2)}) %collective-permute-start.7) | collective-permute-done | bytes 688160 | tf_op jit(solution)/shard_map/ppermute | solution.py:435
  35.7 0.5 shard_map.136
  36.1 0.1 collective-permute-start.12
  36.2 0.4 shard_map.135.own
  36.6 0.0 copy-start.4
  36.6 0.0 copy-start.2
  36.6 0.0 copy-start
  36.6 0.0 copy-start.1
  36.7 1.4 %collective-permute-done.12.received = bf16[2016,128]{1,0:T(8,128)(2,1)S(1)} collective-permute-done((bf16[2016,128]{1,0:T(8,128)(2,1)S(1)}, bf16[2016,128]{1,0:T(8,128)(2,1)S(1)}, u32[]{:S(2)}, u32[]{:S(2)}) %collective-permute-start.12) | collective-permute-done | bytes 516128 | tf_op jit(solution)/shard_map/ppermute | solution.py:461
  38.1 0.3 shard_map.137
  38.4 1.6 %collective-permute-start.13 = (f32[1,192]{1,0:T(1,128)S(1)}, f32[1,192]{1,0:T(1,128)S(1)}, u32[]{:S(2)}, u32[]{:S(2)}) collective-permute-start(f32[1,192]{1,0:T(1,128)S(1)} %get-tuple-element.39.s0), channel_id=1, source_target_pairs={{0,1},{1,2},{2,3},{3,0},{4,5},{5,6},{6,7},{7,4},{8,9},{9,10},{10,1... | collective-permute-start | bytes 2312 | tf_op jit(solution)/shard_map/ppermute | solution.py:394
  40.0 2.7 %collective-permute-start.14 = (f32[1,192]{1,0:T(1,128)S(1)}, f32[1,192]{1,0:T(1,128)S(1)}, u32[]{:S(2)}, u32[]{:S(2)}) collective-permute-start(f32[1,192]{1,0:T(1,128)S(1)} %get-tuple-element.39.s0), channel_id=1, source_target_pairs={{0,2},{1,3},{2,0},{3,1},{4,6},{5,7},{6,4},{7,5},{8,10},{9,11},{10,... | collective-permute-start | bytes 2312 | tf_op jit(solution)/shard_map/ppermute | solution.py:394
  42.7 1.3 %collective-permute-start.15 = (f32[1,192]{1,0:T(1,128)S(1)}, f32[1,192]{1,0:T(1,128)S(1)}, u32[]{:S(2)}, u32[]{:S(2)}) collective-permute-start(f32[1,192]{1,0:T(1,128)S(1)} %get-tuple-element.39.s0), channel_id=1, source_target_pairs={{0,3},{1,0},{2,1},{3,2},{4,7},{5,4},{6,5},{7,6},{8,11},{9,8},{10,9... | collective-permute-start | bytes 2312 | tf_op jit(solution)/shard_map/ppermute | solution.py:394
  43.9 0.0 copy-done.4
  44.0 0.0 copy-done.2
  44.0 1.0 %shard_map.138 = (f32[1344,128]{1,0:T(8,128)S(1)}, f32[64,1344]{1,0:T(8,128)S(1)}, f32[64,128]{1,0:T(8,128)S(1)}, f32[64,128]{1,0:T(8,128)S(1)}) custom-call(s32[1,2]{1,0:T(1,128)S(1)} %copy-done.2, f32[1344,192]{1,0:T(8,128)S(1)} %get-tuple-element.34.projected, f32[1,1344]{1,0:T(1,128)S(1)} %broadcast_in_dim.3.gain), custom_call_target="tpu_custom_call" | custom-call | tf_op jit(solution)/shard_map/pallas_call | solution.py:468
  44.9 0.0 collective-permute-done.13.s1
  44.9 0.0 collective-permute-done.14.s2
  44.9 1.3 %collective-permute-done.15.s3 = f32[1,192]{1,0:T(1,128)S(1)} collective-permute-done((f32[1,192]{1,0:T(1,128)S(1)}, f32[1,192]{1,0:T(1,128)S(1)}, u32[]{:S(2)}, u32[]{:S(2)}) %collective-permute-start.15) | collective-permute-done | bytes 800 | tf_op jit(solution)/shard_map/ppermute | solution.py:394
  46.3 0.0 copy-done
  46.3 0.0 copy-done.1
  46.3 1.2 %shard_map.139 = (bf16[1344,128]{1,0:T(8,128)(2,1)}, bf16[1,64,1344]{2,1,0:T(8,128)(2,1)}, f32[1,1344]{1,0:T(1,128)}) custom-call(f32[1344,128]{1,0:T(8,128)S(1)} %get-tuple-element.35.prefix, f32[64,1344]{1,0:T(8,128)S(1)} %get-tuple-element.36.option, f32[64,128]{1,0:T(8,128)S(1)} %get-tuple-element.37.kept, f32[64,128]{1,0:T(8,128)S(1)} %get-tuple-element.38.share, ...), custom_call_target="tpu_custom_call" | custom-call | tf_op jit(solution)/shard_map/pallas_call | solution.py:480
  (2 shorter events, 0.0 us)
Async XLA Ops:
  0.6 1.7 %collective-permute-start = (bf16[128,256]{1,0:T(8,128)(2,1)}, bf16[128,256]{1,0:T(8,128)(2,1)S(1)}, u32[]{:S(2)}, u32[]{:S(2)}) collective-permute-start(bf16[128,256]{1,0:T(8,128)(2,1)} %k.1), channel_id=1, source_target_pairs={{0,4},{4,0},{8,12},{12,8},{16,20},{20,16},{24,28},{28,24},{1,5},{5... | collective-permute-start | bytes 196616 | tf_op jit(solution)/shard_map/ppermute | solution.py:407
  1.1 1.5 %collective-permute-start.1 = (bf16[128,256]{1,0:T(8,128)(2,1)}, bf16[128,256]{1,0:T(8,128)(2,1)S(1)}, u32[]{:S(2)}, u32[]{:S(2)}) collective-permute-start(bf16[128,256]{1,0:T(8,128)(2,1)} %v.1), channel_id=1, source_target_pairs={{0,4},{4,0},{8,12},{12,8},{16,20},{20,16},{24,28},{28,24},{1,5},{5... | collective-permute-start | bytes 196616 | tf_op jit(solution)/shard_map/ppermute | solution.py:408
  2.6 6.6 %collective-permute-start.6 = (bf16[256,256]{1,0:T(8,128)(2,1)S(1)}, bf16[256,256]{1,0:T(8,128)(2,1)S(1)}, u32[]{:S(2)}, u32[]{:S(2)}) collective-permute-start(bf16[256,256]{1,0:T(8,128)(2,1)S(1)} %get-tuple-element.26), channel_id=1, source_target_pairs={{0,4},{4,0},{8,12},{12,8},{16,20},{20,16},{24,28},{28,24},{1,5},{5... | collective-permute-start | bytes 393224 | tf_op jit(solution)/shard_map/ppermute | solution.py:417
  2.9 8.1 %collective-permute-start.3 = (bf16[256,256]{1,0:T(8,128)(2,1)S(1)}, bf16[256,256]{1,0:T(8,128)(2,1)S(1)}, u32[]{:S(2)}, u32[]{:S(2)}) collective-permute-start(bf16[256,256]{1,0:T(8,128)(2,1)S(1)} %shard_map.131.kv0), channel_id=1, source_target_pairs={{0,24},{4,28},{8,16},{12,20},{16,8},{20,12},{24,0},{28,4},{1,25},{... | collective-permute-start | bytes 393224 | tf_op jit(solution)/shard_map/ppermute | solution.py:418
  6.7 6.6 %collective-permute-start.4 = (bf16[256,256]{1,0:T(8,128)(2,1)S(1)}, bf16[256,256]{1,0:T(8,128)(2,1)S(1)}, u32[]{:S(2)}, u32[]{:S(2)}) collective-permute-start(bf16[256,256]{1,0:T(8,128)(2,1)S(1)} %shard_map.131.kv0), channel_id=1, source_target_pairs={{0,16},{4,12},{8,24},{12,4},{16,0},{20,28},{24,8},{28,20},{1,17},{... | collective-permute-start | bytes 393224 | tf_op jit(solution)/shard_map/ppermute | solution.py:419
  7.2 7.2 %collective-permute-start.5 = (bf16[256,256]{1,0:T(8,128)(2,1)S(1)}, bf16[256,256]{1,0:T(8,128)(2,1)S(1)}, u32[]{:S(2)}, u32[]{:S(2)}) collective-permute-start(bf16[256,256]{1,0:T(8,128)(2,1)S(1)} %shard_map.131.kv0), channel_id=1, source_target_pairs={{0,8},{4,20},{8,0},{12,28},{16,24},{20,4},{24,16},{28,12},{1,9},{5... | collective-permute-start | bytes 393224 | tf_op jit(solution)/shard_map/ppermute | solution.py:420
  7.2 8.9 %copy-start.3 = (bf16[256,1344]{0,1:T(8,128)(2,1)S(1)}, bf16[256,1344]{0,1:T(8,128)(2,1)}, u32[]{:S(2)}) copy-start(bf16[256,1344]{0,1:T(8,128)(2,1)} %param.19) | copy-start | bytes 2064388
  7.2 16.3 %collective-permute-start.2 = (bf16[1344,256]{1,0:T(8,128)(2,1)}, bf16[1344,256]{1,0:T(8,128)(2,1)S(1)}, u32[]{:S(2)}, u32[]{:S(2)}) collective-permute-start(bf16[1344,256]{1,0:T(8,128)(2,1)} %bitcast.4), channel_id=1, source_target_pairs={{0,16},{4,12},{8,24},{12,4},{16,0},{20,28},{24,8},{28,20},{1,17},{... | collective-permute-start | bytes 2064392 | tf_op jit(solution)/shard_map/ppermute | solution.py:433
  16.1 13.1 %collective-permute-start.11 = (bf16[1344,256]{1,0:T(8,128)(2,1)S(1)}, bf16[1344,256]{1,0:T(8,128)(2,1)S(1)}, u32[]{:S(2)}, u32[]{:S(2)}) collective-permute-start(bf16[1344,256]{1,0:T(8,128)(2,1)S(1)} %bitcast.5), channel_id=1, source_target_pairs={{0,8},{4,20},{8,0},{12,28},{16,24},{20,4},{24,16},{28,12},{1,9},{5... | collective-permute-start | bytes 2064392 | tf_op jit(solution)/shard_map/ppermute | solution.py:434
  17.7 10.9 %collective-permute-start.9 = (bf16[384,256]{1,0:T(8,128)(2,1)S(1)}, bf16[384,256]{1,0:T(8,128)(2,1)S(1)}, u32[]{:S(2)}, u32[]{:S(2)}) collective-permute-start(bf16[384,256]{1,0:T(8,128)(2,1)S(1)} %shard_map.132.a0), channel_id=1, source_target_pairs={{0,2},{1,3},{2,0},{3,1},{4,6},{5,7},{6,4},{7,5},{8,10},{9,11},{10,... | collective-permute-start | bytes 589832 | tf_op jit(solution)/shard_map/ppermute | solution.py:403
  20.2 8.9 %collective-permute-start.8 = (bf16[384,256]{1,0:T(8,128)(2,1)S(1)}, bf16[384,256]{1,0:T(8,128)(2,1)S(1)}, u32[]{:S(2)}, u32[]{:S(2)}) collective-permute-start(bf16[384,256]{1,0:T(8,128)(2,1)S(1)} %shard_map.132.a0), channel_id=1, source_target_pairs={{0,1},{1,0},{2,3},{3,2},{4,5},{5,4},{6,7},{7,6},{8,9},{9,8},{10,11... | collective-permute-start | bytes 589832 | tf_op jit(solution)/shard_map/ppermute | solution.py:403
  23.5 12.1 %collective-permute-start.7 = (bf16[1344,256]{1,0:T(8,128)(2,1)S(1)}, bf16[1344,256]{1,0:T(8,128)(2,1)S(1)}, u32[]{:S(2)}, u32[]{:S(2)}) collective-permute-start(bf16[1344,256]{1,0:T(8,128)(2,1)S(1)} %collective-permute-done.2.w1), channel_id=1, source_target_pairs={{0,8},{4,20},{8,0},{12,28},{16,24},{20,4},{24,16},{28,12},{1,9},{5... | collective-permute-start | bytes 2064392 | tf_op jit(solution)/shard_map/ppermute | solution.py:435
  28.6 5.7 %collective-permute-start.10 = (bf16[384,256]{1,0:T(8,128)(2,1)S(1)}, bf16[384,256]{1,0:T(8,128)(2,1)S(1)}, u32[]{:S(2)}, u32[]{:S(2)}) collective-permute-start(bf16[384,256]{1,0:T(8,128)(2,1)S(1)} %collective-permute-done.9.a2), channel_id=1, source_target_pairs={{0,1},{1,0},{2,3},{3,2},{4,5},{5,4},{6,7},{7,6},{8,9},{9,8},{10,11... | collective-permute-start | bytes 589832 | tf_op jit(solution)/shard_map/ppermute | solution.py:403
  36.1 2.0 %collective-permute-start.12 = (bf16[2016,128]{1,0:T(8,128)(2,1)S(1)}, bf16[2016,128]{1,0:T(8,128)(2,1)S(1)}, u32[]{:S(2)}, u32[]{:S(2)}) collective-permute-start(bf16[2016,128]{1,0:T(8,128)(2,1)S(1)} %shard_map.136), channel_id=1, source_target_pairs={{0,4},{4,0},{8,12},{12,8},{16,20},{20,16},{24,28},{28,24},{1,5},{5... | collective-permute-start | bytes 1548296 | tf_op jit(solution)/shard_map/ppermute | solution.py:461
  36.6 7.3 %copy-start.4 = (f32[1344]{0:T(1024)S(1)}, f32[1344]{0:T(1024)}, u32[]{:S(2)}) copy-start(f32[1344]{0:T(1024)} %param.20) | copy-start | bytes 16132
  36.6 7.3 %copy-start.2 = (s32[1,2]{1,0:T(1,128)S(1)}, s32[1,2]{1,0:T(1,128)}, u32[]{:S(2)}) copy-start(s32[1,2]{1,0:T(1,128)} %bounds.1) | copy-start | bytes 28
  36.6 9.6 %copy-start = (bf16[128,1344]{0,1:T(8,128)(2,1)S(1)}, bf16[128,1344]{0,1:T(8,128)(2,1)}, u32[]{:S(2)}) copy-start(bf16[128,1344]{0,1:T(8,128)(2,1)} %param.14) | copy-start | bytes 1032196
  36.6 9.6 %copy-start.1 = (bf16[1,64,1344]{2,1,0:T(8,128)(2,1)S(1)}, bf16[1,64,1344]{2,1,0:T(8,128)(2,1)}, u32[]{:S(2)}) copy-start(bf16[1,64,1344]{2,1,0:T(8,128)(2,1)} %opt_resid.1) | copy-start | bytes 516100
  38.4 6.5 %collective-permute-start.13 = (f32[1,192]{1,0:T(1,128)S(1)}, f32[1,192]{1,0:T(1,128)S(1)}, u32[]{:S(2)}, u32[]{:S(2)}) collective-permute-start(f32[1,192]{1,0:T(1,128)S(1)} %get-tuple-element.39.s0), channel_id=1, source_target_pairs={{0,1},{1,2},{2,3},{3,0},{4,5},{5,6},{6,7},{7,4},{8,9},{9,10},{10,1... | collective-permute-start | bytes 2312 | tf_op jit(solution)/shard_map/ppermute | solution.py:394
  40.0 4.9 %collective-permute-start.14 = (f32[1,192]{1,0:T(1,128)S(1)}, f32[1,192]{1,0:T(1,128)S(1)}, u32[]{:S(2)}, u32[]{:S(2)}) collective-permute-start(f32[1,192]{1,0:T(1,128)S(1)} %get-tuple-element.39.s0), channel_id=1, source_target_pairs={{0,2},{1,3},{2,0},{3,1},{4,6},{5,7},{6,4},{7,5},{8,10},{9,11},{10,... | collective-permute-start | bytes 2312 | tf_op jit(solution)/shard_map/ppermute | solution.py:394
  42.7 3.6 %collective-permute-start.15 = (f32[1,192]{1,0:T(1,128)S(1)}, f32[1,192]{1,0:T(1,128)S(1)}, u32[]{:S(2)}, u32[]{:S(2)}) collective-permute-start(f32[1,192]{1,0:T(1,128)S(1)} %get-tuple-element.39.s0), channel_id=1, source_target_pairs={{0,3},{1,0},{2,1},{3,2},{4,7},{5,4},{6,5},{7,6},{8,11},{9,8},{10,9... | collective-permute-start | bytes 2312 | tf_op jit(solution)/shard_map/ppermute | solution.py:394
